TPU v7x, 32 devices: a whole 2x2x4 slice. The times are simulated.
32 devices in a mesh: row: 16 (over z, x, core), col: 2 (over y).
Axes of the slice: x: 2, y: 2, z: 4, core: 2. Of those that a mesh axis runs over, the one named last changes fastest.
Arguments:
- c_panel: float32 [8192, 128], P('row', 'col'), may hold values from -0.0625 to 0.0625
- cbar_in: float32 [8192, 128], P('row', 'col'), may hold values from -6 to 6
- factor_diagonal_block: float32 [128, 128], replicated, may hold values from -0.9 to 4, as said below
- dbar_in: float32 [128, 128], replicated, may hold values from -6 to 6
- r_panel: float32 [128, 4096], P('row', 'col'), may hold values from -0.6 to 0.6
- rbar_in: float32 [128, 4096], P('row', 'col'), may hold values from -6 to 6
- b_block: float32 [8192, 4096], P('row', 'col'), may hold values from -0.0625 to 0.0625
- bbar_in: float32 [8192, 4096], P('row', 'col'), may hold values from -6 to 6
Outputs:
- cbar_out: float32 [8192, 128], P('row', 'col')
- bbar_out: float32 [8192, 4096], P('row', 'col')
- kernel_diagonal_adjoint: float32 [128, 128], P('row', 'col')
- rbar_out: float32 [128, 4096], P('row', 'col')
Inputs may be any that keep to these rules, and one draw needn't show every extreme that they name: factor_diagonal_block is lower triangular; its diagonal entries lie in 2 to 4 and its entries below the diagonal in -0.9 to 0.9.
All inputs are finite; a program needn't handle non-finite values.
Results may differ from a plain program's by a relative error of at most 0.00007.
Values sent between devices are 32-bit elements; how exact they have to be, the bound alone decides.
No kernel may reach another device: no remote copies, remote signals or barrier semaphores. Data moves between devices by JAX's collectives and lax.ppermute only.
A program may use at most 64 MiB of HBM per device.

v0:
```python
import jax
import jax.numpy as jnp
from jax import lax
from jax.sharding import PartitionSpec as P


def lower_half_term(matrix):
    return jnp.tril(matrix) - 0.5 * jnp.diag(jnp.diag(matrix))


def body(c_panel, cbar_in, factor_diagonal_block, dbar_in, r_panel, rbar_in, b_block, bbar_in):
    highest = lax.Precision.HIGHEST
    col_width = c_panel.shape[1]
    row_height = r_panel.shape[0]
    col_index = lax.axis_index("col")
    row_index = lax.axis_index("row")
    column_adjoint_whole, c_full = (
        lax.all_gather(cbar_in, "col", axis=1, tiled=True),
        lax.all_gather(c_panel, "col", axis=1, tiled=True),
    )
    cbar_new = jax.scipy.linalg.solve_triangular(
        factor_diagonal_block, column_adjoint_whole.T, lower=True, trans="T"
    ).T
    product = jnp.dot(cbar_new.T, c_full, precision=highest, preferred_element_type=jnp.float32)
    product = lax.psum(product, "row")
    cbar_out = lax.dynamic_slice_in_dim(cbar_new, col_index * col_width, col_width, 1)
    r_full = lax.all_gather(r_panel, "row", axis=0, tiled=True)
    bbar_out = bbar_in - jnp.dot(
        cbar_new, r_full, precision=highest, preferred_element_type=jnp.float32
    )
    diagonal_adjoint_middle = dbar_in - jnp.tril(product)
    proj = lower_half_term(
        jnp.dot(
            factor_diagonal_block.T,
            diagonal_adjoint_middle,
            precision=highest,
            preferred_element_type=jnp.float32,
        )
    )
    left_product_term = jax.scipy.linalg.solve_triangular(
        factor_diagonal_block, proj, lower=True, trans="T"
    )
    sandwich_product = jax.scipy.linalg.solve_triangular(
        factor_diagonal_block, left_product_term.T, lower=True, trans="T"
    ).T
    diagonal_adjoint_whole = lower_half_term(sandwich_product + sandwich_product.T)
    dbar_rows = lax.dynamic_slice_in_dim(
        diagonal_adjoint_whole, row_index * row_height, row_height, 0
    )
    kernel_diagonal_adjoint = lax.dynamic_slice_in_dim(
        dbar_rows, col_index * col_width, col_width, 1
    )
    trailing_full = lax.dot_general(
        cbar_new,
        b_block,
        (((0,), (0,)), ((), ())),
        precision=highest,
        preferred_element_type=jnp.float32,
    )
    summed = lax.psum_scatter(trailing_full, "row", scatter_dimension=0, tiled=True)
    sym_full = diagonal_adjoint_whole + diagonal_adjoint_whole.T
    sym_rows = lax.dynamic_slice_in_dim(sym_full, row_index * row_height, row_height, 0)
    rbar_out = (
        rbar_in
        - summed
        - jnp.dot(sym_rows, r_full, precision=highest, preferred_element_type=jnp.float32)
    )
    return (cbar_out, bbar_out, kernel_diagonal_adjoint, rbar_out)


def solution(mesh):
    in_specs = (
        P("row", "col"),
        P("row", "col"),
        P(),
        P(),
        P("row", "col"),
        P("row", "col"),
        P("row", "col"),
        P("row", "col"),
    )
    out_specs = (P("row", "col"), P("row", "col"), P("row", "col"), P("row", "col"))
    return jax.shard_map(body, mesh=mesh, in_specs=in_specs, out_specs=out_specs, check_vma=False)
```

profile of v0, /device:TPU:0, one launch (start us, length us, event | category | flops | bytes accessed | tf_op | source)
XLA Modules:
  0.0 229.6 jit_solution(15127322025527314387)
XLA Ops:
  7.2 0.0 all-reduce.2.cloned.1.call-start
  7.2 0.9 select_bitcast_fusion
  8.1 9.8 %custom-call.7 = f32[1,128,128]{1,2,0:T(8,128)S(1)} custom-call(f32[1,128,128]{2,1,0:T(8,128)S(1)} %select_bitcast_fusion), custom_call_target="InvertDiagBlocksLowerTriangular" | custom-call | tf_op jit(solution)/shard_map/jit(_solve_triangular)/triangular_solve | solution.py:21
  17.9 7.4 %all_gather.11 = f32[512,128]{0,1:T(8,128)S(1)} all-gather(f32[512,64]{0,1:T(8,128)} %param.10), channel_id=1, replica_groups=mesh['row'=16,'col'=2] {'col'}, dimensions={1}, use_global_device_ids=true | all-gather | bytes 393216 | tf_op jit(solution)/shard_map/all_gather | solution.py:19
  25.3 0.0 copy-start.1
  25.3 0.0 copy-start.3
  25.3 6.0 %all_gather.9 = f32[512,128]{0,1:T(8,128)S(1)} all-gather(f32[512,64]{0,1:T(8,128)} %param.11), channel_id=1, replica_groups=mesh['row'=16,'col'=2] {'col'}, dimensions={1}, use_global_device_ids=true | all-gather | bytes 393216 | tf_op jit(solution)/shard_map/all_gather | solution.py:18
  31.3 0.4 fusion.3
  31.6 1.0 fusion.20
  32.6 0.0 all-reduce.2.cloned.1.call-update
  32.7 0.0 all-gather.2.cloned.1.call-start
  32.7 0.7 all-gather.2.cloned.1.call-update
  33.4 0.0 reduce-scatter.2.cloned.1.call-start
  33.5 5.6 %fusion.21 = f32[128,2048]{1,0:T(8,128)} fusion(f32[128,512]{1,0:T(8,128)S(1)} %fusion.3, f32[512,2048]{1,0:T(8,128)} %param.16), kind=kOutput, calls=%fused_computation.35 | convolution fusion | flops 1610612736 | bytes 5505024 | tf_op jit(solution)/shard_map/dot_general | solution.py:53
  39.0 0.0 reduce-scatter.2.cloned.1.call-update
  39.1 0.7 dynamic-slice_bitcast_fusion
  39.7 79.0 %all-reduce.2.cloned.1.call-done = f32[128,128]{1,0:T(8,128)} async-done(((f32[128,128]{1,0:T(8,128)}), f32[128,128]{1,0:T(8,128)}) %all-reduce.2.cloned.1.call-update) | async-done | bytes 65552 | tf_op jit(solution)/shard_map/psum | solution.py:25
  118.7 0.0 copy-done.1
  118.7 0.0 copy-done.3
  118.7 1.1 convolution_bitcast_fusion.1
  119.8 1.2 gather_fusion
  121.1 0.3 convolution_bitcast_fusion
  121.4 0.3 fusion.1
  121.7 0.1 copy.16
  121.8 1.2 gather_fusion.1
  123.0 0.1 multiply_subtract_fusion
  123.1 0.1 copy.17
  123.2 0.7 dynamic_slice.11
  123.9 0.0 copy-start.2
  123.9 36.8 %all-gather.2.cloned.1.call-done = f32[128,2048]{1,0:T(8,128)} async-done(((f32[8,2048]{1,0:T(8,128)}), f32[128,2048]{1,0:T(8,128)}) %all-gather.2.cloned.1.call-update) | async-done | bytes 1048592 | tf_op jit(solution)/shard_map/all_gather | solution.py:27
  160.7 0.0 copy-start
  160.7 7.3 %convolution_subtract_fusion = f32[512,2048]{1,0:T(8,128)} fusion(f32[512,2048]{1,0:T(8,128)} %param.17, f32[128,512]{1,0:T(8,128)S(1)} %fusion.3, f32[128,2048]{1,0:T(8,128)} %all-gather.2.cloned.1.call-done), kind=kOutput, calls=%fused_computation.2 | convolution fusion | flops 1611661312 | bytes 9699328 | tf_op jit(solution)/shard_map/dot_general | solution.py:28
  167.9 53.1 %reduce-scatter.2.cloned.1.call-done = f32[8,2048]{1,0:T(8,128)} async-done(((f32[128,2048]{1,0:T(8,128)}), f32[8,2048]{1,0:T(8,128)}) %reduce-scatter.2.cloned.1.call-update) | async-done | bytes 65552 | tf_op jit(solution)/shard_map/reduce_scatter | solution.py:60
  221.0 0.0 copy-done.2
  221.0 0.0 copy-done
  221.0 2.1 convolution_subtract_fusion.1
  (2 shorter events, 0.0 us)
Async XLA Ops:
  7.2 111.5 %all-reduce.2.cloned.1.call-start = ((), (), s32[]{:S(2)}) async-start(), calls=%async_computation.2 | async-start | bytes 131072 | tf_op jit(solution)/shard_map/psum | solution.py:25
  25.3 93.4 %copy-start.1 = (f32[128,128]{1,0:T(8,128)S(1)}, f32[128,128]{1,0:T(8,128)}, u32[]{:S(2)}) copy-start(f32[128,128]{1,0:T(8,128)} %param.12) | copy-start | bytes 196612
  25.3 93.4 %copy-start.3 = (f32[128,128]{1,0:T(8,128)S(1)}, f32[128,128]{1,0:T(8,128)}, u32[]{:S(2)}) copy-start(f32[128,128]{1,0:T(8,128)} %param.13) | copy-start | bytes 196612
  32.7 128.0 %all-gather.2.cloned.1.call-start = ((), (), s32[]{:S(2)}) async-start(), calls=%async_computation.1 | async-start | bytes 1114112 | tf_op jit(solution)/shard_map/all_gather | solution.py:27
  33.4 187.6 %reduce-scatter.2.cloned.1.call-start = ((), (), s32[]{:S(2)}) async-start(), calls=%async_computation.3 | async-start | bytes 1114112 | tf_op jit(solution)/shard_map/reduce_scatter | solution.py:60
  123.9 97.1 %copy-start.2 = (f32[8,2048]{1,0:T(8,128)S(1)}, f32[8,2048]{1,0:T(8,128)}, u32[]{:S(2)}) copy-start(f32[8,2048]{1,0:T(8,128)} %param.15) | copy-start | bytes 196612
  160.7 60.3 %copy-start = (f32[128,2048]{1,0:T(8,128)S(1)}, f32[128,2048]{1,0:T(8,128)}, u32[]{:S(2)}) copy-start(f32[128,2048]{1,0:T(8,128)} %all-gather.2.cloned.1.call-done) | copy-start | bytes 3145732
Sparse Core Ops, SparseCore 0:
  32.8 85.8 all-reduce.1
  121.1 39.5 all-gather.1
  164.7 56.2 reduce-scatter.1
where the time goes:
time: 230 us
  waiting for transfers between devices  170 us (74%)
  matrix products  17.9 us (8%)
  between operations  13.8 us (6%)
  blocking collectives  13.4 us (6%)
  other arithmetic  10.8 us (5%)
  local copies, waits for them, and re-layouts  4.03 us (2%)
    psum x1, waiting for transfers between devices, body(): product = lax.psum(product, 'row')  79 us
    reduce_scatter x1, waiting for transfers between devices, body(): lax.psum_scatter(trailing_full, 'row', scatter_dimension=0, tiled=True)  53.1 us
    all_gather x1, waiting for transfers between devices, body(): r_full = lax.all_gather(r_panel, 'row', axis=0, tiled=True)  36.8 us
    another operation x2, other arithmetic, body(): jax.scipy.linalg.solve_triangular(factor_diagonal_block, column_adjoint_w...  10.7 us
    all_gather x1, blocking collectives, body(): lax.all_gather(c_panel, 'col', axis=1, tiled=True)  7.39 us
    dot_general x1, matrix products, body(): jnp.dot(cbar_new, r_full, precision=highest, preferred_element_type=jnp.f...  7.26 us
    all_gather x1, blocking collectives, body(): lax.all_gather(cbar_in, 'col', axis=1, tiled=True)  5.98 us
    dot_general x1, matrix products, body(): lax.dot_general(cbar_new, b_block, (((0,), (0,)), ((), ())), precision=hi...  5.56 us
  transfers between devices with their start and end apart: 3, of which 3 were waited for; matrix products, arithmetic and copies ran while one was open for 8% of the time, Pallas kernels for 0%

commit v1 on v0

v1 whole, which is shorter than its diff:
```python
import jax
import jax.numpy as jnp
from jax import lax
from jax.experimental import pallas as pl
from jax.experimental.pallas import tpu as pltpu
from jax.sharding import PartitionSpec as P

HIGHEST = lax.Precision.HIGHEST
HIGH = lax.Precision.HIGH
F32 = jnp.float32
BF16 = jnp.bfloat16
MIB = 1 << 20
LANES = 128


def dot(a, b, dims=((1,), (0,)), precision=HIGHEST):
    return lax.dot_general(a, b, (dims, ((), ())), precision=precision, preferred_element_type=F32)


def iotas(shape):
    return lax.broadcasted_iota(jnp.int32, shape, 0), lax.broadcasted_iota(jnp.int32, shape, 1)


def phi(matrix):
    i, j = iotas(matrix.shape)
    return jnp.where(i > j, matrix, jnp.where(i == j, 0.5 * matrix, 0.0))


def split(value):
    high = value.astype(BF16)
    return high, (value - high.astype(F32)).astype(BF16)


def hot(cond):
    return jnp.where(cond, 1.0, 0.0).astype(F32)


def swap(value, axis, size, offset):
    return lax.ppermute(value, axis, [(i, i ^ offset) for i in range(size)])


def full(shape, dtype=F32):
    return jax.ShapeDtypeStruct(shape, dtype)


class Grid:
    def __init__(self, rows, cols, height, width):
        self.rows, self.cols, self.height, self.width = rows, cols, height, width
        cores, zs = 2, 4
        xs = rows // (cores * zs)
        self.core, self.x, self.z = (cores, 1), (xs, cores), (zs, xs * cores)
        self.z_near, self.z_far = (2, xs * cores), (2, 2 * xs * cores)
        self.order = (self.core, self.x, self.z)

    def offsets(self):
        found = [0]
        for count, stride in self.order:
            found = [base + d * stride for base in found for d in range(count)]
        return found

    def relative_row(self, position, me):
        block, inner = position // self.height, position % self.height
        offset = jnp.zeros_like(block)
        for count, stride in self.order[::-1]:
            offset = offset + (block % count) * stride
            block = block // count
        return (offset ^ me) * self.height + inner

    def permute_rows(self, ref, me):
        n, h = ref.shape[0], self.height
        if h % 8 == 0:
            return jnp.concatenate(
                [ref[pl.ds(pl.multiple_of((offset ^ me) * h, h), h), :] for offset in self.offsets()], axis=0
            )
        i, j = iotas((n, n))
        return dot(hot(j == self.relative_row(i, me)), ref[...])


def prepare_kernel(factor_ref, b_hbm, inverse_ref, high_ref, low_ref, b_ref, sems):
    chunks = sems.shape[0]
    step = b_ref.shape[0] // chunks
    copies = [
        pltpu.make_async_copy(b_hbm.at[pl.ds(k * step, step)], b_ref.at[pl.ds(k * step, step)], sems.at[k])
        for k in range(chunks)
    ]
    for copy in copies:
        copy.start()

    def split_chunk(k):
        copies[k].wait()
        at = slice(k * step, (k + 1) * step)
        high_ref[at, :], low_ref[at, :] = split(b_ref[at, :])

    factor = factor_ref[...]
    n = factor.shape[0]
    i, j = iotas((n, n))
    diagonal = jnp.where(i == j, factor, 0.0)
    recip_row = 1.0 / jnp.sum(diagonal, axis=0, keepdims=True)
    recip_col = 1.0 / jnp.sum(diagonal, axis=1, keepdims=True)
    size, level = 1, 0
    while size < n:
        below = (i // (2 * size) == j // (2 * size)) & ((i // size) % 2 == 1) & ((j // size) % 2 == 0)
        block = jnp.where(below, factor, 0.0)
        if level == 0:
            inverse = jnp.where(i == j, recip_row, -(recip_col * block * recip_row))
        else:
            inverse = inverse - dot(dot(inverse, block), inverse)
        if 2 <= level < 2 + chunks:
            split_chunk(level - 2)
        size, level = 2 * size, level + 1
    inverse_ref[...] = inverse
    for k in range(max(level - 2, 0), chunks):
        split_chunk(k)


def fold(matrix):
    n = matrix.shape[0]
    m = n // 2
    i, j = iotas((m, m))
    corner = matrix[m:, m:]
    mixed = jnp.where(i >= j, matrix[:m, :m], corner.T)
    diagonal = jnp.sum(jnp.where(i == j, corner, 0.0), axis=0, keepdims=True)
    top = jnp.concatenate([matrix[m:, :m], mixed], axis=1)
    last = jnp.broadcast_to(jnp.concatenate([diagonal, diagonal], axis=1), (8, n))
    return jnp.concatenate([top[k:k + 8] for k in range(0, m, 8)] + [last], axis=1)


def unfold(folded, n):
    folded = jnp.concatenate([folded[:, k:k + n] for k in range(0, folded.shape[1], n)], axis=0)
    m = n // 2
    i, j = iotas((m, m))
    mixed = folded[:m, m:]
    corner = jnp.where(i == j, folded[m:m + 1, :m], jnp.where(i > j, mixed.T, 0.0))
    upper = jnp.concatenate([jnp.where(i >= j, mixed, 0.0), jnp.zeros((m, m), F32)], axis=1)
    return jnp.concatenate([upper, jnp.concatenate([folded[:m, :m], corner], axis=1)], axis=0)


def cbar_kernel(grid, inverse_ref, *refs):
    cols = grid.cols
    cbar_refs, c_refs = refs[:cols], refs[cols:2 * cols]
    out_ref, product_ref, perm_ref, stack_ref, cbar, c, new = refs[2 * cols:]
    me, my_col = lax.axis_index("row"), lax.axis_index("col")
    n = inverse_ref.shape[0]
    for d in range(cols):
        at = pl.ds(pl.multiple_of((my_col ^ d) * grid.width, grid.width), grid.width)
        cbar[at, :] = cbar_refs[d][...]
        c[at, :] = c_refs[d][...]
    absolute = dot(inverse_ref[...].T, cbar[...])
    new[...] = absolute
    perm = grid.permute_rows(new, me)
    perm_ref[...] = perm
    stack_ref[:n, :], stack_ref[n:, :] = split(perm)
    out_ref[...] = new[pl.ds(pl.multiple_of(my_col * grid.width, grid.width), grid.width), :]
    product_ref[...] = fold(dot(absolute, c[...], ((1,), (1,))))


def trailing_kernel(stack_ref, high_ref, low_ref, keep_ref, send_ref):
    n = stack_ref.shape[0] // 2
    breadth = high_ref.shape[1]
    tile = 256
    for k in range(breadth // tile):
        at = slice(k * tile, (k + 1) * tile)
        stacked = dot(stack_ref[...], high_ref[:, at], precision=None)
        total = stacked[:n] + stacked[n:] + dot(stack_ref[:n, :], low_ref[:, at], precision=None)
        keep_ref[:, at] = total[:n // 2]
        send_ref[:, at] = total[n // 2:]


def bbar_kernel(perm_ref, sym_ref, panel_ref, bbar_ref, rbar_ref, out_hbm, rbar_out_ref, out_ref, left_ref, sems):
    n, depth = perm_ref.shape
    height = sym_ref.shape[0]
    left_ref[:depth, :n], left_ref[:depth, n:] = split(perm_ref[...].T)
    sym = jnp.concatenate([sym_ref[...], jnp.zeros((16 - height, n), F32)], axis=0)
    left_ref[depth:, :n], left_ref[depth:, n:] = split(sym)
    count = sems.shape[0]
    tile = panel_ref.shape[1] // count
    copies = []
    for k in range(count):
        at = slice(k * tile, (k + 1) * tile)
        high, low = split(panel_ref[:, at])
        update = dot(left_ref[...], jnp.concatenate([high, high], axis=0), precision=None)
        update = update + dot(left_ref[:, :n], low, precision=None)
        out_ref[:, at] = bbar_ref[:, at] - update[:depth]
        rbar_out_ref[:, at] = rbar_ref[:, at] - update[depth:depth + height]
        copies.append(pltpu.make_async_copy(out_ref.at[:, pl.ds(k * tile, tile)], out_hbm.at[:, pl.ds(k * tile, tile)], sems.at[k]))
        copies[-1].start()
    for copy in copies:
        copy.wait()


def diagonal_kernel(grid, factor_ref, inverse_ref, dbar_ref, *refs):
    products, (out_ref, sym_ref) = refs[:-2], refs[-2:]
    me, my_col = lax.axis_index("row"), lax.axis_index("col")
    n, height, width = factor_ref.shape[0], grid.height, grid.width
    i, j = iotas((n, n))
    inverse = inverse_ref[...]
    si, sj = iotas((height, n))
    own_row = me * height + si
    weights = dot(hot(sj == own_row), inverse.T)
    inverse_perm = dot(inverse, hot(i == grid.relative_row(j, me)))
    product = unfold(add_pairs([ref[...] for ref in products]), n)
    proj = phi(dot(factor_ref[...].T, dbar_ref[...] - product))
    half = dot(weights, proj + proj.T)
    rows_sym = dot(half, inverse)
    sym_ref[...] = dot(half, inverse_perm)
    rows_kernel = jnp.where(sj < own_row, rows_sym, jnp.where(sj == own_row, 0.5 * rows_sym, 0.0))
    ci, cj = iotas((n, width))
    out_ref[...] = dot(rows_kernel, hot(ci == my_col * width + cj))


def call(kernel, out_shape, scratch=(), limit=8 * MIB, flops=0, specs=None):
    return pl.pallas_call(
        kernel,
        out_shape=out_shape,
        scratch_shapes=list(scratch),
        compiler_params=pltpu.CompilerParams(vmem_limit_bytes=limit),
        cost_estimate=pl.CostEstimate(flops=flops, bytes_accessed=1, transcendentals=0),
        **({"in_specs": specs} if specs else {}),
    )


def add_pairs(terms):
    while len(terms) > 1:
        terms = [a + b for a, b in zip(terms[::2], terms[1::2])]
    return terms[0]


def make_body(rows, cols):
    def row_parts(value, step):
        count, stride = step
        return [value] + [swap(value, "row", rows, d * stride) for d in range(1, count)]

    def col_parts(value):
        return [value] + [swap(value, "col", cols, d) for d in range(1, cols)]

    def body(c_panel, cbar_in, factor, dbar_in, r_panel, rbar_in, b_block, bbar_in):
        n = factor.shape[0]
        depth, width = c_panel.shape
        height, breadth = r_panel.shape
        grid = Grid(rows, cols, height, width)

        cbar_parts, c_parts = col_parts(cbar_in.T), col_parts(c_panel.T)
        panel = jnp.concatenate(row_parts(r_panel, grid.z), axis=0)
        panel = jnp.concatenate(row_parts(panel, grid.x), axis=0)

        inverse, high, low = call(
            prepare_kernel,
            (full((n, n)), full((depth, breadth), BF16), full((depth, breadth), BF16)),
            [pltpu.VMEM((depth, breadth), F32), pltpu.SemaphoreType.DMA((8,))],
            limit=48 * MIB, flops=4 * 10 ** 9,
            specs=[pl.BlockSpec(memory_space=pltpu.VMEM), pl.BlockSpec(memory_space=pltpu.HBM)],
        )(factor, b_block)
        cbar_out_t, product, cbar_perm, stack = call(
            lambda *refs: cbar_kernel(grid, *refs),
            (full((width, depth)), full((8, (n // 16 + 1) * n)), full((n, depth)), full((2 * n, depth), BF16)),
            [pltpu.VMEM((n, depth), F32)] * 3, flops=10 ** 9,
        )(inverse, *cbar_parts, *c_parts)

        keep, send = call(trailing_kernel, (full((n // 2, breadth)),) * 2, flops=10 ** 9)(stack, high, low)
        summed = keep + swap(send, "row", rows, grid.core[1])
        product = add_pairs(row_parts(product, grid.z_near))
        product, summed = lax.optimization_barrier((product, summed))
        product = add_pairs(row_parts(product, grid.core))
        product, panel = lax.optimization_barrier((product, panel))
        panel = jnp.concatenate(row_parts(panel, grid.core), axis=0)
        product = add_pairs(row_parts(product, grid.z_far))
        product_parts = row_parts(product, grid.x)
        for count, stride in grid.order[1:]:
            blocks = summed.reshape(count, -1, breadth)
            summed = add_pairs([blocks[0]] + [swap(blocks[d], "row", rows, d * stride) for d in range(1, count)])
            if stride == grid.x[1]:
                summed, dbar_in = lax.optimization_barrier((summed, dbar_in))
        kernel_out, sym = call(
            lambda *refs: diagonal_kernel(grid, *refs), (full((height, width)), full((height, n)))
        )(factor, inverse, dbar_in, *product_parts)
        vmem = pl.BlockSpec(memory_space=pltpu.VMEM)
        bbar_out, rbar = pl.pallas_call(
            bbar_kernel,
            in_specs=[vmem] * 5,
            out_specs=[pl.BlockSpec(memory_space=pltpu.HBM), vmem],
            out_shape=(full((depth, breadth)), full((height, breadth))),
            scratch_shapes=[
                pltpu.VMEM((depth, breadth), F32), pltpu.VMEM((depth + 16, 2 * n), BF16), pltpu.SemaphoreType.DMA((breadth // 256,))
            ],
            compiler_params=pltpu.CompilerParams(vmem_limit_bytes=16 * MIB),
            cost_estimate=pl.CostEstimate(flops=10 ** 9, bytes_accessed=1, transcendentals=0),
        )(cbar_perm, sym, panel, bbar_in, rbar_in)
        return (cbar_out_t.T, bbar_out, kernel_out, rbar - summed)

    return body


def solution(mesh):
    spec = P("row", "col")
    in_specs = (spec, spec, P(), P(), spec, spec, spec, spec)
    return jax.shard_map(
        make_body(mesh.shape["row"], mesh.shape["col"]),
        mesh=mesh, in_specs=in_specs, out_specs=(spec,) * 4, check_vma=False,
    )
```

time: 230 us -> 39.1 us (0.17)
  waiting for transfers between devices: 170 us -> 7.9 us
  starting transfers between devices: 0.12 us -> 18.2 us
  matrix products: 17.9 us -> 0 us
  blocking collectives: 13.4 us -> 0 us
  between operations: 13.8 us -> 0.85 us
  Pallas kernels: 0 us -> 10.1 us
  other arithmetic: 10.8 us -> 0.87 us
  local copies, waits for them, and re-layouts: 4.03 us -> 0.95 us
    psum x1 -> x0, waiting for transfers between devices: 79 us -> none  [body(): product = lax.psum(product, 'row')]
    reduce_scatter x1 -> x0, waiting for transfers between devices: 53.1 us -> none  [body(): lax.psum_scatter(trailing_full, 'row', scatter_dimension=0, tiled=True)]
    all_gather x1 -> x0, waiting for transfers between devices: 36.8 us -> none  [body(): r_full = lax.all_gather(r_panel, 'row', axis=0, tiled=True)]
    ppermute x0 -> x16, starting transfers between devices: none -> 18.2 us  [swap(): return lax.ppermute(value, axis, [(i, i ^ offset) for i in range(size)])]
    dot_general x5 -> x0, matrix products: 17 us -> none  [the longest x1 7.26 us: body(): jnp.dot(cbar_new, r_full, precision=highest, preferred_element_type=jnp.f...]
    all_gather x2 -> x0, blocking collectives: 13.4 us -> none  [the longest x1 7.39 us: body(): lax.all_gather(c_panel, 'col', axis=1, tiled=True)]
    another operation x2 -> x0, other arithmetic: 10.7 us -> none  [body(): jax.scipy.linalg.solve_triangular(factor_diagonal_block, column_adjoint_w...]
    pallas_call x0 -> x5, Pallas kernels: none -> 10.1 us  [the longest x1 3.44 us: body(): call(prepare_kernel, (full((n, n)), full((depth, breadth), BF16), full((d...]
  transfers between devices with their start and end apart: 3 -> 16, of which waited for: 3 -> 3; matrix products, arithmetic and copies ran while one was open for 8% -> 1% of each run, Pallas kernels for 0% -> 26%
where the time goes in v1:
time: 39.1 us; the launch traced here: 38.9 us
  starting transfers between devices  18.2 us (47%)
  Pallas kernels  10.1 us (26%)
  waiting for transfers between devices  7.9 us (20%)
  local copies, waits for them, and re-layouts  0.95 us (2%)
  other arithmetic  0.87 us (2%)
  between operations  0.85 us (2%)
    ppermute x16, starting transfers between devices, swap(): return lax.ppermute(value, axis, [(i, i ^ offset) for i in range(size)])  18.2 us
    ppermute x16, waiting for transfers between devices, swap(): return lax.ppermute(value, axis, [(i, i ^ offset) for i in range(size)])  7.9 us
    pallas_call x1, Pallas kernels, body(): call(prepare_kernel, (full((n, n)), full((depth, breadth), BF16), full((d...  3.44 us
    pallas_call x1, Pallas kernels, body(): pl.pallas_call(bbar_kernel, in_specs=[vmem] * 5, out_specs=[pl.BlockSpec(...  2.63 us
    pallas_call x1, Pallas kernels, body(): call(lambda *refs: diagonal_kernel(grid, *refs), (full((height, width)),...  1.77 us
    pallas_call x1, Pallas kernels, body(): call(lambda *refs: cbar_kernel(grid, *refs), (full((width, depth)), full(...  1.33 us
    pallas_call x1, Pallas kernels, body(): call(trailing_kernel, (full((n // 2, breadth)),) * 2, flops=10 ** 9)  0.97 us
    unnamed x18, local copies, waits for them, and re-layouts  0.89 us
  transfers between devices with their start and end apart: 16, of which 3 were waited for; matrix products, arithmetic and copies ran while one was open for 1% of the time, Pallas kernels for 26%

profile of v1, /device:TPU:0, one launch (start us, length us, event | category | flops | bytes accessed | tf_op | source)
XLA Modules:
  0.0 38.9 jit_solution(13185173480733519887)
XLA Ops:
  0.6 3.1 %collective-permute-start.6 = (f32[8,2048]{1,0:T(8,128)}, f32[8,2048]{1,0:T(8,128)S(1)}, u32[]{:S(2)}, u32[]{:S(2)}) collective-permute-start(f32[8,2048]{1,0:T(8,128)} %param.12), channel_id=1, source_target_pairs={{0,8},{2,10},{4,12},{6,14},{8,0},{10,2},{12,4},{14,6},{16,24},{18,... | collective-permute-start | bytes 196616 | tf_op jit(solution)/shard_map/ppermute | solution.py:39
  3.7 2.6 %collective-permute-start.7 = (f32[8,2048]{1,0:T(8,128)}, f32[8,2048]{1,0:T(8,128)S(1)}, u32[]{:S(2)}, u32[]{:S(2)}) collective-permute-start(f32[8,2048]{1,0:T(8,128)} %param.12), channel_id=1, source_target_pairs={{0,16},{2,18},{4,20},{6,22},{8,24},{10,26},{12,28},{14,30},{16,0},... | collective-permute-start | bytes 196616 | tf_op jit(solution)/shard_map/ppermute | solution.py:39
  6.3 0.0 collective-permute-start.8
  6.3 1.7 %collective-permute-start = (f32[64,512]{1,0:T(8,128)}, f32[64,512]{1,0:T(8,128)S(1)}, u32[]{:S(2)}, u32[]{:S(2)}) collective-permute-start(f32[64,512]{1,0:T(8,128)} %bitcast.3), channel_id=1, source_target_pairs={{0,1},{1,0},{2,3},{3,2},{4,5},{5,4},{6,7},{7,6},{8,9},{9,8},{10,11... | collective-permute-start | bytes 393224 | tf_op jit(solution)/shard_map/ppermute | solution.py:39
  8.1 0.3 collective-permute-start.1
  8.3 0.0 copy-start.2
  8.3 0.8 %copy-done.2 = f32[128,128]{1,0:T(8,128)S(1)} copy-done((f32[128,128]{1,0:T(8,128)S(1)}, f32[128,128]{1,0:T(8,128)}, u32[]{:S(2)}) %copy-start.2) | copy-done | bytes 65560
  9.2 0.0 copy-start.6
  9.2 0.0 copy-start.4
  9.2 0.0 copy-start.5
  9.2 3.4 %shard_map.111 = (f32[128,128]{1,0:T(8,128)S(1)}, bf16[512,2048]{1,0:T(8,128)(2,1)S(1)}, bf16[512,2048]{1,0:T(8,128)(2,1)S(1)}) custom-call(f32[128,128]{1,0:T(8,128)S(1)} %copy-done.2, f32[512,2048]{1,0:T(8,128)} %b_hbm.1), custom_call_target="tpu_custom_call" | custom-call | flops 4000000000 | bytes 1 | tf_op jit(solution)/shard_map/pallas_call | solution.py:246
  12.6 0.0 copy-done.6
  12.7 0.0 collective-permute-done.6
  12.7 0.0 collective-permute-done.7
  12.7 0.0 collective-permute-done.8
  12.7 1.8 %collective-permute-start.9 = (f32[32,2048]{1,0:T(8,128)S(1)}, f32[32,2048]{1,0:T(8,128)S(1)}, u32[]{:S(2)}, u32[]{:S(2)}) collective-permute-start(f32[32,2048]{1,0:T(8,128)S(1)} %pad_maximum_fusion.1), channel_id=1, source_target_pairs={{0,4},{2,6},{4,0},{6,2},{8,12},{10,14},{12,8},{14,10},{16,20},{18,... | collective-permute-start | bytes 786440 | tf_op jit(solution)/shard_map/ppermute | solution.py:39
  14.5 0.0 collective-permute-done.refs_2_
  14.5 0.0 collective-permute-done.1.refs_4_
  14.5 0.0 copy-done.4
  14.5 0.0 copy-done.5
  14.5 1.3 %shard_map.112 = (f32[64,512]{1,0:T(8,128)}, f32[8,1152]{1,0:T(8,128)S(1)}, f32[128,512]{1,0:T(8,128)S(1)}, bf16[256,512]{1,0:T(8,128)(2,1)S(1)}) custom-call(f32[128,128]{1,0:T(8,128)S(1)} %get-tuple-element.23.refs_0_.refs_1_, f32[64,512]{1,0:T(8,128)S(1)} %bitcast.4, f32[64,512]{1,0:T(8,128)S(1)} %collective-permute-done.refs_2_, f32[64,512]{1,0:T(8,128)S(1)} %bitcast.6, ...), custom_call_target="tpu_custom_call" | custom-call | flops 1000000000 | bytes 1 | tf_op jit(solution)/shard_map/pallas_call | solution.py:253
  15.8 0.0 copy-start.3
  15.8 1.0 %shard_map.113 = (f32[64,2048]{1,0:T(8,128)S(1)}, f32[64,2048]{1,0:T(8,128)S(1)}) custom-call(bf16[256,512]{1,0:T(8,128)(2,1)S(1)} %get-tuple-element.27.stack_ref, bf16[512,2048]{1,0:T(8,128)(2,1)S(1)} %get-tuple-element.28.high_ref, bf16[512,2048]{1,0:T(8,128)(2,1)S(1)} %get-tuple-element.29.low_ref), custom_call_target="tpu_custom_call" | custom-call | flops 1000000000 | bytes 1 | tf_op jit(solution)/shard_map/pallas_call | solution.py:259
  16.8 0.0 copy-start
  16.8 0.0 copy-start.1
  16.9 0.1 collective-permute-start.3
  17.0 0.7 %collective-permute-start.2 = (f32[8,1152]{1,0:T(8,128)S(1)}, f32[8,1152]{1,0:T(8,128)S(1)}, u32[]{:S(2)}, u32[]{:S(2)}) collective-permute-start(f32[8,1152]{1,0:T(8,128)S(1)} %get-tuple-element.26), channel_id=1, source_target_pairs={{0,8},{2,10},{4,12},{6,14},{8,0},{10,2},{12,4},{14,6},{16,24},{18,... | collective-permute-start | bytes 110600 | tf_op jit(solution)/shard_map/ppermute | solution.py:39
  17.7 3.3 %collective-permute-done.2 = f32[8,1152]{1,0:T(8,128)S(1)} collective-permute-done((f32[8,1152]{1,0:T(8,128)S(1)}, f32[8,1152]{1,0:T(8,128)S(1)}, u32[]{:S(2)}, u32[]{:S(2)}) %collective-permute-start.2) | collective-permute-done | bytes 36896 | tf_op jit(solution)/shard_map/ppermute | solution.py:39
  21.0 0.0 collective-permute-done.3
  21.0 0.1 add.25
  21.1 1.1 %collective-permute-start.4 = (f32[32,2048]{1,0:T(8,128)S(1)}, f32[32,2048]{1,0:T(8,128)S(1)}, u32[]{:S(2)}, u32[]{:S(2)}) collective-permute-start(f32[32,2048]{1,0:T(8,128)S(1)} %slice.25), channel_id=1, source_target_pairs={{0,4},{2,6},{4,0},{6,2},{8,12},{10,14},{12,8},{14,10},{16,20},{18,... | collective-permute-start | bytes 786440 | tf_op jit(solution)/shard_map/ppermute | solution.py:39
  22.1 0.0 collective-permute-start.5
  22.1 0.0 collective-permute-done.9
  22.2 1.2 %collective-permute-done.5 = f32[8,1152]{1,0:T(8,128)S(1)} collective-permute-done((f32[8,1152]{1,0:T(8,128)S(1)}, f32[8,1152]{1,0:T(8,128)S(1)}, u32[]{:S(2)}, u32[]{:S(2)}) %collective-permute-start.5) | collective-permute-done | bytes 36896 | tf_op jit(solution)/shard_map/ppermute | solution.py:39
  23.4 2.3 %collective-permute-start.10 = (f32[8,1152]{1,0:T(8,128)S(1)}, f32[8,1152]{1,0:T(8,128)S(1)}, u32[]{:S(2)}, u32[]{:S(2)}) collective-permute-start(f32[8,1152]{1,0:T(8,128)S(1)} %add.27), channel_id=1, source_target_pairs={{0,16},{2,18},{4,20},{6,22},{8,24},{10,26},{12,28},{14,30},{16,0},... | collective-permute-start | bytes 110600 | tf_op jit(solution)/shard_map/ppermute | solution.py:39
  25.6 0.0 collective-permute-start.12
  25.6 3.4 %collective-permute-done.10 = f32[8,1152]{1,0:T(8,128)S(1)} collective-permute-done((f32[8,1152]{1,0:T(8,128)S(1)}, f32[8,1152]{1,0:T(8,128)S(1)}, u32[]{:S(2)}, u32[]{:S(2)}) %collective-permute-start.10) | collective-permute-done | bytes 36896 | tf_op jit(solution)/shard_map/ppermute | solution.py:39
  29.0 1.0 %collective-permute-start.11 = (f32[8,1152]{1,0:T(8,128)S(1)}, f32[8,1152]{1,0:T(8,128)S(1)}, u32[]{:S(2)}, u32[]{:S(2)}) collective-permute-start(f32[8,1152]{1,0:T(8,128)S(1)} %add.28.refs_3_), channel_id=1, source_target_pairs={{0,4},{2,6},{4,0},{6,2},{8,12},{10,14},{12,8},{14,10},{16,20},{18,... | collective-permute-start | bytes 110600 | tf_op jit(solution)/shard_map/ppermute | solution.py:39
  30.1 0.0 collective-permute-done.4
  30.1 1.6 %collective-permute-start.14 = (f32[8,2048]{1,0:T(8,128)S(1)}, f32[8,2048]{1,0:T(8,128)S(1)}, u32[]{:S(2)}, u32[]{:S(2)}) collective-permute-start(f32[8,2048]{1,0:T(8,128)S(1)} %get-tuple-element.44), channel_id=1, source_target_pairs={{0,16},{2,18},{4,20},{6,22},{8,24},{10,26},{12,28},{14,30},{16,0},... | collective-permute-start | bytes 196616 | tf_op jit(solution)/shard_map/ppermute | solution.py:39
  31.7 1.4 %collective-permute-start.15 = (f32[8,2048]{1,0:T(8,128)S(1)}, f32[8,2048]{1,0:T(8,128)S(1)}, u32[]{:S(2)}, u32[]{:S(2)}) collective-permute-start(f32[8,2048]{1,0:T(8,128)S(1)} %get-tuple-element.43), channel_id=1, source_target_pairs={{0,24},{2,26},{4,28},{6,30},{8,16},{10,18},{12,20},{14,22},{16,8},... | collective-permute-start | bytes 196616 | tf_op jit(solution)/shard_map/ppermute | solution.py:39
  33.1 0.6 %collective-permute-start.13 = (f32[8,2048]{1,0:T(8,128)S(1)}, f32[8,2048]{1,0:T(8,128)S(1)}, u32[]{:S(2)}, u32[]{:S(2)}) collective-permute-start(f32[8,2048]{1,0:T(8,128)S(1)} %get-tuple-element.42), channel_id=1, source_target_pairs={{0,8},{2,10},{4,12},{6,14},{8,0},{10,2},{12,4},{14,6},{16,24},{18,... | collective-permute-start | bytes 196616 | tf_op jit(solution)/shard_map/ppermute | solution.py:39
  33.7 0.0 collective-permute-done.11.refs_4_
  33.7 0.0 copy-done.3
  33.7 1.8 %shard_map.114 = (f32[8,64]{1,0:T(8,128)}, f32[8,128]{1,0:T(8,128)S(1)}) custom-call(f32[128,128]{1,0:T(8,128)S(1)} %copy-done.2, f32[128,128]{1,0:T(8,128)S(1)} %get-tuple-element.23.refs_0_.refs_1_, f32[128,128]{1,0:T(8,128)S(1)} %copy-done.3, f32[8,1152]{1,0:T(8,128)S(1)} %add.28.refs_3_, f32[8,1152]{1,0:T(8,128)S(1)} %collective-permute-done.11.refs_4_), custom_call_target="tpu_custom_call" | custom-call | bytes 1 | tf_op jit(solution)/shard_map/pallas_call | solution.py:273
  35.5 0.0 collective-permute-done.12
  35.5 0.1 pad_maximum_fusion.panel_ref
  35.6 0.0 copy-done
  35.6 0.0 copy-done.1
  35.6 2.6 %shard_map.115 = (f32[512,2048]{1,0:T(8,128)}, f32[8,2048]{1,0:T(8,128)S(1)}) custom-call(f32[128,512]{1,0:T(8,128)S(1)} %get-tuple-element.25.perm_ref, f32[8,128]{1,0:T(8,128)S(1)} %get-tuple-element.36.sym_ref, f32[128,2048]{1,0:T(8,128)S(1)} %pad_maximum_fusion.panel_ref, f32[512,2048]{1,0:T(8,128)S(1)} %copy-done, f32[8,2048]{1,0:T(8,128)S(1)} %copy-done.1), custom_call_target="tpu_custom_call" | custom-call | flops 1000000000 | bytes 1 | tf_op jit(solution)/shard_map/pallas_call | solution.py:277
  38.2 0.0 collective-permute-done.14
  38.2 0.0 collective-permute-done.15
  38.2 0.0 collective-permute-done.13
  38.3 0.6 %add_subtract_fusion = f32[8,2048]{1,0:T(8,128)} fusion(f32[8,2048]{1,0:T(8,128)S(1)} %get-tuple-element.40, f32[8,2048]{1,0:T(8,128)S(1)} %collective-permute-done.14, f32[8,2048]{1,0:T(8,128)S(1)} %collective-permute-done.15, f32[8,2048]{1,0:T(8,128)S(1)} %collective-permute-done.13, f32[32,2048]{1,0:T(8,128)S(1)} %slice_add_fusion), kind=kLoop, calls=%fused_computation.3 | loop fusion | flops 65536 | bytes 393216 | tf_op jit(solution)/shard_map/sub | solution.py:288
  (12 shorter events, 0.2 us)
Async XLA Ops:
  0.6 12.0 %collective-permute-start.6 = (f32[8,2048]{1,0:T(8,128)}, f32[8,2048]{1,0:T(8,128)S(1)}, u32[]{:S(2)}, u32[]{:S(2)}) collective-permute-start(f32[8,2048]{1,0:T(8,128)} %param.12), channel_id=1, source_target_pairs={{0,8},{2,10},{4,12},{6,14},{8,0},{10,2},{12,4},{14,6},{16,24},{18,... | collective-permute-start | bytes 196616 | tf_op jit(solution)/shard_map/ppermute | solution.py:39
  3.7 8.9 %collective-permute-start.7 = (f32[8,2048]{1,0:T(8,128)}, f32[8,2048]{1,0:T(8,128)S(1)}, u32[]{:S(2)}, u32[]{:S(2)}) collective-permute-start(f32[8,2048]{1,0:T(8,128)} %param.12), channel_id=1, source_target_pairs={{0,16},{2,18},{4,20},{6,22},{8,24},{10,26},{12,28},{14,30},{16,0},... | collective-permute-start | bytes 196616 | tf_op jit(solution)/shard_map/ppermute | solution.py:39
  6.3 6.4 %collective-permute-start.8 = (f32[8,2048]{1,0:T(8,128)}, f32[8,2048]{1,0:T(8,128)S(1)}, u32[]{:S(2)}, u32[]{:S(2)}) collective-permute-start(f32[8,2048]{1,0:T(8,128)} %param.12), channel_id=1, source_target_pairs={{0,24},{2,26},{4,28},{6,30},{8,16},{10,18},{12,20},{14,22},{16,8},... | collective-permute-start | bytes 196616 | tf_op jit(solution)/shard_map/ppermute | solution.py:39
  6.3 8.2 %collective-permute-start = (f32[64,512]{1,0:T(8,128)}, f32[64,512]{1,0:T(8,128)S(1)}, u32[]{:S(2)}, u32[]{:S(2)}) collective-permute-start(f32[64,512]{1,0:T(8,128)} %bitcast.3), channel_id=1, source_target_pairs={{0,1},{1,0},{2,3},{3,2},{4,5},{5,4},{6,7},{7,6},{8,9},{9,8},{10,11... | collective-permute-start | bytes 393224 | tf_op jit(solution)/shard_map/ppermute | solution.py:39
  8.1 6.4 %collective-permute-start.1 = (f32[64,512]{1,0:T(8,128)}, f32[64,512]{1,0:T(8,128)S(1)}, u32[]{:S(2)}, u32[]{:S(2)}) collective-permute-start(f32[64,512]{1,0:T(8,128)} %bitcast.5), channel_id=1, source_target_pairs={{0,1},{1,0},{2,3},{3,2},{4,5},{5,4},{6,7},{7,6},{8,9},{9,8},{10,11... | collective-permute-start | bytes 393224 | tf_op jit(solution)/shard_map/ppermute | solution.py:39
  8.3 0.8 %copy-start.2 = (f32[128,128]{1,0:T(8,128)S(1)}, f32[128,128]{1,0:T(8,128)}, u32[]{:S(2)}) copy-start(f32[128,128]{1,0:T(8,128)} %refs_0_.1) | copy-start | bytes 196612
  9.2 3.5 %copy-start.6 = (f32[8,2048]{1,0:T(8,128)S(1)}, f32[8,2048]{1,0:T(8,128)}, u32[]{:S(2)}) copy-start(f32[8,2048]{1,0:T(8,128)} %param.12) | copy-start | bytes 196612
  9.2 5.3 %copy-start.4 = (f32[512,64]{0,1:T(8,128)S(1)}, f32[512,64]{0,1:T(8,128)}, u32[]{:S(2)}) copy-start(f32[512,64]{0,1:T(8,128)} %param.9) | copy-start | bytes 393220
  9.2 5.3 %copy-start.5 = (f32[512,64]{0,1:T(8,128)S(1)}, f32[512,64]{0,1:T(8,128)}, u32[]{:S(2)}) copy-start(f32[512,64]{0,1:T(8,128)} %param.8) | copy-start | bytes 393220
  12.7 9.4 %collective-permute-start.9 = (f32[32,2048]{1,0:T(8,128)S(1)}, f32[32,2048]{1,0:T(8,128)S(1)}, u32[]{:S(2)}, u32[]{:S(2)}) collective-permute-start(f32[32,2048]{1,0:T(8,128)S(1)} %pad_maximum_fusion.1), channel_id=1, source_target_pairs={{0,4},{2,6},{4,0},{6,2},{8,12},{10,14},{12,8},{14,10},{16,20},{18,... | collective-permute-start | bytes 786440 | tf_op jit(solution)/shard_map/ppermute | solution.py:39
  15.8 17.8 %copy-start.3 = (f32[128,128]{1,0:T(8,128)S(1)}, f32[128,128]{1,0:T(8,128)}, u32[]{:S(2)}) copy-start(f32[128,128]{1,0:T(8,128)} %refs_2_) | copy-start | bytes 196612
  16.8 18.7 %copy-start = (f32[512,2048]{1,0:T(8,128)S(1)}, f32[512,2048]{1,0:T(8,128)}, u32[]{:S(2)}) copy-start(f32[512,2048]{1,0:T(8,128)} %bbar_ref.1) | copy-start | bytes 12582916
  16.8 18.7 %copy-start.1 = (f32[8,2048]{1,0:T(8,128)S(1)}, f32[8,2048]{1,0:T(8,128)}, u32[]{:S(2)}) copy-start(f32[8,2048]{1,0:T(8,128)} %rbar_ref.1) | copy-start | bytes 196612
  16.9 4.1 %collective-permute-start.3 = (f32[64,2048]{1,0:T(8,128)S(1)}, f32[64,2048]{1,0:T(8,128)S(1)}, u32[]{:S(2)}, u32[]{:S(2)}) collective-permute-start(f32[64,2048]{1,0:T(8,128)S(1)} %get-tuple-element.31), channel_id=1, source_target_pairs={{0,2},{2,0},{4,6},{6,4},{8,10},{10,8},{12,14},{14,12},{16,18},{18,... | collective-permute-start | bytes 1572872 | tf_op jit(solution)/shard_map/ppermute | solution.py:39
  17.0 4.0 %collective-permute-start.2 = (f32[8,1152]{1,0:T(8,128)S(1)}, f32[8,1152]{1,0:T(8,128)S(1)}, u32[]{:S(2)}, u32[]{:S(2)}) collective-permute-start(f32[8,1152]{1,0:T(8,128)S(1)} %get-tuple-element.26), channel_id=1, source_target_pairs={{0,8},{2,10},{4,12},{6,14},{8,0},{10,2},{12,4},{14,6},{16,24},{18,... | collective-permute-start | bytes 110600 | tf_op jit(solution)/shard_map/ppermute | solution.py:39
  21.1 9.0 %collective-permute-start.4 = (f32[32,2048]{1,0:T(8,128)S(1)}, f32[32,2048]{1,0:T(8,128)S(1)}, u32[]{:S(2)}, u32[]{:S(2)}) collective-permute-start(f32[32,2048]{1,0:T(8,128)S(1)} %slice.25), channel_id=1, source_target_pairs={{0,4},{2,6},{4,0},{6,2},{8,12},{10,14},{12,8},{14,10},{16,20},{18,... | collective-permute-start | bytes 786440 | tf_op jit(solution)/shard_map/ppermute | solution.py:39
  22.1 1.2 %collective-permute-start.5 = (f32[8,1152]{1,0:T(8,128)S(1)}, f32[8,1152]{1,0:T(8,128)S(1)}, u32[]{:S(2)}, u32[]{:S(2)}) collective-permute-start(f32[8,1152]{1,0:T(8,128)S(1)} %add.24), channel_id=1, source_target_pairs={{0,2},{2,0},{4,6},{6,4},{8,10},{10,8},{12,14},{14,12},{16,18},{18,... | collective-permute-start | bytes 110600 | tf_op jit(solution)/shard_map/ppermute | solution.py:39
  23.4 5.6 %collective-permute-start.10 = (f32[8,1152]{1,0:T(8,128)S(1)}, f32[8,1152]{1,0:T(8,128)S(1)}, u32[]{:S(2)}, u32[]{:S(2)}) collective-permute-start(f32[8,1152]{1,0:T(8,128)S(1)} %add.27), channel_id=1, source_target_pairs={{0,16},{2,18},{4,20},{6,22},{8,24},{10,26},{12,28},{14,30},{16,0},... | collective-permute-start | bytes 110600 | tf_op jit(solution)/shard_map/ppermute | solution.py:39
  25.6 9.8 %collective-permute-start.12 = (f32[64,2048]{1,0:T(8,128)S(1)}, f32[64,2048]{1,0:T(8,128)S(1)}, u32[]{:S(2)}, u32[]{:S(2)}) collective-permute-start(f32[64,2048]{1,0:T(8,128)S(1)} %constant_dynamic-update-slice_fusion), channel_id=1, source_target_pairs={{0,2},{2,0},{4,6},{6,4},{8,10},{10,8},{12,14},{14,12},{16,18},{18,... | collective-permute-start | bytes 1572872 | tf_op jit(solution)/shard_map/ppermute | solution.py:39
  29.0 4.7 %collective-permute-start.11 = (f32[8,1152]{1,0:T(8,128)S(1)}, f32[8,1152]{1,0:T(8,128)S(1)}, u32[]{:S(2)}, u32[]{:S(2)}) collective-permute-start(f32[8,1152]{1,0:T(8,128)S(1)} %add.28.refs_3_), channel_id=1, source_target_pairs={{0,4},{2,6},{4,0},{6,2},{8,12},{10,14},{12,8},{14,10},{16,20},{18,... | collective-permute-start | bytes 110600 | tf_op jit(solution)/shard_map/ppermute | solution.py:39
  30.1 8.1 %collective-permute-start.14 = (f32[8,2048]{1,0:T(8,128)S(1)}, f32[8,2048]{1,0:T(8,128)S(1)}, u32[]{:S(2)}, u32[]{:S(2)}) collective-permute-start(f32[8,2048]{1,0:T(8,128)S(1)} %get-tuple-element.44), channel_id=1, source_target_pairs={{0,16},{2,18},{4,20},{6,22},{8,24},{10,26},{12,28},{14,30},{16,0},... | collective-permute-start | bytes 196616 | tf_op jit(solution)/shard_map/ppermute | solution.py:39
  31.7 6.5 %collective-permute-start.15 = (f32[8,2048]{1,0:T(8,128)S(1)}, f32[8,2048]{1,0:T(8,128)S(1)}, u32[]{:S(2)}, u32[]{:S(2)}) collective-permute-start(f32[8,2048]{1,0:T(8,128)S(1)} %get-tuple-element.43), channel_id=1, source_target_pairs={{0,24},{2,26},{4,28},{6,30},{8,16},{10,18},{12,20},{14,22},{16,8},... | collective-permute-start | bytes 196616 | tf_op jit(solution)/shard_map/ppermute | solution.py:39
  33.1 5.2 %collective-permute-start.13 = (f32[8,2048]{1,0:T(8,128)S(1)}, f32[8,2048]{1,0:T(8,128)S(1)}, u32[]{:S(2)}, u32[]{:S(2)}) collective-permute-start(f32[8,2048]{1,0:T(8,128)S(1)} %get-tuple-element.42), channel_id=1, source_target_pairs={{0,8},{2,10},{4,12},{6,14},{8,0},{10,2},{12,4},{14,6},{16,24},{18,... | collective-permute-start | bytes 196616 | tf_op jit(solution)/shard_map/ppermute | solution.py:39

commit v2 on v1

--- a/solution.py
+++ b/solution.py
@@ -76,7 +76,12 @@
         return dot(hot(j == self.relative_row(i, me)), ref[...])
 
 
-def prepare_kernel(factor_ref, b_hbm, inverse_ref, high_ref, low_ref, b_ref, sems):
+def identity_kernel(out_ref):
+    i, j = iotas(out_ref.shape)
+    out_ref[...] = hot(i == j)
+
+
+def prepare_kernel(factor_ref, identity_ref, b_hbm, inverse_ref, high_ref, low_ref, b_ref, sems):
     chunks = sems.shape[0]
     step = b_ref.shape[0] // chunks
     copies = [
@@ -94,7 +99,7 @@
     factor = factor_ref[...]
     n = factor.shape[0]
     i, j = iotas((n, n))
-    diagonal = jnp.where(i == j, factor, 0.0)
+    diagonal = factor * identity_ref[...]
     recip_row = 1.0 / jnp.sum(diagonal, axis=0, keepdims=True)
     recip_col = 1.0 / jnp.sum(diagonal, axis=1, keepdims=True)
     size, level = 1, 0
@@ -166,30 +171,27 @@
         send_ref[:, at] = total[n // 2:]
 
 
-def bbar_kernel(perm_ref, sym_ref, panel_ref, bbar_ref, rbar_ref, out_hbm, rbar_out_ref, out_ref, left_ref, sems):
-    n, depth = perm_ref.shape
-    height = sym_ref.shape[0]
-    left_ref[:depth, :n], left_ref[:depth, n:] = split(perm_ref[...].T)
-    sym = jnp.concatenate([sym_ref[...], jnp.zeros((16 - height, n), F32)], axis=0)
-    left_ref[depth:, :n], left_ref[depth:, n:] = split(sym)
+def bbar_kernel(perm_ref, bbar_ref, *refs):
+    panel_refs, (out_hbm, out_ref, left_ref, sems) = refs[:-4], refs[-4:]
+    n = perm_ref.shape[0]
+    left_ref[:, :n], left_ref[:, n:] = split(perm_ref[...].T)
     count = sems.shape[0]
-    tile = panel_ref.shape[1] // count
+    tile = bbar_ref.shape[1] // count
     copies = []
     for k in range(count):
         at = slice(k * tile, (k + 1) * tile)
-        high, low = split(panel_ref[:, at])
+        high, low = split(jnp.concatenate([ref[:, at] for ref in panel_refs], axis=0))
         update = dot(left_ref[...], jnp.concatenate([high, high], axis=0), precision=None)
-        update = update + dot(left_ref[:, :n], low, precision=None)
-        out_ref[:, at] = bbar_ref[:, at] - update[:depth]
-        rbar_out_ref[:, at] = rbar_ref[:, at] - update[depth:depth + height]
+        out_ref[:, at] = bbar_ref[:, at] - (update + dot(left_ref[:, :n], low, precision=None))
         copies.append(pltpu.make_async_copy(out_ref.at[:, pl.ds(k * tile, tile)], out_hbm.at[:, pl.ds(k * tile, tile)], sems.at[k]))
         copies[-1].start()
     for copy in copies:
         copy.wait()
 
 
-def diagonal_kernel(grid, factor_ref, inverse_ref, dbar_ref, *refs):
-    products, (out_ref, sym_ref) = refs[:-2], refs[-2:]
+def diagonal_kernel(grid, factor_ref, inverse_ref, dbar_ref, rbar_ref, *refs):
+    cores = grid.core[0]
+    panel_refs, products, (out_ref, rbar_out_ref) = refs[:cores], refs[cores:-2], refs[-2:]
     me, my_col = lax.axis_index("row"), lax.axis_index("col")
     n, height, width = factor_ref.shape[0], grid.height, grid.width
     i, j = iotas((n, n))
@@ -201,8 +203,11 @@
     product = unfold(add_pairs([ref[...] for ref in products]), n)
     proj = phi(dot(factor_ref[...].T, dbar_ref[...] - product))
     half = dot(weights, proj + proj.T)
-    rows_sym = dot(half, inverse)
-    sym_ref[...] = dot(half, inverse_perm)
+    rows_sym, rows_perm = dot(half, inverse), dot(half, inverse_perm)
+    high, low = split(rows_perm)
+    panel_high, panel_low = split(jnp.concatenate([ref[...] for ref in panel_refs], axis=0))
+    update = dot(high, panel_high, precision=None) + dot(low, panel_high, precision=None) + dot(high, panel_low, precision=None)
+    rbar_out_ref[...] = rbar_ref[...] - update
     rows_kernel = jnp.where(sj < own_row, rows_sym, jnp.where(sj == own_row, 0.5 * rows_sym, 0.0))
     ci, cj = iotas((n, width))
     out_ref[...] = dot(rows_kernel, hot(ci == my_col * width + cj))
@@ -219,6 +224,10 @@
     )
 
 
+def after(value, *others):
+    return lax.optimization_barrier((value, *others))[0]
+
+
 def add_pairs(terms):
     while len(terms) > 1:
         terms = [a + b for a, b in zip(terms[::2], terms[1::2])]
@@ -243,48 +252,48 @@
         panel = jnp.concatenate(row_parts(r_panel, grid.z), axis=0)
         panel = jnp.concatenate(row_parts(panel, grid.x), axis=0)
 
+        identity = call(identity_kernel, full((n, n)), flops=4 * 10 ** 9)()
         inverse, high, low = call(
             prepare_kernel,
             (full((n, n)), full((depth, breadth), BF16), full((depth, breadth), BF16)),
             [pltpu.VMEM((depth, breadth), F32), pltpu.SemaphoreType.DMA((8,))],
-            limit=48 * MIB, flops=4 * 10 ** 9,
-            specs=[pl.BlockSpec(memory_space=pltpu.VMEM), pl.BlockSpec(memory_space=pltpu.HBM)],
-        )(factor, b_block)
+            limit=48 * MIB, flops=4000000000,
+            specs=[pl.BlockSpec(memory_space=pltpu.VMEM)] * 2 + [pl.BlockSpec(memory_space=pltpu.HBM)],
+        )(factor, identity, b_block)
         cbar_out_t, product, cbar_perm, stack = call(
             lambda *refs: cbar_kernel(grid, *refs),
             (full((width, depth)), full((8, (n // 16 + 1) * n)), full((n, depth)), full((2 * n, depth), BF16)),
-            [pltpu.VMEM((n, depth), F32)] * 3, flops=10 ** 9,
+            [pltpu.VMEM((n, depth), F32)] * 3, flops=1000000000,
         )(inverse, *cbar_parts, *c_parts)
 
-        keep, send = call(trailing_kernel, (full((n // 2, breadth)),) * 2, flops=10 ** 9)(stack, high, low)
-        summed = keep + swap(send, "row", rows, grid.core[1])
+        keep, send = call(trailing_kernel, (full((n // 2, breadth)),) * 2, flops=1000000000)(stack, high, low)
+        summed = after(keep, panel) + swap(send, "row", rows, grid.core[1])
+        product = add_pairs(row_parts(product, grid.core))
+        product, summed = lax.optimization_barrier((product, summed))
         product = add_pairs(row_parts(product, grid.z_near))
-        product, summed = lax.optimization_barrier((product, summed))
-        product = add_pairs(row_parts(product, grid.core))
         product, panel = lax.optimization_barrier((product, panel))
-        panel = jnp.concatenate(row_parts(panel, grid.core), axis=0)
+        panel_parts = row_parts(panel, grid.core)
         product = add_pairs(row_parts(product, grid.z_far))
-        product_parts = row_parts(product, grid.x)
-        for count, stride in grid.order[1:]:
-            blocks = summed.reshape(count, -1, breadth)
-            summed = add_pairs([blocks[0]] + [swap(blocks[d], "row", rows, d * stride) for d in range(1, count)])
-            if stride == grid.x[1]:
-                summed, dbar_in = lax.optimization_barrier((summed, dbar_in))
-        kernel_out, sym = call(
-            lambda *refs: diagonal_kernel(grid, *refs), (full((height, width)), full((height, n)))
-        )(factor, inverse, dbar_in, *product_parts)
-        vmem = pl.BlockSpec(memory_space=pltpu.VMEM)
-        bbar_out, rbar = pl.pallas_call(
+
+        bbar_out = pl.pallas_call(
             bbar_kernel,
-            in_specs=[vmem] * 5,
-            out_specs=[pl.BlockSpec(memory_space=pltpu.HBM), vmem],
-            out_shape=(full((depth, breadth)), full((height, breadth))),
+            in_specs=[pl.BlockSpec(memory_space=pltpu.VMEM)] * (2 + len(panel_parts)),
+            out_specs=pl.BlockSpec(memory_space=pltpu.HBM),
+            out_shape=full((depth, breadth)),
             scratch_shapes=[
-                pltpu.VMEM((depth, breadth), F32), pltpu.VMEM((depth + 16, 2 * n), BF16), pltpu.SemaphoreType.DMA((breadth // 256,))
+                pltpu.VMEM((depth, breadth), F32), pltpu.VMEM((depth, 2 * n), BF16), pltpu.SemaphoreType.DMA((breadth // 256,))
             ],
             compiler_params=pltpu.CompilerParams(vmem_limit_bytes=16 * MIB),
-            cost_estimate=pl.CostEstimate(flops=10 ** 9, bytes_accessed=1, transcendentals=0),
-        )(cbar_perm, sym, panel, bbar_in, rbar_in)
+            cost_estimate=pl.CostEstimate(flops=0, bytes_accessed=1, transcendentals=0),
+        )(cbar_perm, bbar_in, *panel_parts)
+        for count, stride in grid.order[1:]:
+            own, *sends = summed.reshape(count, -1, breadth)
+            summed = add_pairs([own] + [swap(value, "row", rows, d * stride) for d, value in enumerate(sends, 1)])
+            if stride == grid.x[1]:
+                product = after(product, summed)
+        kernel_out, rbar = call(
+            lambda *refs: diagonal_kernel(grid, *refs), (full((height, width)), full((height, breadth))), flops=0
+        )(factor, inverse, dbar_in, rbar_in, *panel_parts, *row_parts(product, grid.x))
         return (cbar_out_t.T, bbar_out, kernel_out, rbar - summed)
 
     return body

time: 39.1 us -> 38.5 us (0.985)
  waiting for transfers between devices: 7.9 us -> 6.16 us
  starting transfers between devices: 18.2 us -> 19.8 us
    ppermute x16, waiting for transfers between devices: 7.9 us -> 6.16 us  [swap(): return lax.ppermute(value, axis, [(i, i ^ offset) for i in range(size)])]
    ppermute x16, starting transfers between devices: 18.2 us -> 19.8 us  [swap(): return lax.ppermute(value, axis, [(i, i ^ offset) for i in range(size)])]
    pallas_call x2 -> x3, Pallas kernels: 3.6 us -> 3.56 us  [the longest x1 2.58 us: body(): pl.pallas_call(bbar_kernel, in_specs=[pl.BlockSpec(memory_space=pltpu.VME...]
  transfers between devices with their start and end apart: 16 -> 16, of which waited for: 3 -> 5; matrix products, arithmetic and copies ran while one was open for 1% -> 0% of each run, Pallas kernels for 26% -> 26%
where the time goes in v2:
time: 38.5 us; the launch traced here: 38.3 us
  starting transfers between devices  19.8 us (51%)
  Pallas kernels  10.1 us (26%)
  waiting for transfers between devices  6.16 us (16%)
  between operations  0.8 us (2%)
  other arithmetic  0.79 us (2%)
  local copies, waits for them, and re-layouts  0.64 us (2%)
    ppermute x16, starting transfers between devices, swap(): return lax.ppermute(value, axis, [(i, i ^ offset) for i in range(size)])  19.8 us
    ppermute x16, waiting for transfers between devices, swap(): return lax.ppermute(value, axis, [(i, i ^ offset) for i in range(size)])  6.16 us
    pallas_call x1, Pallas kernels, body(): call(prepare_kernel, (full((n, n)), full((depth, breadth), BF16), full((d...  3.43 us
    pallas_call x1, Pallas kernels, body(): pl.pallas_call(bbar_kernel, in_specs=[pl.BlockSpec(memory_space=pltpu.VME...  2.58 us
    pallas_call x1, Pallas kernels, body(): call(lambda *refs: diagonal_kernel(grid, *refs), (full((height, width)),...  1.82 us
    pallas_call x1, Pallas kernels, body(): call(lambda *refs: cbar_kernel(grid, *refs), (full((width, depth)), full(...  1.33 us
    pallas_call x1, Pallas kernels, body(): call(trailing_kernel, (full((n // 2, breadth)),) * 2, flops=1000000000)  0.97 us
  transfers between devices with their start and end apart: 16, of which 5 were waited for; matrix products, arithmetic and copies ran while one was open for 0% of the time, Pallas kernels for 26%

profile of v2, /device:TPU:0, one launch (start us, length us, event | category | flops | bytes accessed | tf_op | source)
XLA Modules:
  0.0 38.3 jit_solution(16120951085975742862)
XLA Ops:
  0.6 3.1 %collective-permute-start.3 = (f32[8,2048]{1,0:T(8,128)}, f32[8,2048]{1,0:T(8,128)S(1)}, u32[]{:S(2)}, u32[]{:S(2)}) collective-permute-start(f32[8,2048]{1,0:T(8,128)} %param.12), channel_id=1, source_target_pairs={{0,8},{2,10},{4,12},{6,14},{8,0},{10,2},{12,4},{14,6},{16,24},{18,... | collective-permute-start | bytes 196616 | tf_op jit(solution)/shard_map/ppermute | solution.py:39
  3.7 2.6 %collective-permute-start.4 = (f32[8,2048]{1,0:T(8,128)}, f32[8,2048]{1,0:T(8,128)S(1)}, u32[]{:S(2)}, u32[]{:S(2)}) collective-permute-start(f32[8,2048]{1,0:T(8,128)} %param.12), channel_id=1, source_target_pairs={{0,16},{2,18},{4,20},{6,22},{8,24},{10,26},{12,28},{14,30},{16,0},... | collective-permute-start | bytes 196616 | tf_op jit(solution)/shard_map/ppermute | solution.py:39
  6.3 0.0 collective-permute-start.5
  6.3 1.7 %collective-permute-start = (f32[64,512]{1,0:T(8,128)}, f32[64,512]{1,0:T(8,128)S(1)}, u32[]{:S(2)}, u32[]{:S(2)}) collective-permute-start(f32[64,512]{1,0:T(8,128)} %bitcast.3), channel_id=1, source_target_pairs={{0,1},{1,0},{2,3},{3,2},{4,5},{5,4},{6,7},{7,6},{8,9},{9,8},{10,11... | collective-permute-start | bytes 393224 | tf_op jit(solution)/shard_map/ppermute | solution.py:39
  8.1 0.0 copy-start.1
  8.1 0.3 collective-permute-start.1
  8.4 0.5 %copy-done.1 = f32[128,128]{1,0:T(8,128)S(1)} copy-done((f32[128,128]{1,0:T(8,128)S(1)}, f32[128,128]{1,0:T(8,128)}, u32[]{:S(2)}) %copy-start.1) | copy-done | bytes 65560
  8.9 0.0 copy-start.6
  8.9 0.0 copy-start.4
  8.9 0.0 copy-start.5
  8.9 3.4 %shard_map.112 = (f32[128,128]{1,0:T(8,128)S(1)}, bf16[512,2048]{1,0:T(8,128)(2,1)S(1)}, bf16[512,2048]{1,0:T(8,128)(2,1)S(1)}) custom-call(f32[128,128]{1,0:T(8,128)S(1)} %copy-done.1, f32[128,128]{1,0:T(8,128)S(1)} %shard_map.111.identity_ref, f32[512,2048]{1,0:T(8,128)} %b_hbm.1), custom_call_target="tpu_custom_call" | custom-call | flops 4000000000 | bytes 1 | tf_op jit(solution)/shard_map/pallas_call | solution.py:256
  12.3 0.0 copy-done.6
  12.4 0.0 collective-permute-done.3
  12.4 0.0 collective-permute-done.4
  12.4 0.2 collective-permute-done.5
  12.6 1.6 %collective-permute-start.6 = (f32[32,2048]{1,0:T(8,128)S(1)}, f32[32,2048]{1,0:T(8,128)S(1)}, u32[]{:S(2)}, u32[]{:S(2)}) collective-permute-start(f32[32,2048]{1,0:T(8,128)S(1)} %pad_maximum_fusion), channel_id=1, source_target_pairs={{0,4},{2,6},{4,0},{6,2},{8,12},{10,14},{12,8},{14,10},{16,20},{18,... | collective-permute-start | bytes 786440 | tf_op jit(solution)/shard_map/ppermute | solution.py:39
  14.2 0.0 collective-permute-done.refs_2_
  14.2 0.0 collective-permute-done.1.refs_4_
  14.2 0.0 copy-done.4
  14.2 0.0 copy-done.5
  14.2 1.3 %shard_map.113 = (f32[64,512]{1,0:T(8,128)}, f32[8,1152]{1,0:T(8,128)S(1)}, f32[128,512]{1,0:T(8,128)S(1)}, bf16[256,512]{1,0:T(8,128)(2,1)S(1)}) custom-call(f32[128,128]{1,0:T(8,128)S(1)} %get-tuple-element.21.refs_0_.refs_1_, f32[64,512]{1,0:T(8,128)S(1)} %bitcast.4, f32[64,512]{1,0:T(8,128)S(1)} %collective-permute-done.refs_2_, f32[64,512]{1,0:T(8,128)S(1)} %bitcast.6, ...), custom_call_target="tpu_custom_call" | custom-call | flops 1000000000 | bytes 1 | tf_op jit(solution)/shard_map/pallas_call | solution.py:263
  15.6 0.0 copy-start
  15.6 1.0 %shard_map.114 = (f32[64,2048]{1,0:T(8,128)S(1)}, f32[64,2048]{1,0:T(8,128)S(1)}) custom-call(bf16[256,512]{1,0:T(8,128)(2,1)S(1)} %get-tuple-element.25.stack_ref, bf16[512,2048]{1,0:T(8,128)(2,1)S(1)} %get-tuple-element.26.high_ref, bf16[512,2048]{1,0:T(8,128)(2,1)S(1)} %get-tuple-element.27.low_ref), custom_call_target="tpu_custom_call" | custom-call | flops 1000000000 | bytes 1 | tf_op jit(solution)/shard_map/pallas_call | solution.py:269
  16.5 0.1 collective-permute-start.7
  16.6 0.5 %collective-permute-start.2 = (f32[8,1152]{1,0:T(8,128)S(1)}, f32[8,1152]{1,0:T(8,128)S(1)}, u32[]{:S(2)}, u32[]{:S(2)}) collective-permute-start(f32[8,1152]{1,0:T(8,128)S(1)} %get-tuple-element.24), channel_id=1, source_target_pairs={{0,2},{2,0},{4,6},{6,4},{8,10},{10,8},{12,14},{14,12},{16,18},{18,... | collective-permute-start | bytes 110600 | tf_op jit(solution)/shard_map/ppermute | solution.py:39
  17.1 1.4 %collective-permute-done.2 = f32[8,1152]{1,0:T(8,128)S(1)} collective-permute-done((f32[8,1152]{1,0:T(8,128)S(1)}, f32[8,1152]{1,0:T(8,128)S(1)}, u32[]{:S(2)}, u32[]{:S(2)}) %collective-permute-start.2) | collective-permute-done | bytes 36896 | tf_op jit(solution)/shard_map/ppermute | solution.py:39
  18.6 0.9 %collective-permute-done.6 = f32[32,2048]{1,0:T(8,128)S(1)} collective-permute-done((f32[32,2048]{1,0:T(8,128)S(1)}, f32[32,2048]{1,0:T(8,128)S(1)}, u32[]{:S(2)}, u32[]{:S(2)}) %collective-permute-start.6) | collective-permute-done | bytes 262176 | tf_op jit(solution)/shard_map/ppermute | solution.py:39
  19.5 0.0 collective-permute-done.7
  19.5 0.1 add.25
  19.6 1.6 %collective-permute-start.11 = (f32[32,2048]{1,0:T(8,128)S(1)}, f32[32,2048]{1,0:T(8,128)S(1)}, u32[]{:S(2)}, u32[]{:S(2)}) collective-permute-start(f32[32,2048]{1,0:T(8,128)S(1)} %unstack.25), channel_id=1, source_target_pairs={{0,4},{2,6},{4,0},{6,2},{8,12},{10,14},{12,8},{14,10},{16,20},{18,... | collective-permute-start | bytes 786440 | tf_op jit(solution)/shard_map/ppermute | solution.py:39
  21.2 0.6 %collective-permute-start.8 = (f32[8,1152]{1,0:T(8,128)S(1)}, f32[8,1152]{1,0:T(8,128)S(1)}, u32[]{:S(2)}, u32[]{:S(2)}) collective-permute-start(f32[8,1152]{1,0:T(8,128)S(1)} %add.24), channel_id=1, source_target_pairs={{0,8},{2,10},{4,12},{6,14},{8,0},{10,2},{12,4},{14,6},{16,24},{18,... | collective-permute-start | bytes 110600 | tf_op jit(solution)/shard_map/ppermute | solution.py:39
  21.8 3.3 %collective-permute-done.8 = f32[8,1152]{1,0:T(8,128)S(1)} collective-permute-done((f32[8,1152]{1,0:T(8,128)S(1)}, f32[8,1152]{1,0:T(8,128)S(1)}, u32[]{:S(2)}, u32[]{:S(2)}) %collective-permute-start.8) | collective-permute-done | bytes 36896 | tf_op jit(solution)/shard_map/ppermute | solution.py:39
  25.1 2.1 %collective-permute-start.10 = (f32[8,1152]{1,0:T(8,128)S(1)}, f32[8,1152]{1,0:T(8,128)S(1)}, u32[]{:S(2)}, u32[]{:S(2)}) collective-permute-start(f32[8,1152]{1,0:T(8,128)S(1)} %add.26), channel_id=1, source_target_pairs={{0,16},{2,18},{4,20},{6,22},{8,24},{10,26},{12,28},{14,30},{16,0},... | collective-permute-start | bytes 110600 | tf_op jit(solution)/shard_map/ppermute | solution.py:39
  27.2 0.0 collective-permute-start.9
  27.2 0.0 collective-permute-done.11
  27.3 2.1 %collective-permute-start.13 = (f32[8,2048]{1,0:T(8,128)S(1)}, f32[8,2048]{1,0:T(8,128)S(1)}, u32[]{:S(2)}, u32[]{:S(2)}) collective-permute-start(f32[8,2048]{1,0:T(8,128)S(1)} %get-tuple-element.40), channel_id=1, source_target_pairs={{0,8},{2,10},{4,12},{6,14},{8,0},{10,2},{12,4},{14,6},{16,24},{18,... | collective-permute-start | bytes 196616 | tf_op jit(solution)/shard_map/ppermute | solution.py:39
  29.4 1.9 %collective-permute-start.14 = (f32[8,2048]{1,0:T(8,128)S(1)}, f32[8,2048]{1,0:T(8,128)S(1)}, u32[]{:S(2)}, u32[]{:S(2)}) collective-permute-start(f32[8,2048]{1,0:T(8,128)S(1)} %get-tuple-element.39), channel_id=1, source_target_pairs={{0,16},{2,18},{4,20},{6,22},{8,24},{10,26},{12,28},{14,30},{16,0},... | collective-permute-start | bytes 196616 | tf_op jit(solution)/shard_map/ppermute | solution.py:39
  31.2 0.6 %collective-permute-start.15 = (f32[8,2048]{1,0:T(8,128)S(1)}, f32[8,2048]{1,0:T(8,128)S(1)}, u32[]{:S(2)}, u32[]{:S(2)}) collective-permute-start(f32[8,2048]{1,0:T(8,128)S(1)} %get-tuple-element.38), channel_id=1, source_target_pairs={{0,24},{2,26},{4,28},{6,30},{8,16},{10,18},{12,20},{14,22},{16,8},... | collective-permute-start | bytes 196616 | tf_op jit(solution)/shard_map/ppermute | solution.py:39
  31.8 0.0 collective-permute-done.10
  31.8 1.2 %collective-permute-start.12 = (f32[8,1152]{1,0:T(8,128)S(1)}, f32[8,1152]{1,0:T(8,128)S(1)}, u32[]{:S(2)}, u32[]{:S(2)}) collective-permute-start(f32[8,1152]{1,0:T(8,128)S(1)} %add.27.refs_6_), channel_id=1, source_target_pairs={{0,4},{2,6},{4,0},{6,2},{8,12},{10,14},{12,8},{14,10},{16,20},{18,... | collective-permute-start | bytes 110600 | tf_op jit(solution)/shard_map/ppermute | solution.py:39
  33.0 0.0 collective-permute-done.9.refs_1_.refs_5_
  33.0 0.0 copy-done
  33.0 0.0 copy-start.2
  33.0 0.0 copy-start.3
  33.0 2.6 %shard_map.115 = f32[512,2048]{1,0:T(8,128)} custom-call(f32[128,512]{1,0:T(8,128)S(1)} %get-tuple-element.23.perm_ref, f32[512,2048]{1,0:T(8,128)S(1)} %copy-done, f32[64,2048]{1,0:T(8,128)S(1)} %constant_dynamic-update-slice_fusion.refs_0_.refs_4_, f32[64,2048]{1,0:T(8,128)S(1)} %collective-permute-done.9.refs_1_.refs_5_), custom_call_target="tpu_custom_call" | custom-call | bytes 1 | tf_op jit(solution)/shard_map/pallas_call | solution.py:278
  35.6 0.2 collective-permute-done.12.refs_7_
  35.8 0.0 copy-done.2
  35.8 0.0 copy-done.3
  35.8 1.8 %shard_map.116 = (f32[8,64]{1,0:T(8,128)}, f32[8,2048]{1,0:T(8,128)S(1)}) custom-call(f32[128,128]{1,0:T(8,128)S(1)} %copy-done.1, f32[128,128]{1,0:T(8,128)S(1)} %get-tuple-element.21.refs_0_.refs_1_, f32[128,128]{1,0:T(8,128)S(1)} %copy-done.2, f32[8,2048]{1,0:T(8,128)S(1)} %copy-done.3, f32[64,2048]{1,0:T(8,128)S(1)} %constant_dynamic-update-slice_fusion.refs_0_.refs_4_, ...), custom_call_target="tpu_custom_call" | custom-call | bytes 1 | tf_op jit(solution)/shard_map/pallas_call | solution.py:294
  37.7 0.0 collective-permute-done.13
  37.7 0.0 collective-permute-done.14
  37.7 0.0 collective-permute-done.15
  37.7 0.7 %fusion.1 = f32[8,2048]{1,0:T(8,128)} fusion(f32[8,2048]{1,0:T(8,128)S(1)} %get-tuple-element.37, f32[8,2048]{1,0:T(8,128)S(1)} %collective-permute-done.13, f32[32,2048]{1,0:T(8,128)S(1)} %slice_add_fusion, f32[8,2048]{1,0:T(8,128)S(1)} %collective-permute-done.14, f32[8,2048]{1,0:T(8,128)S(1)} %collective-permute-done.15), kind=kLoop, calls=%fused_computation.4 | loop fusion | flops 65536 | bytes 393216 | tf_op jit(solution)/shard_map/sub | solution.py:297
  (13 shorter events, 0.2 us)
Async XLA Ops:
  0.6 11.7 %collective-permute-start.3 = (f32[8,2048]{1,0:T(8,128)}, f32[8,2048]{1,0:T(8,128)S(1)}, u32[]{:S(2)}, u32[]{:S(2)}) collective-permute-start(f32[8,2048]{1,0:T(8,128)} %param.12), channel_id=1, source_target_pairs={{0,8},{2,10},{4,12},{6,14},{8,0},{10,2},{12,4},{14,6},{16,24},{18,... | collective-permute-start | bytes 196616 | tf_op jit(solution)/shard_map/ppermute | solution.py:39
  3.7 8.7 %collective-permute-start.4 = (f32[8,2048]{1,0:T(8,128)}, f32[8,2048]{1,0:T(8,128)S(1)}, u32[]{:S(2)}, u32[]{:S(2)}) collective-permute-start(f32[8,2048]{1,0:T(8,128)} %param.12), channel_id=1, source_target_pairs={{0,16},{2,18},{4,20},{6,22},{8,24},{10,26},{12,28},{14,30},{16,0},... | collective-permute-start | bytes 196616 | tf_op jit(solution)/shard_map/ppermute | solution.py:39
  6.3 6.3 %collective-permute-start.5 = (f32[8,2048]{1,0:T(8,128)}, f32[8,2048]{1,0:T(8,128)S(1)}, u32[]{:S(2)}, u32[]{:S(2)}) collective-permute-start(f32[8,2048]{1,0:T(8,128)} %param.12), channel_id=1, source_target_pairs={{0,24},{2,26},{4,28},{6,30},{8,16},{10,18},{12,20},{14,22},{16,8},... | collective-permute-start | bytes 196616 | tf_op jit(solution)/shard_map/ppermute | solution.py:39
  6.3 7.9 %collective-permute-start = (f32[64,512]{1,0:T(8,128)}, f32[64,512]{1,0:T(8,128)S(1)}, u32[]{:S(2)}, u32[]{:S(2)}) collective-permute-start(f32[64,512]{1,0:T(8,128)} %bitcast.3), channel_id=1, source_target_pairs={{0,1},{1,0},{2,3},{3,2},{4,5},{5,4},{6,7},{7,6},{8,9},{9,8},{10,11... | collective-permute-start | bytes 393224 | tf_op jit(solution)/shard_map/ppermute | solution.py:39
  8.1 0.8 %copy-start.1 = (f32[128,128]{1,0:T(8,128)S(1)}, f32[128,128]{1,0:T(8,128)}, u32[]{:S(2)}) copy-start(f32[128,128]{1,0:T(8,128)} %refs_0_.1) | copy-start | bytes 196612
  8.1 6.2 %collective-permute-start.1 = (f32[64,512]{1,0:T(8,128)}, f32[64,512]{1,0:T(8,128)S(1)}, u32[]{:S(2)}, u32[]{:S(2)}) collective-permute-start(f32[64,512]{1,0:T(8,128)} %bitcast.5), channel_id=1, source_target_pairs={{0,1},{1,0},{2,3},{3,2},{4,5},{5,4},{6,7},{7,6},{8,9},{9,8},{10,11... | collective-permute-start | bytes 393224 | tf_op jit(solution)/shard_map/ppermute | solution.py:39
  8.9 3.4 %copy-start.6 = (f32[8,2048]{1,0:T(8,128)S(1)}, f32[8,2048]{1,0:T(8,128)}, u32[]{:S(2)}) copy-start(f32[8,2048]{1,0:T(8,128)} %param.12) | copy-start | bytes 196612
  8.9 5.3 %copy-start.4 = (f32[512,64]{0,1:T(8,128)S(1)}, f32[512,64]{0,1:T(8,128)}, u32[]{:S(2)}) copy-start(f32[512,64]{0,1:T(8,128)} %param.9) | copy-start | bytes 393220
  8.9 5.3 %copy-start.5 = (f32[512,64]{0,1:T(8,128)S(1)}, f32[512,64]{0,1:T(8,128)}, u32[]{:S(2)}) copy-start(f32[512,64]{0,1:T(8,128)} %param.8) | copy-start | bytes 393220
  12.6 6.8 %collective-permute-start.6 = (f32[32,2048]{1,0:T(8,128)S(1)}, f32[32,2048]{1,0:T(8,128)S(1)}, u32[]{:S(2)}, u32[]{:S(2)}) collective-permute-start(f32[32,2048]{1,0:T(8,128)S(1)} %pad_maximum_fusion), channel_id=1, source_target_pairs={{0,4},{2,6},{4,0},{6,2},{8,12},{10,14},{12,8},{14,10},{16,20},{18,... | collective-permute-start | bytes 786440 | tf_op jit(solution)/shard_map/ppermute | solution.py:39
  15.6 17.4 %copy-start = (f32[512,2048]{1,0:T(8,128)S(1)}, f32[512,2048]{1,0:T(8,128)}, u32[]{:S(2)}) copy-start(f32[512,2048]{1,0:T(8,128)} %bbar_ref.1) | copy-start | bytes 12582916
  16.5 3.0 %collective-permute-start.7 = (f32[64,2048]{1,0:T(8,128)S(1)}, f32[64,2048]{1,0:T(8,128)S(1)}, u32[]{:S(2)}, u32[]{:S(2)}) collective-permute-start(f32[64,2048]{1,0:T(8,128)S(1)} %get-tuple-element.30), channel_id=1, source_target_pairs={{0,2},{2,0},{4,6},{6,4},{8,10},{10,8},{12,14},{14,12},{16,18},{18,... | collective-permute-start | bytes 1572872 | tf_op jit(solution)/shard_map/ppermute | solution.py:39
  16.6 1.9 %collective-permute-start.2 = (f32[8,1152]{1,0:T(8,128)S(1)}, f32[8,1152]{1,0:T(8,128)S(1)}, u32[]{:S(2)}, u32[]{:S(2)}) collective-permute-start(f32[8,1152]{1,0:T(8,128)S(1)} %get-tuple-element.24), channel_id=1, source_target_pairs={{0,2},{2,0},{4,6},{6,4},{8,10},{10,8},{12,14},{14,12},{16,18},{18,... | collective-permute-start | bytes 110600 | tf_op jit(solution)/shard_map/ppermute | solution.py:39
  19.6 7.6 %collective-permute-start.11 = (f32[32,2048]{1,0:T(8,128)S(1)}, f32[32,2048]{1,0:T(8,128)S(1)}, u32[]{:S(2)}, u32[]{:S(2)}) collective-permute-start(f32[32,2048]{1,0:T(8,128)S(1)} %unstack.25), channel_id=1, source_target_pairs={{0,4},{2,6},{4,0},{6,2},{8,12},{10,14},{12,8},{14,10},{16,20},{18,... | collective-permute-start | bytes 786440 | tf_op jit(solution)/shard_map/ppermute | solution.py:39
  21.2 4.0 %collective-permute-start.8 = (f32[8,1152]{1,0:T(8,128)S(1)}, f32[8,1152]{1,0:T(8,128)S(1)}, u32[]{:S(2)}, u32[]{:S(2)}) collective-permute-start(f32[8,1152]{1,0:T(8,128)S(1)} %add.24), channel_id=1, source_target_pairs={{0,8},{2,10},{4,12},{6,14},{8,0},{10,2},{12,4},{14,6},{16,24},{18,... | collective-permute-start | bytes 110600 | tf_op jit(solution)/shard_map/ppermute | solution.py:39
  25.1 6.7 %collective-permute-start.10 = (f32[8,1152]{1,0:T(8,128)S(1)}, f32[8,1152]{1,0:T(8,128)S(1)}, u32[]{:S(2)}, u32[]{:S(2)}) collective-permute-start(f32[8,1152]{1,0:T(8,128)S(1)} %add.26), channel_id=1, source_target_pairs={{0,16},{2,18},{4,20},{6,22},{8,24},{10,26},{12,28},{14,30},{16,0},... | collective-permute-start | bytes 110600 | tf_op jit(solution)/shard_map/ppermute | solution.py:39
  27.2 5.8 %collective-permute-start.9 = (f32[64,2048]{1,0:T(8,128)S(1)}, f32[64,2048]{1,0:T(8,128)S(1)}, u32[]{:S(2)}, u32[]{:S(2)}) collective-permute-start(f32[64,2048]{1,0:T(8,128)S(1)} %constant_dynamic-update-slice_fusion.refs_0_.refs_4_), channel_id=1, source_target_pairs={{0,2},{2,0},{4,6},{6,4},{8,10},{10,8},{12,14},{14,12},{16,18},{18,... | collective-permute-start | bytes 1572872 | tf_op jit(solution)/shard_map/ppermute | solution.py:39
  27.3 10.4 %collective-permute-start.13 = (f32[8,2048]{1,0:T(8,128)S(1)}, f32[8,2048]{1,0:T(8,128)S(1)}, u32[]{:S(2)}, u32[]{:S(2)}) collective-permute-start(f32[8,2048]{1,0:T(8,128)S(1)} %get-tuple-element.40), channel_id=1, source_target_pairs={{0,8},{2,10},{4,12},{6,14},{8,0},{10,2},{12,4},{14,6},{16,24},{18,... | collective-permute-start | bytes 196616 | tf_op jit(solution)/shard_map/ppermute | solution.py:39
  29.4 8.3 %collective-permute-start.14 = (f32[8,2048]{1,0:T(8,128)S(1)}, f32[8,2048]{1,0:T(8,128)S(1)}, u32[]{:S(2)}, u32[]{:S(2)}) collective-permute-start(f32[8,2048]{1,0:T(8,128)S(1)} %get-tuple-element.39), channel_id=1, source_target_pairs={{0,16},{2,18},{4,20},{6,22},{8,24},{10,26},{12,28},{14,30},{16,0},... | collective-permute-start | bytes 196616 | tf_op jit(solution)/shard_map/ppermute | solution.py:39
  31.2 6.5 %collective-permute-start.15 = (f32[8,2048]{1,0:T(8,128)S(1)}, f32[8,2048]{1,0:T(8,128)S(1)}, u32[]{:S(2)}, u32[]{:S(2)}) collective-permute-start(f32[8,2048]{1,0:T(8,128)S(1)} %get-tuple-element.38), channel_id=1, source_target_pairs={{0,24},{2,26},{4,28},{6,30},{8,16},{10,18},{12,20},{14,22},{16,8},... | collective-permute-start | bytes 196616 | tf_op jit(solution)/shard_map/ppermute | solution.py:39
  31.8 4.0 %collective-permute-start.12 = (f32[8,1152]{1,0:T(8,128)S(1)}, f32[8,1152]{1,0:T(8,128)S(1)}, u32[]{:S(2)}, u32[]{:S(2)}) collective-permute-start(f32[8,1152]{1,0:T(8,128)S(1)} %add.27.refs_6_), channel_id=1, source_target_pairs={{0,4},{2,6},{4,0},{6,2},{8,12},{10,14},{12,8},{14,10},{16,20},{18,... | collective-permute-start | bytes 110600 | tf_op jit(solution)/shard_map/ppermute | solution.py:39
  33.0 2.8 %copy-start.2 = (f32[128,128]{1,0:T(8,128)S(1)}, f32[128,128]{1,0:T(8,128)}, u32[]{:S(2)}) copy-start(f32[128,128]{1,0:T(8,128)} %refs_2_.1) | copy-start | bytes 196612
  33.0 2.8 %copy-start.3 = (f32[8,2048]{1,0:T(8,128)S(1)}, f32[8,2048]{1,0:T(8,128)}, u32[]{:S(2)}) copy-start(f32[8,2048]{1,0:T(8,128)} %refs_3_.1) | copy-start | bytes 196612

commit v3 on v2

--- a/solution.py
+++ b/solution.py
@@ -29,6 +29,24 @@
 def split(value):
     high = value.astype(BF16)
     return high, (value - high.astype(F32)).astype(BF16)
+
+
+def split3(value):
+    high = value.astype(BF16)
+    rest = value - high.astype(F32)
+    middle = rest.astype(BF16)
+    return high, middle, (rest - middle.astype(F32)).astype(BF16)
+
+
+def dot6(a, b):
+    a1, a2, a3 = split3(a)
+    b1, b2, b3 = split3(b)
+    n = b.shape[1]
+    left = jnp.concatenate([a1, a2], axis=1)
+    right = jnp.concatenate([jnp.concatenate([b1, b1], axis=0), jnp.concatenate([b2, b2], axis=0)], axis=1)
+    large = dot(left, right, precision=None)
+    small = dot(jnp.concatenate([a1, a3], axis=1), jnp.concatenate([b3, b1], axis=0), precision=None)
+    return large[:, :n] + (large[:, n:] + small)
 
 
 def hot(cond):
@@ -81,7 +99,7 @@
     out_ref[...] = hot(i == j)
 
 
-def prepare_kernel(factor_ref, identity_ref, b_hbm, inverse_ref, high_ref, low_ref, b_ref, sems):
+def prepare_kernel(factor_ref, identity_ref, b_hbm, inverse_t_ref, high_ref, low_ref, b_ref, sems):
     chunks = sems.shape[0]
     step = b_ref.shape[0] // chunks
     copies = [
@@ -109,11 +127,11 @@
         if level == 0:
             inverse = jnp.where(i == j, recip_row, -(recip_col * block * recip_row))
         else:
-            inverse = inverse - dot(dot(inverse, block), inverse)
+            inverse = inverse - dot6(dot6(inverse, block), inverse)
         if 2 <= level < 2 + chunks:
             split_chunk(level - 2)
         size, level = 2 * size, level + 1
-    inverse_ref[...] = inverse
+    inverse_t_ref[...] = inverse.T
     for k in range(max(level - 2, 0), chunks):
         split_chunk(k)
 
@@ -140,17 +158,17 @@
     return jnp.concatenate([upper, jnp.concatenate([folded[:m, :m], corner], axis=1)], axis=0)
 
 
-def cbar_kernel(grid, inverse_ref, *refs):
+def cbar_kernel(grid, inverse_t_ref, *refs):
     cols = grid.cols
     cbar_refs, c_refs = refs[:cols], refs[cols:2 * cols]
     out_ref, product_ref, perm_ref, stack_ref, cbar, c, new = refs[2 * cols:]
     me, my_col = lax.axis_index("row"), lax.axis_index("col")
-    n = inverse_ref.shape[0]
+    n = inverse_t_ref.shape[0]
     for d in range(cols):
         at = pl.ds(pl.multiple_of((my_col ^ d) * grid.width, grid.width), grid.width)
         cbar[at, :] = cbar_refs[d][...]
         c[at, :] = c_refs[d][...]
-    absolute = dot(inverse_ref[...].T, cbar[...])
+    absolute = dot6(inverse_t_ref[...], cbar[...])
     new[...] = absolute
     perm = grid.permute_rows(new, me)
     perm_ref[...] = perm
@@ -189,28 +207,33 @@
         copy.wait()
 
 
-def diagonal_kernel(grid, factor_ref, inverse_ref, dbar_ref, rbar_ref, *refs):
+def diagonal_kernel(grid, factor_ref, inverse_t_ref, dbar_ref, rbar_ref, *refs):
     cores = grid.core[0]
     panel_refs, products, (out_ref, rbar_out_ref) = refs[:cores], refs[cores:-2], refs[-2:]
     me, my_col = lax.axis_index("row"), lax.axis_index("col")
     n, height, width = factor_ref.shape[0], grid.height, grid.width
-    i, j = iotas((n, n))
-    inverse = inverse_ref[...]
-    si, sj = iotas((height, n))
-    own_row = me * height + si
-    weights = dot(hot(sj == own_row), inverse.T)
-    inverse_perm = dot(inverse, hot(i == grid.relative_row(j, me)))
     product = unfold(add_pairs([ref[...] for ref in products]), n)
-    proj = phi(dot(factor_ref[...].T, dbar_ref[...] - product))
-    half = dot(weights, proj + proj.T)
-    rows_sym, rows_perm = dot(half, inverse), dot(half, inverse_perm)
-    high, low = split(rows_perm)
+    proj = phi(dot6(factor_ref[...].T, dbar_ref[...] - product))
+    if height % 8 == 0:
+        weights = inverse_t_ref[pl.ds(pl.multiple_of(me * height, height), height), :]
+    else:
+        si, sj = iotas((height, n))
+        weights = dot(hot(sj == me * height + si), inverse_t_ref[...])
+    half = dot6(weights, proj + proj.T)
+    both = jnp.concatenate([inverse_t_ref[...], grid.permute_rows(inverse_t_ref, me)], axis=0)
+    rows = dot6(half, both.T)
+    rows_sym = rows[:, :n]
+    high, low = split(rows[:, n:])
     panel_high, panel_low = split(jnp.concatenate([ref[...] for ref in panel_refs], axis=0))
     update = dot(high, panel_high, precision=None) + dot(low, panel_high, precision=None) + dot(high, panel_low, precision=None)
     rbar_out_ref[...] = rbar_ref[...] - update
+    si, sj = iotas((height, n))
+    own_row = me * height + si
     rows_kernel = jnp.where(sj < own_row, rows_sym, jnp.where(sj == own_row, 0.5 * rows_sym, 0.0))
-    ci, cj = iotas((n, width))
-    out_ref[...] = dot(rows_kernel, hot(ci == my_col * width + cj))
+    out = rows_kernel[:, :width]
+    for k in range(1, grid.cols):
+        out = jnp.where(my_col == k, rows_kernel[:, k * width:(k + 1) * width], out)
+    out_ref[...] = out
 
 
 def call(kernel, out_shape, scratch=(), limit=8 * MIB, flops=0, specs=None):
@@ -249,11 +272,11 @@
         grid = Grid(rows, cols, height, width)
 
         cbar_parts, c_parts = col_parts(cbar_in.T), col_parts(c_panel.T)
+        identity = call(identity_kernel, full((n, n)), flops=4 * 10 ** 9)()
         panel = jnp.concatenate(row_parts(r_panel, grid.z), axis=0)
         panel = jnp.concatenate(row_parts(panel, grid.x), axis=0)
 
-        identity = call(identity_kernel, full((n, n)), flops=4 * 10 ** 9)()
-        inverse, high, low = call(
+        inverse_t, high, low = call(
             prepare_kernel,
             (full((n, n)), full((depth, breadth), BF16), full((depth, breadth), BF16)),
             [pltpu.VMEM((depth, breadth), F32), pltpu.SemaphoreType.DMA((8,))],
@@ -264,7 +287,7 @@
             lambda *refs: cbar_kernel(grid, *refs),
             (full((width, depth)), full((8, (n // 16 + 1) * n)), full((n, depth)), full((2 * n, depth), BF16)),
             [pltpu.VMEM((n, depth), F32)] * 3, flops=1000000000,
-        )(inverse, *cbar_parts, *c_parts)
+        )(inverse_t, *cbar_parts, *c_parts)
 
         keep, send = call(trailing_kernel, (full((n // 2, breadth)),) * 2, flops=1000000000)(stack, high, low)
         summed = after(keep, panel) + swap(send, "row", rows, grid.core[1])
@@ -293,7 +316,7 @@
                 product = after(product, summed)
         kernel_out, rbar = call(
             lambda *refs: diagonal_kernel(grid, *refs), (full((height, width)), full((height, breadth))), flops=0
-        )(factor, inverse, dbar_in, rbar_in, *panel_parts, *row_parts(product, grid.x))
+        )(factor, inverse_t, dbar_in, rbar_in, *panel_parts, *row_parts(product, grid.x))
         return (cbar_out_t.T, bbar_out, kernel_out, rbar - summed)
 
     return body

time: 38.5 us -> 38 us (0.987)
  Pallas kernels: 10.1 us -> 9.42 us
  starting transfers between devices: 19.8 us -> 20.2 us
    ppermute x16, starting transfers between devices: 19.8 us -> 20.2 us  [swap(): return lax.ppermute(value, axis, [(i, i ^ offset) for i in range(size)])]
  transfers between devices with their start and end apart: 16 -> 16, of which waited for: 5 -> 5; matrix products, arithmetic and copies ran while one was open for 0% -> 0% of each run, Pallas kernels for 26% -> 25%
where the time goes in v3:
time: 38 us; the launch traced here: 37.9 us
  starting transfers between devices  20.2 us (53%)
  Pallas kernels  9.42 us (25%)
  waiting for transfers between devices  6 us (16%)
  between operations  0.8 us (2%)
  other arithmetic  0.79 us (2%)
  local copies, waits for them, and re-layouts  0.64 us (2%)
    ppermute x16, starting transfers between devices, swap(): return lax.ppermute(value, axis, [(i, i ^ offset) for i in range(size)])  20.2 us
    ppermute x16, waiting for transfers between devices, swap(): return lax.ppermute(value, axis, [(i, i ^ offset) for i in range(size)])  6 us
    pallas_call x1, Pallas kernels, body(): call(prepare_kernel, (full((n, n)), full((depth, breadth), BF16), full((d...  3.13 us
    pallas_call x1, Pallas kernels, body(): pl.pallas_call(bbar_kernel, in_specs=[pl.BlockSpec(memory_space=pltpu.VME...  2.58 us
    pallas_call x1, Pallas kernels, body(): call(lambda *refs: diagonal_kernel(grid, *refs), (full((height, width)),...  1.58 us
    pallas_call x1, Pallas kernels, body(): call(lambda *refs: cbar_kernel(grid, *refs), (full((width, depth)), full(...  1.15 us
    pallas_call x1, Pallas kernels, body(): call(trailing_kernel, (full((n // 2, breadth)),) * 2, flops=1000000000)  0.97 us
  transfers between devices with their start and end apart: 16, of which 5 were waited for; matrix products, arithmetic and copies ran while one was open for 0% of the time, Pallas kernels for 25%

profile of v3, /device:TPU:0, one launch (start us, length us, event | category | flops | bytes accessed | tf_op | source)
XLA Modules:
  0.0 37.9 jit_solution(16340583950831425192)
XLA Ops:
  0.6 3.1 %collective-permute-start.3 = (f32[8,2048]{1,0:T(8,128)}, f32[8,2048]{1,0:T(8,128)S(1)}, u32[]{:S(2)}, u32[]{:S(2)}) collective-permute-start(f32[8,2048]{1,0:T(8,128)} %param.12), channel_id=1, source_target_pairs={{0,8},{2,10},{4,12},{6,14},{8,0},{10,2},{12,4},{14,6},{16,24},{18,... | collective-permute-start | bytes 196616 | tf_op jit(solution)/shard_map/ppermute | solution.py:57
  3.7 2.6 %collective-permute-start.4 = (f32[8,2048]{1,0:T(8,128)}, f32[8,2048]{1,0:T(8,128)S(1)}, u32[]{:S(2)}, u32[]{:S(2)}) collective-permute-start(f32[8,2048]{1,0:T(8,128)} %param.12), channel_id=1, source_target_pairs={{0,16},{2,18},{4,20},{6,22},{8,24},{10,26},{12,28},{14,30},{16,0},... | collective-permute-start | bytes 196616 | tf_op jit(solution)/shard_map/ppermute | solution.py:57
  6.3 0.0 collective-permute-start.5
  6.3 1.7 %collective-permute-start = (f32[64,512]{1,0:T(8,128)}, f32[64,512]{1,0:T(8,128)S(1)}, u32[]{:S(2)}, u32[]{:S(2)}) collective-permute-start(f32[64,512]{1,0:T(8,128)} %bitcast.3), channel_id=1, source_target_pairs={{0,1},{1,0},{2,3},{3,2},{4,5},{5,4},{6,7},{7,6},{8,9},{9,8},{10,11... | collective-permute-start | bytes 393224 | tf_op jit(solution)/shard_map/ppermute | solution.py:57
  8.1 0.0 copy-start.1
  8.1 0.3 collective-permute-start.1
  8.4 0.5 %copy-done.1 = f32[128,128]{1,0:T(8,128)S(1)} copy-done((f32[128,128]{1,0:T(8,128)S(1)}, f32[128,128]{1,0:T(8,128)}, u32[]{:S(2)}) %copy-start.1) | copy-done | bytes 65560
  8.9 0.0 copy-start.6
  8.9 0.0 copy-start.4
  8.9 0.0 copy-start.5
  8.9 3.1 %shard_map.112 = (f32[128,128]{1,0:T(8,128)S(1)}, bf16[512,2048]{1,0:T(8,128)(2,1)S(1)}, bf16[512,2048]{1,0:T(8,128)(2,1)S(1)}) custom-call(f32[128,128]{1,0:T(8,128)S(1)} %copy-done.1, f32[128,128]{1,0:T(8,128)S(1)} %shard_map.111.identity_ref, f32[512,2048]{1,0:T(8,128)} %b_hbm.1), custom_call_target="tpu_custom_call" | custom-call | flops 4000000000 | bytes 1 | tf_op jit(solution)/shard_map/pallas_call | solution.py:279
  12.0 0.0 copy-done.6
  12.1 0.0 collective-permute-done.3
  12.1 0.0 collective-permute-done.4
  12.1 0.5 %collective-permute-done.5 = f32[8,2048]{1,0:T(8,128)S(1)} collective-permute-done((f32[8,2048]{1,0:T(8,128)}, f32[8,2048]{1,0:T(8,128)S(1)}, u32[]{:S(2)}, u32[]{:S(2)}) %collective-permute-start.5) | collective-permute-done | bytes 65568 | tf_op jit(solution)/shard_map/ppermute | solution.py:57
  12.6 1.6 %collective-permute-start.6 = (f32[32,2048]{1,0:T(8,128)S(1)}, f32[32,2048]{1,0:T(8,128)S(1)}, u32[]{:S(2)}, u32[]{:S(2)}) collective-permute-start(f32[32,2048]{1,0:T(8,128)S(1)} %pad_maximum_fusion), channel_id=1, source_target_pairs={{0,4},{2,6},{4,0},{6,2},{8,12},{10,14},{12,8},{14,10},{16,20},{18,... | collective-permute-start | bytes 786440 | tf_op jit(solution)/shard_map/ppermute | solution.py:57
  14.2 0.0 collective-permute-done.refs_2_
  14.2 0.0 collective-permute-done.1.refs_4_
  14.2 0.0 copy-done.4
  14.2 0.0 copy-done.5
  14.2 1.1 %shard_map.113 = (f32[64,512]{1,0:T(8,128)}, f32[8,1152]{1,0:T(8,128)S(1)}, f32[128,512]{1,0:T(8,128)S(1)}, bf16[256,512]{1,0:T(8,128)(2,1)S(1)}) custom-call(f32[128,128]{1,0:T(8,128)S(1)} %get-tuple-element.21.refs_0_.refs_1_, f32[64,512]{1,0:T(8,128)S(1)} %bitcast.4, f32[64,512]{1,0:T(8,128)S(1)} %collective-permute-done.refs_2_, f32[64,512]{1,0:T(8,128)S(1)} %bitcast.6, ...), custom_call_target="tpu_custom_call" | custom-call | flops 1000000000 | bytes 1 | tf_op jit(solution)/shard_map/pallas_call | solution.py:286
  15.4 0.0 copy-start
  15.4 1.0 %shard_map.114 = (f32[64,2048]{1,0:T(8,128)S(1)}, f32[64,2048]{1,0:T(8,128)S(1)}) custom-call(bf16[256,512]{1,0:T(8,128)(2,1)S(1)} %get-tuple-element.25.stack_ref, bf16[512,2048]{1,0:T(8,128)(2,1)S(1)} %get-tuple-element.26.high_ref, bf16[512,2048]{1,0:T(8,128)(2,1)S(1)} %get-tuple-element.27.low_ref), custom_call_target="tpu_custom_call" | custom-call | flops 1000000000 | bytes 1 | tf_op jit(solution)/shard_map/pallas_call | solution.py:292
  16.4 0.1 collective-permute-start.7
  16.5 0.5 %collective-permute-start.2 = (f32[8,1152]{1,0:T(8,128)S(1)}, f32[8,1152]{1,0:T(8,128)S(1)}, u32[]{:S(2)}, u32[]{:S(2)}) collective-permute-start(f32[8,1152]{1,0:T(8,128)S(1)} %get-tuple-element.24), channel_id=1, source_target_pairs={{0,2},{2,0},{4,6},{6,4},{8,10},{10,8},{12,14},{14,12},{16,18},{18,... | collective-permute-start | bytes 110600 | tf_op jit(solution)/shard_map/ppermute | solution.py:57
  17.0 1.4 %collective-permute-done.2 = f32[8,1152]{1,0:T(8,128)S(1)} collective-permute-done((f32[8,1152]{1,0:T(8,128)S(1)}, f32[8,1152]{1,0:T(8,128)S(1)}, u32[]{:S(2)}, u32[]{:S(2)}) %collective-permute-start.2) | collective-permute-done | bytes 36896 | tf_op jit(solution)/shard_map/ppermute | solution.py:57
  18.4 0.8 %collective-permute-done.6 = f32[32,2048]{1,0:T(8,128)S(1)} collective-permute-done((f32[32,2048]{1,0:T(8,128)S(1)}, f32[32,2048]{1,0:T(8,128)S(1)}, u32[]{:S(2)}, u32[]{:S(2)}) %collective-permute-start.6) | collective-permute-done | bytes 262176 | tf_op jit(solution)/shard_map/ppermute | solution.py:57
  19.2 0.0 collective-permute-done.7
  19.2 0.1 add.25
  19.3 1.6 %collective-permute-start.11 = (f32[32,2048]{1,0:T(8,128)S(1)}, f32[32,2048]{1,0:T(8,128)S(1)}, u32[]{:S(2)}, u32[]{:S(2)}) collective-permute-start(f32[32,2048]{1,0:T(8,128)S(1)} %unstack.25), channel_id=1, source_target_pairs={{0,4},{2,6},{4,0},{6,2},{8,12},{10,14},{12,8},{14,10},{16,20},{18,... | collective-permute-start | bytes 786440 | tf_op jit(solution)/shard_map/ppermute | solution.py:57
  20.9 0.9 %collective-permute-start.8 = (f32[8,1152]{1,0:T(8,128)S(1)}, f32[8,1152]{1,0:T(8,128)S(1)}, u32[]{:S(2)}, u32[]{:S(2)}) collective-permute-start(f32[8,1152]{1,0:T(8,128)S(1)} %add.24), channel_id=1, source_target_pairs={{0,8},{2,10},{4,12},{6,14},{8,0},{10,2},{12,4},{14,6},{16,24},{18,... | collective-permute-start | bytes 110600 | tf_op jit(solution)/shard_map/ppermute | solution.py:57
  21.8 3.0 %collective-permute-done.8 = f32[8,1152]{1,0:T(8,128)S(1)} collective-permute-done((f32[8,1152]{1,0:T(8,128)S(1)}, f32[8,1152]{1,0:T(8,128)S(1)}, u32[]{:S(2)}, u32[]{:S(2)}) %collective-permute-start.8) | collective-permute-done | bytes 36896 | tf_op jit(solution)/shard_map/ppermute | solution.py:57
  24.8 2.2 %collective-permute-start.10 = (f32[8,1152]{1,0:T(8,128)S(1)}, f32[8,1152]{1,0:T(8,128)S(1)}, u32[]{:S(2)}, u32[]{:S(2)}) collective-permute-start(f32[8,1152]{1,0:T(8,128)S(1)} %add.26), channel_id=1, source_target_pairs={{0,16},{2,18},{4,20},{6,22},{8,24},{10,26},{12,28},{14,30},{16,0},... | collective-permute-start | bytes 110600 | tf_op jit(solution)/shard_map/ppermute | solution.py:57
  27.1 0.0 collective-permute-start.9
  27.1 0.0 collective-permute-done.11
  27.1 1.9 %collective-permute-start.13 = (f32[8,2048]{1,0:T(8,128)S(1)}, f32[8,2048]{1,0:T(8,128)S(1)}, u32[]{:S(2)}, u32[]{:S(2)}) collective-permute-start(f32[8,2048]{1,0:T(8,128)S(1)} %get-tuple-element.40), channel_id=1, source_target_pairs={{0,8},{2,10},{4,12},{6,14},{8,0},{10,2},{12,4},{14,6},{16,24},{18,... | collective-permute-start | bytes 196616 | tf_op jit(solution)/shard_map/ppermute | solution.py:57
  29.1 1.9 %collective-permute-start.14 = (f32[8,2048]{1,0:T(8,128)S(1)}, f32[8,2048]{1,0:T(8,128)S(1)}, u32[]{:S(2)}, u32[]{:S(2)}) collective-permute-start(f32[8,2048]{1,0:T(8,128)S(1)} %get-tuple-element.39), channel_id=1, source_target_pairs={{0,16},{2,18},{4,20},{6,22},{8,24},{10,26},{12,28},{14,30},{16,0},... | collective-permute-start | bytes 196616 | tf_op jit(solution)/shard_map/ppermute | solution.py:57
  31.0 0.6 %collective-permute-start.15 = (f32[8,2048]{1,0:T(8,128)S(1)}, f32[8,2048]{1,0:T(8,128)S(1)}, u32[]{:S(2)}, u32[]{:S(2)}) collective-permute-start(f32[8,2048]{1,0:T(8,128)S(1)} %get-tuple-element.38), channel_id=1, source_target_pairs={{0,24},{2,26},{4,28},{6,30},{8,16},{10,18},{12,20},{14,22},{16,8},... | collective-permute-start | bytes 196616 | tf_op jit(solution)/shard_map/ppermute | solution.py:57
  31.6 0.0 collective-permute-done.10
  31.6 1.2 %collective-permute-start.12 = (f32[8,1152]{1,0:T(8,128)S(1)}, f32[8,1152]{1,0:T(8,128)S(1)}, u32[]{:S(2)}, u32[]{:S(2)}) collective-permute-start(f32[8,1152]{1,0:T(8,128)S(1)} %add.27.refs_6_), channel_id=1, source_target_pairs={{0,4},{2,6},{4,0},{6,2},{8,12},{10,14},{12,8},{14,10},{16,20},{18,... | collective-permute-start | bytes 110600 | tf_op jit(solution)/shard_map/ppermute | solution.py:57
  32.8 0.0 collective-permute-done.9.refs_1_.refs_5_
  32.8 0.0 copy-done
  32.8 0.0 copy-start.2
  32.8 0.0 copy-start.3
  32.8 2.6 %shard_map.115 = f32[512,2048]{1,0:T(8,128)} custom-call(f32[128,512]{1,0:T(8,128)S(1)} %get-tuple-element.23.perm_ref, f32[512,2048]{1,0:T(8,128)S(1)} %copy-done, f32[64,2048]{1,0:T(8,128)S(1)} %constant_dynamic-update-slice_fusion.refs_0_.refs_4_, f32[64,2048]{1,0:T(8,128)S(1)} %collective-permute-done.9.refs_1_.refs_5_), custom_call_target="tpu_custom_call" | custom-call | bytes 1 | tf_op jit(solution)/shard_map/pallas_call | solution.py:301
  35.4 0.2 collective-permute-done.12.refs_7_
  35.6 0.0 copy-done.2
  35.6 0.0 copy-done.3
  35.6 1.6 %shard_map.116 = (f32[8,64]{1,0:T(8,128)}, f32[8,2048]{1,0:T(8,128)S(1)}) custom-call(f32[128,128]{1,0:T(8,128)S(1)} %copy-done.1, f32[128,128]{1,0:T(8,128)S(1)} %get-tuple-element.21.refs_0_.refs_1_, f32[128,128]{1,0:T(8,128)S(1)} %copy-done.2, f32[8,2048]{1,0:T(8,128)S(1)} %copy-done.3, f32[64,2048]{1,0:T(8,128)S(1)} %constant_dynamic-update-slice_fusion.refs_0_.refs_4_, ...), custom_call_target="tpu_custom_call" | custom-call | bytes 1 | tf_op jit(solution)/shard_map/pallas_call | solution.py:317
  37.2 0.0 collective-permute-done.13
  37.2 0.0 collective-permute-done.14
  37.2 0.0 collective-permute-done.15
  37.2 0.7 %fusion.1 = f32[8,2048]{1,0:T(8,128)} fusion(f32[8,2048]{1,0:T(8,128)S(1)} %get-tuple-element.37, f32[8,2048]{1,0:T(8,128)S(1)} %collective-permute-done.13, f32[32,2048]{1,0:T(8,128)S(1)} %slice_add_fusion, f32[8,2048]{1,0:T(8,128)S(1)} %collective-permute-done.14, f32[8,2048]{1,0:T(8,128)S(1)} %collective-permute-done.15), kind=kLoop, calls=%fused_computation.4 | loop fusion | flops 65536 | bytes 393216 | tf_op jit(solution)/shard_map/sub | solution.py:320
  (13 shorter events, 0.2 us)
Async XLA Ops:
  0.6 11.4 %collective-permute-start.3 = (f32[8,2048]{1,0:T(8,128)}, f32[8,2048]{1,0:T(8,128)S(1)}, u32[]{:S(2)}, u32[]{:S(2)}) collective-permute-start(f32[8,2048]{1,0:T(8,128)} %param.12), channel_id=1, source_target_pairs={{0,8},{2,10},{4,12},{6,14},{8,0},{10,2},{12,4},{14,6},{16,24},{18,... | collective-permute-start | bytes 196616 | tf_op jit(solution)/shard_map/ppermute | solution.py:57
  3.7 8.4 %collective-permute-start.4 = (f32[8,2048]{1,0:T(8,128)}, f32[8,2048]{1,0:T(8,128)S(1)}, u32[]{:S(2)}, u32[]{:S(2)}) collective-permute-start(f32[8,2048]{1,0:T(8,128)} %param.12), channel_id=1, source_target_pairs={{0,16},{2,18},{4,20},{6,22},{8,24},{10,26},{12,28},{14,30},{16,0},... | collective-permute-start | bytes 196616 | tf_op jit(solution)/shard_map/ppermute | solution.py:57
  6.3 6.3 %collective-permute-start.5 = (f32[8,2048]{1,0:T(8,128)}, f32[8,2048]{1,0:T(8,128)S(1)}, u32[]{:S(2)}, u32[]{:S(2)}) collective-permute-start(f32[8,2048]{1,0:T(8,128)} %param.12), channel_id=1, source_target_pairs={{0,24},{2,26},{4,28},{6,30},{8,16},{10,18},{12,20},{14,22},{16,8},... | collective-permute-start | bytes 196616 | tf_op jit(solution)/shard_map/ppermute | solution.py:57
  6.3 7.9 %collective-permute-start = (f32[64,512]{1,0:T(8,128)}, f32[64,512]{1,0:T(8,128)S(1)}, u32[]{:S(2)}, u32[]{:S(2)}) collective-permute-start(f32[64,512]{1,0:T(8,128)} %bitcast.3), channel_id=1, source_target_pairs={{0,1},{1,0},{2,3},{3,2},{4,5},{5,4},{6,7},{7,6},{8,9},{9,8},{10,11... | collective-permute-start | bytes 393224 | tf_op jit(solution)/shard_map/ppermute | solution.py:57
  8.1 0.8 %copy-start.1 = (f32[128,128]{1,0:T(8,128)S(1)}, f32[128,128]{1,0:T(8,128)}, u32[]{:S(2)}) copy-start(f32[128,128]{1,0:T(8,128)} %refs_0_.1) | copy-start | bytes 196612
  8.1 6.2 %collective-permute-start.1 = (f32[64,512]{1,0:T(8,128)}, f32[64,512]{1,0:T(8,128)S(1)}, u32[]{:S(2)}, u32[]{:S(2)}) collective-permute-start(f32[64,512]{1,0:T(8,128)} %bitcast.5), channel_id=1, source_target_pairs={{0,1},{1,0},{2,3},{3,2},{4,5},{5,4},{6,7},{7,6},{8,9},{9,8},{10,11... | collective-permute-start | bytes 393224 | tf_op jit(solution)/shard_map/ppermute | solution.py:57
  8.9 3.1 %copy-start.6 = (f32[8,2048]{1,0:T(8,128)S(1)}, f32[8,2048]{1,0:T(8,128)}, u32[]{:S(2)}) copy-start(f32[8,2048]{1,0:T(8,128)} %param.12) | copy-start | bytes 196612
  8.9 5.3 %copy-start.4 = (f32[512,64]{0,1:T(8,128)S(1)}, f32[512,64]{0,1:T(8,128)}, u32[]{:S(2)}) copy-start(f32[512,64]{0,1:T(8,128)} %param.9) | copy-start | bytes 393220
  8.9 5.3 %copy-start.5 = (f32[512,64]{0,1:T(8,128)S(1)}, f32[512,64]{0,1:T(8,128)}, u32[]{:S(2)}) copy-start(f32[512,64]{0,1:T(8,128)} %param.8) | copy-start | bytes 393220
  12.6 6.5 %collective-permute-start.6 = (f32[32,2048]{1,0:T(8,128)S(1)}, f32[32,2048]{1,0:T(8,128)S(1)}, u32[]{:S(2)}, u32[]{:S(2)}) collective-permute-start(f32[32,2048]{1,0:T(8,128)S(1)} %pad_maximum_fusion), channel_id=1, source_target_pairs={{0,4},{2,6},{4,0},{6,2},{8,12},{10,14},{12,8},{14,10},{16,20},{18,... | collective-permute-start | bytes 786440 | tf_op jit(solution)/shard_map/ppermute | solution.py:57
  15.4 17.4 %copy-start = (f32[512,2048]{1,0:T(8,128)S(1)}, f32[512,2048]{1,0:T(8,128)}, u32[]{:S(2)}) copy-start(f32[512,2048]{1,0:T(8,128)} %bbar_ref.1) | copy-start | bytes 12582916
  16.4 2.8 %collective-permute-start.7 = (f32[64,2048]{1,0:T(8,128)S(1)}, f32[64,2048]{1,0:T(8,128)S(1)}, u32[]{:S(2)}, u32[]{:S(2)}) collective-permute-start(f32[64,2048]{1,0:T(8,128)S(1)} %get-tuple-element.30), channel_id=1, source_target_pairs={{0,2},{2,0},{4,6},{6,4},{8,10},{10,8},{12,14},{14,12},{16,18},{18,... | collective-permute-start | bytes 1572872 | tf_op jit(solution)/shard_map/ppermute | solution.py:57
  16.5 1.9 %collective-permute-start.2 = (f32[8,1152]{1,0:T(8,128)S(1)}, f32[8,1152]{1,0:T(8,128)S(1)}, u32[]{:S(2)}, u32[]{:S(2)}) collective-permute-start(f32[8,1152]{1,0:T(8,128)S(1)} %get-tuple-element.24), channel_id=1, source_target_pairs={{0,2},{2,0},{4,6},{6,4},{8,10},{10,8},{12,14},{14,12},{16,18},{18,... | collective-permute-start | bytes 110600 | tf_op jit(solution)/shard_map/ppermute | solution.py:57
  19.3 7.8 %collective-permute-start.11 = (f32[32,2048]{1,0:T(8,128)S(1)}, f32[32,2048]{1,0:T(8,128)S(1)}, u32[]{:S(2)}, u32[]{:S(2)}) collective-permute-start(f32[32,2048]{1,0:T(8,128)S(1)} %unstack.25), channel_id=1, source_target_pairs={{0,4},{2,6},{4,0},{6,2},{8,12},{10,14},{12,8},{14,10},{16,20},{18,... | collective-permute-start | bytes 786440 | tf_op jit(solution)/shard_map/ppermute | solution.py:57
  20.9 4.0 %collective-permute-start.8 = (f32[8,1152]{1,0:T(8,128)S(1)}, f32[8,1152]{1,0:T(8,128)S(1)}, u32[]{:S(2)}, u32[]{:S(2)}) collective-permute-start(f32[8,1152]{1,0:T(8,128)S(1)} %add.24), channel_id=1, source_target_pairs={{0,8},{2,10},{4,12},{6,14},{8,0},{10,2},{12,4},{14,6},{16,24},{18,... | collective-permute-start | bytes 110600 | tf_op jit(solution)/shard_map/ppermute | solution.py:57
  24.8 6.8 %collective-permute-start.10 = (f32[8,1152]{1,0:T(8,128)S(1)}, f32[8,1152]{1,0:T(8,128)S(1)}, u32[]{:S(2)}, u32[]{:S(2)}) collective-permute-start(f32[8,1152]{1,0:T(8,128)S(1)} %add.26), channel_id=1, source_target_pairs={{0,16},{2,18},{4,20},{6,22},{8,24},{10,26},{12,28},{14,30},{16,0},... | collective-permute-start | bytes 110600 | tf_op jit(solution)/shard_map/ppermute | solution.py:57
  27.1 5.8 %collective-permute-start.9 = (f32[64,2048]{1,0:T(8,128)S(1)}, f32[64,2048]{1,0:T(8,128)S(1)}, u32[]{:S(2)}, u32[]{:S(2)}) collective-permute-start(f32[64,2048]{1,0:T(8,128)S(1)} %constant_dynamic-update-slice_fusion.refs_0_.refs_4_), channel_id=1, source_target_pairs={{0,2},{2,0},{4,6},{6,4},{8,10},{10,8},{12,14},{14,12},{16,18},{18,... | collective-permute-start | bytes 1572872 | tf_op jit(solution)/shard_map/ppermute | solution.py:57
  27.1 10.1 %collective-permute-start.13 = (f32[8,2048]{1,0:T(8,128)S(1)}, f32[8,2048]{1,0:T(8,128)S(1)}, u32[]{:S(2)}, u32[]{:S(2)}) collective-permute-start(f32[8,2048]{1,0:T(8,128)S(1)} %get-tuple-element.40), channel_id=1, source_target_pairs={{0,8},{2,10},{4,12},{6,14},{8,0},{10,2},{12,4},{14,6},{16,24},{18,... | collective-permute-start | bytes 196616 | tf_op jit(solution)/shard_map/ppermute | solution.py:57
  29.1 8.2 %collective-permute-start.14 = (f32[8,2048]{1,0:T(8,128)S(1)}, f32[8,2048]{1,0:T(8,128)S(1)}, u32[]{:S(2)}, u32[]{:S(2)}) collective-permute-start(f32[8,2048]{1,0:T(8,128)S(1)} %get-tuple-element.39), channel_id=1, source_target_pairs={{0,16},{2,18},{4,20},{6,22},{8,24},{10,26},{12,28},{14,30},{16,0},... | collective-permute-start | bytes 196616 | tf_op jit(solution)/shard_map/ppermute | solution.py:57
  31.0 6.3 %collective-permute-start.15 = (f32[8,2048]{1,0:T(8,128)S(1)}, f32[8,2048]{1,0:T(8,128)S(1)}, u32[]{:S(2)}, u32[]{:S(2)}) collective-permute-start(f32[8,2048]{1,0:T(8,128)S(1)} %get-tuple-element.38), channel_id=1, source_target_pairs={{0,24},{2,26},{4,28},{6,30},{8,16},{10,18},{12,20},{14,22},{16,8},... | collective-permute-start | bytes 196616 | tf_op jit(solution)/shard_map/ppermute | solution.py:57
  31.6 4.0 %collective-permute-start.12 = (f32[8,1152]{1,0:T(8,128)S(1)}, f32[8,1152]{1,0:T(8,128)S(1)}, u32[]{:S(2)}, u32[]{:S(2)}) collective-permute-start(f32[8,1152]{1,0:T(8,128)S(1)} %add.27.refs_6_), channel_id=1, source_target_pairs={{0,4},{2,6},{4,0},{6,2},{8,12},{10,14},{12,8},{14,10},{16,20},{18,... | collective-permute-start | bytes 110600 | tf_op jit(solution)/shard_map/ppermute | solution.py:57
  32.8 2.8 %copy-start.2 = (f32[128,128]{1,0:T(8,128)S(1)}, f32[128,128]{1,0:T(8,128)}, u32[]{:S(2)}) copy-start(f32[128,128]{1,0:T(8,128)} %refs_2_.1) | copy-start | bytes 196612
  32.8 2.8 %copy-start.3 = (f32[8,2048]{1,0:T(8,128)S(1)}, f32[8,2048]{1,0:T(8,128)}, u32[]{:S(2)}) copy-start(f32[8,2048]{1,0:T(8,128)} %refs_3_.1) | copy-start | bytes 196612

commit v4 on v3

--- a/solution.py
+++ b/solution.py
@@ -158,23 +158,28 @@
     return jnp.concatenate([upper, jnp.concatenate([folded[:m, :m], corner], axis=1)], axis=0)
 
 
+def place_parts(grid, refs, out_ref):
+    for d, ref in enumerate(refs):
+        start = (lax.axis_index("col") ^ d) * grid.width
+        out_ref[pl.ds(pl.multiple_of(start, grid.width), grid.width), :] = ref[...]
+
+
 def cbar_kernel(grid, inverse_t_ref, *refs):
-    cols = grid.cols
-    cbar_refs, c_refs = refs[:cols], refs[cols:2 * cols]
-    out_ref, product_ref, perm_ref, stack_ref, cbar, c, new = refs[2 * cols:]
+    parts, (new_ref, out_ref, perm_ref, stack_ref, cbar) = refs[:grid.cols], refs[grid.cols:]
     me, my_col = lax.axis_index("row"), lax.axis_index("col")
     n = inverse_t_ref.shape[0]
-    for d in range(cols):
-        at = pl.ds(pl.multiple_of((my_col ^ d) * grid.width, grid.width), grid.width)
-        cbar[at, :] = cbar_refs[d][...]
-        c[at, :] = c_refs[d][...]
-    absolute = dot6(inverse_t_ref[...], cbar[...])
-    new[...] = absolute
-    perm = grid.permute_rows(new, me)
+    place_parts(grid, parts, cbar)
+    new_ref[...] = dot6(inverse_t_ref[...], cbar[...])
+    perm = grid.permute_rows(new_ref, me)
     perm_ref[...] = perm
     stack_ref[:n, :], stack_ref[n:, :] = split(perm)
-    out_ref[...] = new[pl.ds(pl.multiple_of(my_col * grid.width, grid.width), grid.width), :]
-    product_ref[...] = fold(dot(absolute, c[...], ((1,), (1,))))
+    out_ref[...] = new_ref[pl.ds(pl.multiple_of(my_col * grid.width, grid.width), grid.width), :]
+
+
+def product_kernel(grid, new_ref, *refs):
+    parts, (product_ref, c) = refs[:grid.cols], refs[grid.cols:]
+    place_parts(grid, parts, c)
+    product_ref[...] = fold(dot(new_ref[...], c[...], ((1,), (1,))))
 
 
 def trailing_kernel(stack_ref, high_ref, low_ref, keep_ref, send_ref):
@@ -280,24 +285,24 @@
             prepare_kernel,
             (full((n, n)), full((depth, breadth), BF16), full((depth, breadth), BF16)),
             [pltpu.VMEM((depth, breadth), F32), pltpu.SemaphoreType.DMA((8,))],
-            limit=48 * MIB, flops=4000000000,
+            limit=48 * MIB, flops=4 * 10 ** 9,
             specs=[pl.BlockSpec(memory_space=pltpu.VMEM)] * 2 + [pl.BlockSpec(memory_space=pltpu.HBM)],
         )(factor, identity, b_block)
-        cbar_out_t, product, cbar_perm, stack = call(
+        cbar_new_t, cbar_out_t, cbar_perm, stack = call(
             lambda *refs: cbar_kernel(grid, *refs),
-            (full((width, depth)), full((8, (n // 16 + 1) * n)), full((n, depth)), full((2 * n, depth), BF16)),
-            [pltpu.VMEM((n, depth), F32)] * 3, flops=1000000000,
-        )(inverse_t, *cbar_parts, *c_parts)
-
-        keep, send = call(trailing_kernel, (full((n // 2, breadth)),) * 2, flops=1000000000)(stack, high, low)
+            (full((n, depth)), full((width, depth)), full((n, depth)), full((2 * n, depth), BF16)),
+            [pltpu.VMEM((n, depth), F32)], flops=10 ** 9,
+        )(inverse_t, *cbar_parts)
+        keep, send = call(trailing_kernel, (full((n // 2, breadth)),) * 2, flops=10 ** 9)(stack, high, low)
+        product = call(
+            lambda *refs: product_kernel(grid, *refs), full((8, (n // 16 + 1) * n)), [pltpu.VMEM((n, depth), F32)],
+        )(after(cbar_new_t, send), *c_parts)
+        product = add_pairs(row_parts(product, grid.core))
         summed = after(keep, panel) + swap(send, "row", rows, grid.core[1])
-        product = add_pairs(row_parts(product, grid.core))
         product, summed = lax.optimization_barrier((product, summed))
-        product = add_pairs(row_parts(product, grid.z_near))
-        product, panel = lax.optimization_barrier((product, panel))
+        panel = after(panel, summed)
+        product_parts = row_parts(product, grid.z_near)
         panel_parts = row_parts(panel, grid.core)
-        product = add_pairs(row_parts(product, grid.z_far))
-
         bbar_out = pl.pallas_call(
             bbar_kernel,
             in_specs=[pl.BlockSpec(memory_space=pltpu.VMEM)] * (2 + len(panel_parts)),
@@ -309,11 +314,14 @@
             compiler_params=pltpu.CompilerParams(vmem_limit_bytes=16 * MIB),
             cost_estimate=pl.CostEstimate(flops=0, bytes_accessed=1, transcendentals=0),
         )(cbar_perm, bbar_in, *panel_parts)
+        product = add_pairs(product_parts)
+        product_parts = row_parts(product, grid.z_far)
         for count, stride in grid.order[1:]:
             own, *sends = summed.reshape(count, -1, breadth)
-            summed = add_pairs([own] + [swap(value, "row", rows, d * stride) for d, value in enumerate(sends, 1)])
+            got = [swap(value, "row", rows, d * stride) for d, value in enumerate(sends, 1)]
+            summed = add_pairs([own] + got)
             if stride == grid.x[1]:
-                product = after(product, summed)
+                product = add_pairs([after(product_parts[0], summed)] + product_parts[1:])
         kernel_out, rbar = call(
             lambda *refs: diagonal_kernel(grid, *refs), (full((height, width)), full((height, breadth))), flops=0
         )(factor, inverse_t, dbar_in, rbar_in, *panel_parts, *row_parts(product, grid.x))

time: 38 us -> 38.2 us (level)
  Pallas kernels: 9.42 us -> 9.87 us
  starting transfers between devices: 20.2 us -> 19.8 us
    pallas_call x2 -> x3, Pallas kernels: 2.12 us -> 2.6 us  [the longest x1 1.01 us: body(): call(lambda *refs: cbar_kernel(grid, *refs), (full((n, depth)), full((wid...]
    ppermute x16, starting transfers between devices: 20.2 us -> 19.8 us  [swap(): return lax.ppermute(value, axis, [(i, i ^ offset) for i in range(size)])]
  transfers between devices with their start and end apart: 16 -> 16, of which waited for: 5 -> 5; matrix products, arithmetic and copies ran while one was open for 0% -> 0% of each run, Pallas kernels for 25% -> 26%
where the time goes in v4:
time: 38.2 us; the launch traced here: 38 us
  starting transfers between devices  19.8 us (52%)
  Pallas kernels  9.87 us (26%)
  waiting for transfers between devices  6.11 us (16%)
  between operations  0.81 us (2%)
  other arithmetic  0.79 us (2%)
  local copies, waits for them, and re-layouts  0.64 us (2%)
    ppermute x16, starting transfers between devices, swap(): return lax.ppermute(value, axis, [(i, i ^ offset) for i in range(size)])  19.8 us
    ppermute x16, waiting for transfers between devices, swap(): return lax.ppermute(value, axis, [(i, i ^ offset) for i in range(size)])  6.11 us
    pallas_call x1, Pallas kernels, body(): call(prepare_kernel, (full((n, n)), full((depth, breadth), BF16), full((d...  3.1 us
    pallas_call x1, Pallas kernels, body(): pl.pallas_call(bbar_kernel, in_specs=[pl.BlockSpec(memory_space=pltpu.VME...  2.58 us
    pallas_call x1, Pallas kernels, body(): call(lambda *refs: diagonal_kernel(grid, *refs), (full((height, width)),...  1.58 us
    pallas_call x1, Pallas kernels, body(): call(lambda *refs: cbar_kernel(grid, *refs), (full((n, depth)), full((wid...  1.01 us
    pallas_call x1, Pallas kernels, body(): call(trailing_kernel, (full((n // 2, breadth)),) * 2, flops=10 ** 9)  0.97 us
  transfers between devices with their start and end apart: 16, of which 5 were waited for; matrix products, arithmetic and copies ran while one was open for 0% of the time, Pallas kernels for 26%

profile of v4, /device:TPU:0, one launch (start us, length us, event | category | flops | bytes accessed | tf_op | source)
XLA Modules:
  0.0 38.0 jit_solution(5952123023360331759)
XLA Ops:
  0.6 3.1 %collective-permute-start.1 = (f32[8,2048]{1,0:T(8,128)}, f32[8,2048]{1,0:T(8,128)S(1)}, u32[]{:S(2)}, u32[]{:S(2)}) collective-permute-start(f32[8,2048]{1,0:T(8,128)} %param.12), channel_id=1, source_target_pairs={{0,8},{2,10},{4,12},{6,14},{8,0},{10,2},{12,4},{14,6},{16,24},{18,... | collective-permute-start | bytes 196616 | tf_op jit(solution)/shard_map/ppermute | solution.py:57
  3.7 2.6 %collective-permute-start.2 = (f32[8,2048]{1,0:T(8,128)}, f32[8,2048]{1,0:T(8,128)S(1)}, u32[]{:S(2)}, u32[]{:S(2)}) collective-permute-start(f32[8,2048]{1,0:T(8,128)} %param.12), channel_id=1, source_target_pairs={{0,16},{2,18},{4,20},{6,22},{8,24},{10,26},{12,28},{14,30},{16,0},... | collective-permute-start | bytes 196616 | tf_op jit(solution)/shard_map/ppermute | solution.py:57
  6.3 0.0 collective-permute-start.3
  6.3 1.7 %collective-permute-start = (f32[64,512]{1,0:T(8,128)}, f32[64,512]{1,0:T(8,128)S(1)}, u32[]{:S(2)}, u32[]{:S(2)}) collective-permute-start(f32[64,512]{1,0:T(8,128)} %bitcast.5), channel_id=1, source_target_pairs={{0,1},{1,0},{2,3},{3,2},{4,5},{5,4},{6,7},{7,6},{8,9},{9,8},{10,11... | collective-permute-start | bytes 393224 | tf_op jit(solution)/shard_map/ppermute | solution.py:57
  8.1 0.0 copy-start.2
  8.1 0.3 collective-permute-start.5
  8.4 0.5 %copy-done.2 = f32[128,128]{1,0:T(8,128)S(1)} copy-done((f32[128,128]{1,0:T(8,128)S(1)}, f32[128,128]{1,0:T(8,128)}, u32[]{:S(2)}) %copy-start.2) | copy-done | bytes 65560
  8.9 0.0 copy-start.6
  8.9 0.0 copy-start.5
  8.9 3.1 %shard_map.112 = (f32[128,128]{1,0:T(8,128)S(1)}, bf16[512,2048]{1,0:T(8,128)(2,1)S(1)}, bf16[512,2048]{1,0:T(8,128)(2,1)S(1)}) custom-call(f32[128,128]{1,0:T(8,128)S(1)} %copy-done.2, f32[128,128]{1,0:T(8,128)S(1)} %shard_map.111.identity_ref, f32[512,2048]{1,0:T(8,128)} %b_hbm.1), custom_call_target="tpu_custom_call" | custom-call | flops 4000000000 | bytes 1 | tf_op jit(solution)/shard_map/pallas_call | solution.py:284
  12.0 0.0 copy-done.6
  12.0 0.0 collective-permute-done.1
  12.0 0.0 collective-permute-done.2
  12.0 0.6 %collective-permute-done.3 = f32[8,2048]{1,0:T(8,128)S(1)} collective-permute-done((f32[8,2048]{1,0:T(8,128)}, f32[8,2048]{1,0:T(8,128)S(1)}, u32[]{:S(2)}, u32[]{:S(2)}) %collective-permute-start.3) | collective-permute-done | bytes 65568 | tf_op jit(solution)/shard_map/ppermute | solution.py:57
  12.6 0.0 copy-start.1
  12.6 1.6 %collective-permute-start.4 = (f32[32,2048]{1,0:T(8,128)S(1)}, f32[32,2048]{1,0:T(8,128)S(1)}, u32[]{:S(2)}, u32[]{:S(2)}) collective-permute-start(f32[32,2048]{1,0:T(8,128)S(1)} %pad_maximum_fusion), channel_id=1, source_target_pairs={{0,4},{2,6},{4,0},{6,2},{8,12},{10,14},{12,8},{14,10},{16,20},{18,... | collective-permute-start | bytes 786440 | tf_op jit(solution)/shard_map/ppermute | solution.py:57
  14.2 0.0 collective-permute-done.refs_2_
  14.2 0.0 copy-done.5
  14.2 1.0 %shard_map.113 = (f32[128,512]{1,0:T(8,128)S(1)}, f32[64,512]{1,0:T(8,128)}, f32[128,512]{1,0:T(8,128)S(1)}, bf16[256,512]{1,0:T(8,128)(2,1)S(1)}) custom-call(f32[128,128]{1,0:T(8,128)S(1)} %get-tuple-element.21.refs_0_.refs_1_, f32[64,512]{1,0:T(8,128)S(1)} %bitcast.6, f32[64,512]{1,0:T(8,128)S(1)} %collective-permute-done.refs_2_), custom_call_target="tpu_custom_call" | custom-call | flops 1000000000 | bytes 1 | tf_op jit(solution)/shard_map/pallas_call | solution.py:291
  15.2 0.0 copy-start
  15.2 1.0 %shard_map.114 = (f32[64,2048]{1,0:T(8,128)S(1)}, f32[64,2048]{1,0:T(8,128)S(1)}) custom-call(bf16[256,512]{1,0:T(8,128)(2,1)S(1)} %get-tuple-element.25.stack_ref, bf16[512,2048]{1,0:T(8,128)(2,1)S(1)} %get-tuple-element.26.high_ref, bf16[512,2048]{1,0:T(8,128)(2,1)S(1)} %get-tuple-element.27.low_ref), custom_call_target="tpu_custom_call" | custom-call | flops 1000000000 | bytes 1 | tf_op jit(solution)/shard_map/pallas_call | solution.py:296
  16.2 0.1 collective-permute-start.7
  16.3 0.0 collective-permute-done.5.refs_2_
  16.3 0.0 copy-done.1
  16.3 0.6 %shard_map.115 = f32[8,1152]{1,0:T(8,128)S(1)} custom-call(f32[128,512]{1,0:T(8,128)S(1)} %get-tuple-element.29.refs_0_, f32[64,512]{1,0:T(8,128)S(1)} %bitcast.4, f32[64,512]{1,0:T(8,128)S(1)} %collective-permute-done.5.refs_2_), custom_call_target="tpu_custom_call" | custom-call | bytes 1 | tf_op jit(solution)/shard_map/pallas_call | solution.py:297
  17.0 0.5 %collective-permute-start.6 = (f32[8,1152]{1,0:T(8,128)S(1)}, f32[8,1152]{1,0:T(8,128)S(1)}, u32[]{:S(2)}, u32[]{:S(2)}) collective-permute-start(f32[8,1152]{1,0:T(8,128)S(1)} %shard_map.115), channel_id=1, source_target_pairs={{0,2},{2,0},{4,6},{6,4},{8,10},{10,8},{12,14},{14,12},{16,18},{18,... | collective-permute-start | bytes 110600 | tf_op jit(solution)/shard_map/ppermute | solution.py:57
  17.5 0.9 %collective-permute-done.6 = f32[8,1152]{1,0:T(8,128)S(1)} collective-permute-done((f32[8,1152]{1,0:T(8,128)S(1)}, f32[8,1152]{1,0:T(8,128)S(1)}, u32[]{:S(2)}, u32[]{:S(2)}) %collective-permute-start.6) | collective-permute-done | bytes 36896 | tf_op jit(solution)/shard_map/ppermute | solution.py:57
  18.4 0.8 %collective-permute-done.4 = f32[32,2048]{1,0:T(8,128)S(1)} collective-permute-done((f32[32,2048]{1,0:T(8,128)S(1)}, f32[32,2048]{1,0:T(8,128)S(1)}, u32[]{:S(2)}, u32[]{:S(2)}) %collective-permute-start.4) | collective-permute-done | bytes 262176 | tf_op jit(solution)/shard_map/ppermute | solution.py:57
  19.2 0.0 collective-permute-done.7
  19.2 0.1 add.25
  19.3 1.6 %collective-permute-start.10 = (f32[32,2048]{1,0:T(8,128)S(1)}, f32[32,2048]{1,0:T(8,128)S(1)}, u32[]{:S(2)}, u32[]{:S(2)}) collective-permute-start(f32[32,2048]{1,0:T(8,128)S(1)} %unstack.25), channel_id=1, source_target_pairs={{0,4},{2,6},{4,0},{6,2},{8,12},{10,14},{12,8},{14,10},{16,20},{18,... | collective-permute-start | bytes 786440 | tf_op jit(solution)/shard_map/ppermute | solution.py:57
  20.8 1.0 %collective-permute-start.9 = (f32[8,1152]{1,0:T(8,128)S(1)}, f32[8,1152]{1,0:T(8,128)S(1)}, u32[]{:S(2)}, u32[]{:S(2)}) collective-permute-start(f32[8,1152]{1,0:T(8,128)S(1)} %add.24), channel_id=1, source_target_pairs={{0,8},{2,10},{4,12},{6,14},{8,0},{10,2},{12,4},{14,6},{16,24},{18,... | collective-permute-start | bytes 110600 | tf_op jit(solution)/shard_map/ppermute | solution.py:57
  21.8 0.0 collective-permute-start.8
  21.8 3.0 %collective-permute-done.9 = f32[8,1152]{1,0:T(8,128)S(1)} collective-permute-done((f32[8,1152]{1,0:T(8,128)S(1)}, f32[8,1152]{1,0:T(8,128)S(1)}, u32[]{:S(2)}, u32[]{:S(2)}) %collective-permute-start.9) | collective-permute-done | bytes 36896 | tf_op jit(solution)/shard_map/ppermute | solution.py:57
  24.8 2.4 %collective-permute-start.11 = (f32[8,1152]{1,0:T(8,128)S(1)}, f32[8,1152]{1,0:T(8,128)S(1)}, u32[]{:S(2)}, u32[]{:S(2)}) collective-permute-start(f32[8,1152]{1,0:T(8,128)S(1)} %add.26), channel_id=1, source_target_pairs={{0,16},{2,18},{4,20},{6,22},{8,24},{10,26},{12,28},{14,30},{16,0},... | collective-permute-start | bytes 110600 | tf_op jit(solution)/shard_map/ppermute | solution.py:57
  27.2 0.0 collective-permute-done.10
  27.3 1.8 %collective-permute-start.13 = (f32[8,2048]{1,0:T(8,128)S(1)}, f32[8,2048]{1,0:T(8,128)S(1)}, u32[]{:S(2)}, u32[]{:S(2)}) collective-permute-start(f32[8,2048]{1,0:T(8,128)S(1)} %get-tuple-element.40), channel_id=1, source_target_pairs={{0,8},{2,10},{4,12},{6,14},{8,0},{10,2},{12,4},{14,6},{16,24},{18,... | collective-permute-start | bytes 196616 | tf_op jit(solution)/shard_map/ppermute | solution.py:57
  29.0 1.8 %collective-permute-start.14 = (f32[8,2048]{1,0:T(8,128)S(1)}, f32[8,2048]{1,0:T(8,128)S(1)}, u32[]{:S(2)}, u32[]{:S(2)}) collective-permute-start(f32[8,2048]{1,0:T(8,128)S(1)} %get-tuple-element.39), channel_id=1, source_target_pairs={{0,16},{2,18},{4,20},{6,22},{8,24},{10,26},{12,28},{14,30},{16,0},... | collective-permute-start | bytes 196616 | tf_op jit(solution)/shard_map/ppermute | solution.py:57
  30.9 0.8 %collective-permute-start.15 = (f32[8,2048]{1,0:T(8,128)S(1)}, f32[8,2048]{1,0:T(8,128)S(1)}, u32[]{:S(2)}, u32[]{:S(2)}) collective-permute-start(f32[8,2048]{1,0:T(8,128)S(1)} %get-tuple-element.38), channel_id=1, source_target_pairs={{0,24},{2,26},{4,28},{6,30},{8,16},{10,18},{12,20},{14,22},{16,8},... | collective-permute-start | bytes 196616 | tf_op jit(solution)/shard_map/ppermute | solution.py:57
  31.7 0.0 collective-permute-done.11
  31.7 0.5 %collective-permute-start.12 = (f32[8,1152]{1,0:T(8,128)S(1)}, f32[8,1152]{1,0:T(8,128)S(1)}, u32[]{:S(2)}, u32[]{:S(2)}) collective-permute-start(f32[8,1152]{1,0:T(8,128)S(1)} %add.28.refs_6_), channel_id=1, source_target_pairs={{0,4},{2,6},{4,0},{6,2},{8,12},{10,14},{12,8},{14,10},{16,20},{18,... | collective-permute-start | bytes 110600 | tf_op jit(solution)/shard_map/ppermute | solution.py:57
  32.3 0.0 collective-permute-done.8.refs_1_.refs_5_
  32.3 0.0 copy-done
  32.3 0.0 copy-start.3
  32.3 0.0 copy-start.4
  32.3 2.6 %shard_map.116 = f32[512,2048]{1,0:T(8,128)} custom-call(f32[128,512]{1,0:T(8,128)S(1)} %get-tuple-element.23.perm_ref, f32[512,2048]{1,0:T(8,128)S(1)} %copy-done, f32[64,2048]{1,0:T(8,128)S(1)} %constant_dynamic-update-slice_fusion.refs_0_.refs_4_, f32[64,2048]{1,0:T(8,128)S(1)} %collective-permute-done.8.refs_1_.refs_5_), custom_call_target="tpu_custom_call" | custom-call | bytes 1 | tf_op jit(solution)/shard_map/pallas_call | solution.py:306
  34.9 0.9 %collective-permute-done.12.refs_7_ = f32[8,1152]{1,0:T(8,128)S(1)} collective-permute-done((f32[8,1152]{1,0:T(8,128)S(1)}, f32[8,1152]{1,0:T(8,128)S(1)}, u32[]{:S(2)}, u32[]{:S(2)}) %collective-permute-start.12) | collective-permute-done | bytes 36896 | tf_op jit(solution)/shard_map/ppermute | solution.py:57
  35.8 0.0 copy-done.3
  35.8 0.0 copy-done.4
  35.8 1.6 %shard_map.117 = (f32[8,64]{1,0:T(8,128)}, f32[8,2048]{1,0:T(8,128)S(1)}) custom-call(f32[128,128]{1,0:T(8,128)S(1)} %copy-done.2, f32[128,128]{1,0:T(8,128)S(1)} %get-tuple-element.21.refs_0_.refs_1_, f32[128,128]{1,0:T(8,128)S(1)} %copy-done.3, f32[8,2048]{1,0:T(8,128)S(1)} %copy-done.4, f32[64,2048]{1,0:T(8,128)S(1)} %constant_dynamic-update-slice_fusion.refs_0_.refs_4_, ...), custom_call_target="tpu_custom_call" | custom-call | bytes 1 | tf_op jit(solution)/shard_map/pallas_call | solution.py:325
  37.4 0.0 collective-permute-done.13
  37.4 0.0 collective-permute-done.14
  37.4 0.0 collective-permute-done.15
  37.4 0.7 %fusion.1 = f32[8,2048]{1,0:T(8,128)} fusion(f32[8,2048]{1,0:T(8,128)S(1)} %get-tuple-element.37, f32[8,2048]{1,0:T(8,128)S(1)} %collective-permute-done.13, f32[32,2048]{1,0:T(8,128)S(1)} %slice_add_fusion, f32[8,2048]{1,0:T(8,128)S(1)} %collective-permute-done.14, f32[8,2048]{1,0:T(8,128)S(1)} %collective-permute-done.15), kind=kLoop, calls=%fused_computation.4 | loop fusion | flops 65536 | bytes 393216 | tf_op jit(solution)/shard_map/sub | solution.py:328
  (13 shorter events, 0.2 us)
Async XLA Ops:
  0.6 11.4 %collective-permute-start.1 = (f32[8,2048]{1,0:T(8,128)}, f32[8,2048]{1,0:T(8,128)S(1)}, u32[]{:S(2)}, u32[]{:S(2)}) collective-permute-start(f32[8,2048]{1,0:T(8,128)} %param.12), channel_id=1, source_target_pairs={{0,8},{2,10},{4,12},{6,14},{8,0},{10,2},{12,4},{14,6},{16,24},{18,... | collective-permute-start | bytes 196616 | tf_op jit(solution)/shard_map/ppermute | solution.py:57
  3.7 8.3 %collective-permute-start.2 = (f32[8,2048]{1,0:T(8,128)}, f32[8,2048]{1,0:T(8,128)S(1)}, u32[]{:S(2)}, u32[]{:S(2)}) collective-permute-start(f32[8,2048]{1,0:T(8,128)} %param.12), channel_id=1, source_target_pairs={{0,16},{2,18},{4,20},{6,22},{8,24},{10,26},{12,28},{14,30},{16,0},... | collective-permute-start | bytes 196616 | tf_op jit(solution)/shard_map/ppermute | solution.py:57
  6.3 6.3 %collective-permute-start.3 = (f32[8,2048]{1,0:T(8,128)}, f32[8,2048]{1,0:T(8,128)S(1)}, u32[]{:S(2)}, u32[]{:S(2)}) collective-permute-start(f32[8,2048]{1,0:T(8,128)} %param.12), channel_id=1, source_target_pairs={{0,24},{2,26},{4,28},{6,30},{8,16},{10,18},{12,20},{14,22},{16,8},... | collective-permute-start | bytes 196616 | tf_op jit(solution)/shard_map/ppermute | solution.py:57
  6.3 7.9 %collective-permute-start = (f32[64,512]{1,0:T(8,128)}, f32[64,512]{1,0:T(8,128)S(1)}, u32[]{:S(2)}, u32[]{:S(2)}) collective-permute-start(f32[64,512]{1,0:T(8,128)} %bitcast.5), channel_id=1, source_target_pairs={{0,1},{1,0},{2,3},{3,2},{4,5},{5,4},{6,7},{7,6},{8,9},{9,8},{10,11... | collective-permute-start | bytes 393224 | tf_op jit(solution)/shard_map/ppermute | solution.py:57
  8.1 0.8 %copy-start.2 = (f32[128,128]{1,0:T(8,128)S(1)}, f32[128,128]{1,0:T(8,128)}, u32[]{:S(2)}) copy-start(f32[128,128]{1,0:T(8,128)} %refs_0_.1) | copy-start | bytes 196612
  8.1 8.3 %collective-permute-start.5 = (f32[64,512]{1,0:T(8,128)}, f32[64,512]{1,0:T(8,128)S(1)}, u32[]{:S(2)}, u32[]{:S(2)}) collective-permute-start(f32[64,512]{1,0:T(8,128)} %bitcast.3), channel_id=1, source_target_pairs={{0,1},{1,0},{2,3},{3,2},{4,5},{5,4},{6,7},{7,6},{8,9},{9,8},{10,11... | collective-permute-start | bytes 393224 | tf_op jit(solution)/shard_map/ppermute | solution.py:57
  8.9 3.1 %copy-start.6 = (f32[8,2048]{1,0:T(8,128)S(1)}, f32[8,2048]{1,0:T(8,128)}, u32[]{:S(2)}) copy-start(f32[8,2048]{1,0:T(8,128)} %param.12) | copy-start | bytes 196612
  8.9 5.3 %copy-start.5 = (f32[512,64]{0,1:T(8,128)S(1)}, f32[512,64]{0,1:T(8,128)}, u32[]{:S(2)}) copy-start(f32[512,64]{0,1:T(8,128)} %param.9) | copy-start | bytes 393220
  12.6 3.7 %copy-start.1 = (f32[512,64]{0,1:T(8,128)S(1)}, f32[512,64]{0,1:T(8,128)}, u32[]{:S(2)}) copy-start(f32[512,64]{0,1:T(8,128)} %param.8) | copy-start | bytes 393220
  12.6 6.5 %collective-permute-start.4 = (f32[32,2048]{1,0:T(8,128)S(1)}, f32[32,2048]{1,0:T(8,128)S(1)}, u32[]{:S(2)}, u32[]{:S(2)}) collective-permute-start(f32[32,2048]{1,0:T(8,128)S(1)} %pad_maximum_fusion), channel_id=1, source_target_pairs={{0,4},{2,6},{4,0},{6,2},{8,12},{10,14},{12,8},{14,10},{16,20},{18,... | collective-permute-start | bytes 786440 | tf_op jit(solution)/shard_map/ppermute | solution.py:57
  15.2 17.0 %copy-start = (f32[512,2048]{1,0:T(8,128)S(1)}, f32[512,2048]{1,0:T(8,128)}, u32[]{:S(2)}) copy-start(f32[512,2048]{1,0:T(8,128)} %bbar_ref.1) | copy-start | bytes 12582916
  16.2 3.0 %collective-permute-start.7 = (f32[64,2048]{1,0:T(8,128)S(1)}, f32[64,2048]{1,0:T(8,128)S(1)}, u32[]{:S(2)}, u32[]{:S(2)}) collective-permute-start(f32[64,2048]{1,0:T(8,128)S(1)} %get-tuple-element.28), channel_id=1, source_target_pairs={{0,2},{2,0},{4,6},{6,4},{8,10},{10,8},{12,14},{14,12},{16,18},{18,... | collective-permute-start | bytes 1572872 | tf_op jit(solution)/shard_map/ppermute | solution.py:57
  17.0 1.4 %collective-permute-start.6 = (f32[8,1152]{1,0:T(8,128)S(1)}, f32[8,1152]{1,0:T(8,128)S(1)}, u32[]{:S(2)}, u32[]{:S(2)}) collective-permute-start(f32[8,1152]{1,0:T(8,128)S(1)} %shard_map.115), channel_id=1, source_target_pairs={{0,2},{2,0},{4,6},{6,4},{8,10},{10,8},{12,14},{14,12},{16,18},{18,... | collective-permute-start | bytes 110600 | tf_op jit(solution)/shard_map/ppermute | solution.py:57
  19.3 7.9 %collective-permute-start.10 = (f32[32,2048]{1,0:T(8,128)S(1)}, f32[32,2048]{1,0:T(8,128)S(1)}, u32[]{:S(2)}, u32[]{:S(2)}) collective-permute-start(f32[32,2048]{1,0:T(8,128)S(1)} %unstack.25), channel_id=1, source_target_pairs={{0,4},{2,6},{4,0},{6,2},{8,12},{10,14},{12,8},{14,10},{16,20},{18,... | collective-permute-start | bytes 786440 | tf_op jit(solution)/shard_map/ppermute | solution.py:57
  20.8 4.0 %collective-permute-start.9 = (f32[8,1152]{1,0:T(8,128)S(1)}, f32[8,1152]{1,0:T(8,128)S(1)}, u32[]{:S(2)}, u32[]{:S(2)}) collective-permute-start(f32[8,1152]{1,0:T(8,128)S(1)} %add.24), channel_id=1, source_target_pairs={{0,8},{2,10},{4,12},{6,14},{8,0},{10,2},{12,4},{14,6},{16,24},{18,... | collective-permute-start | bytes 110600 | tf_op jit(solution)/shard_map/ppermute | solution.py:57
  21.8 10.5 %collective-permute-start.8 = (f32[64,2048]{1,0:T(8,128)S(1)}, f32[64,2048]{1,0:T(8,128)S(1)}, u32[]{:S(2)}, u32[]{:S(2)}) collective-permute-start(f32[64,2048]{1,0:T(8,128)S(1)} %constant_dynamic-update-slice_fusion.refs_0_.refs_4_), channel_id=1, source_target_pairs={{0,2},{2,0},{4,6},{6,4},{8,10},{10,8},{12,14},{14,12},{16,18},{18,... | collective-permute-start | bytes 1572872 | tf_op jit(solution)/shard_map/ppermute | solution.py:57
  24.8 6.9 %collective-permute-start.11 = (f32[8,1152]{1,0:T(8,128)S(1)}, f32[8,1152]{1,0:T(8,128)S(1)}, u32[]{:S(2)}, u32[]{:S(2)}) collective-permute-start(f32[8,1152]{1,0:T(8,128)S(1)} %add.26), channel_id=1, source_target_pairs={{0,16},{2,18},{4,20},{6,22},{8,24},{10,26},{12,28},{14,30},{16,0},... | collective-permute-start | bytes 110600 | tf_op jit(solution)/shard_map/ppermute | solution.py:57
  27.3 10.1 %collective-permute-start.13 = (f32[8,2048]{1,0:T(8,128)S(1)}, f32[8,2048]{1,0:T(8,128)S(1)}, u32[]{:S(2)}, u32[]{:S(2)}) collective-permute-start(f32[8,2048]{1,0:T(8,128)S(1)} %get-tuple-element.40), channel_id=1, source_target_pairs={{0,8},{2,10},{4,12},{6,14},{8,0},{10,2},{12,4},{14,6},{16,24},{18,... | collective-permute-start | bytes 196616 | tf_op jit(solution)/shard_map/ppermute | solution.py:57
  29.0 8.3 %collective-permute-start.14 = (f32[8,2048]{1,0:T(8,128)S(1)}, f32[8,2048]{1,0:T(8,128)S(1)}, u32[]{:S(2)}, u32[]{:S(2)}) collective-permute-start(f32[8,2048]{1,0:T(8,128)S(1)} %get-tuple-element.39), channel_id=1, source_target_pairs={{0,16},{2,18},{4,20},{6,22},{8,24},{10,26},{12,28},{14,30},{16,0},... | collective-permute-start | bytes 196616 | tf_op jit(solution)/shard_map/ppermute | solution.py:57
  30.9 6.5 %collective-permute-start.15 = (f32[8,2048]{1,0:T(8,128)S(1)}, f32[8,2048]{1,0:T(8,128)S(1)}, u32[]{:S(2)}, u32[]{:S(2)}) collective-permute-start(f32[8,2048]{1,0:T(8,128)S(1)} %get-tuple-element.38), channel_id=1, source_target_pairs={{0,24},{2,26},{4,28},{6,30},{8,16},{10,18},{12,20},{14,22},{16,8},... | collective-permute-start | bytes 196616 | tf_op jit(solution)/shard_map/ppermute | solution.py:57
  31.7 4.0 %collective-permute-start.12 = (f32[8,1152]{1,0:T(8,128)S(1)}, f32[8,1152]{1,0:T(8,128)S(1)}, u32[]{:S(2)}, u32[]{:S(2)}) collective-permute-start(f32[8,1152]{1,0:T(8,128)S(1)} %add.28.refs_6_), channel_id=1, source_target_pairs={{0,4},{2,6},{4,0},{6,2},{8,12},{10,14},{12,8},{14,10},{16,20},{18,... | collective-permute-start | bytes 110600 | tf_op jit(solution)/shard_map/ppermute | solution.py:57
  32.3 3.5 %copy-start.3 = (f32[128,128]{1,0:T(8,128)S(1)}, f32[128,128]{1,0:T(8,128)}, u32[]{:S(2)}) copy-start(f32[128,128]{1,0:T(8,128)} %refs_2_.1) | copy-start | bytes 196612
  32.3 3.5 %copy-start.4 = (f32[8,2048]{1,0:T(8,128)S(1)}, f32[8,2048]{1,0:T(8,128)}, u32[]{:S(2)}) copy-start(f32[8,2048]{1,0:T(8,128)} %refs_3_.1) | copy-start | bytes 196612

commit v5 on v4

--- a/solution.py
+++ b/solution.py
@@ -194,44 +194,47 @@
         send_ref[:, at] = total[n // 2:]
 
 
-def bbar_kernel(perm_ref, bbar_ref, *refs):
-    panel_refs, (out_hbm, out_ref, left_ref, sems) = refs[:-4], refs[-4:]
-    n = perm_ref.shape[0]
-    left_ref[:, :n], left_ref[:, n:] = split(perm_ref[...].T)
+def finish_kernel(grid, perm_ref, bbar_ref, factor_ref, inverse_t_ref, dbar_ref, rbar_ref, *refs):
+    cores = grid.core[0]
+    panel_refs, refs = refs[:cores], refs[cores:]
+    products, (bbar_hbm, out_ref, rbar_out_ref, bbar_out, left_ref, sems) = refs[:-6], refs[-6:]
+    me, my_col = lax.axis_index("row"), lax.axis_index("col")
+    n, height, width = factor_ref.shape[0], grid.height, grid.width
     count = sems.shape[0]
     tile = bbar_ref.shape[1] // count
-    copies = []
-    for k in range(count):
+    left_ref[:, :n], left_ref[:, n:] = split(perm_ref[...].T)
+    panels, copies = [], []
+
+    def bbar_tile(k):
         at = slice(k * tile, (k + 1) * tile)
         high, low = split(jnp.concatenate([ref[:, at] for ref in panel_refs], axis=0))
+        panels.append((high, low))
         update = dot(left_ref[...], jnp.concatenate([high, high], axis=0), precision=None)
-        out_ref[:, at] = bbar_ref[:, at] - (update + dot(left_ref[:, :n], low, precision=None))
-        copies.append(pltpu.make_async_copy(out_ref.at[:, pl.ds(k * tile, tile)], out_hbm.at[:, pl.ds(k * tile, tile)], sems.at[k]))
+        bbar_out[:, at] = bbar_ref[:, at] - (update + dot(left_ref[:, :n], low, precision=None))
+        copies.append(pltpu.make_async_copy(bbar_out.at[:, pl.ds(k * tile, tile)], bbar_hbm.at[:, pl.ds(k * tile, tile)], sems.at[k]))
         copies[-1].start()
-    for copy in copies:
-        copy.wait()
-
-
-def diagonal_kernel(grid, factor_ref, inverse_t_ref, dbar_ref, rbar_ref, *refs):
-    cores = grid.core[0]
-    panel_refs, products, (out_ref, rbar_out_ref) = refs[:cores], refs[cores:-2], refs[-2:]
-    me, my_col = lax.axis_index("row"), lax.axis_index("col")
-    n, height, width = factor_ref.shape[0], grid.height, grid.width
+
     product = unfold(add_pairs([ref[...] for ref in products]), n)
+    bbar_tile(0)
     proj = phi(dot6(factor_ref[...].T, dbar_ref[...] - product))
+    bbar_tile(1)
     if height % 8 == 0:
         weights = inverse_t_ref[pl.ds(pl.multiple_of(me * height, height), height), :]
     else:
         si, sj = iotas((height, n))
         weights = dot(hot(sj == me * height + si), inverse_t_ref[...])
     half = dot6(weights, proj + proj.T)
+    bbar_tile(2)
     both = jnp.concatenate([inverse_t_ref[...], grid.permute_rows(inverse_t_ref, me)], axis=0)
     rows = dot6(half, both.T)
+    for k in range(3, count):
+        bbar_tile(k)
     rows_sym = rows[:, :n]
     high, low = split(rows[:, n:])
-    panel_high, panel_low = split(jnp.concatenate([ref[...] for ref in panel_refs], axis=0))
-    update = dot(high, panel_high, precision=None) + dot(low, panel_high, precision=None) + dot(high, panel_low, precision=None)
-    rbar_out_ref[...] = rbar_ref[...] - update
+    for k, (panel_high, panel_low) in enumerate(panels):
+        at = slice(k * tile, (k + 1) * tile)
+        update = dot(high, panel_high, precision=None) + dot(low, panel_high, precision=None)
+        rbar_out_ref[:, at] = rbar_ref[:, at] - (update + dot(high, panel_low, precision=None))
     si, sj = iotas((height, n))
     own_row = me * height + si
     rows_kernel = jnp.where(sj < own_row, rows_sym, jnp.where(sj == own_row, 0.5 * rows_sym, 0.0))
@@ -239,6 +242,8 @@
     for k in range(1, grid.cols):
         out = jnp.where(my_col == k, rows_kernel[:, k * width:(k + 1) * width], out)
     out_ref[...] = out
+    for copy in copies:
+        copy.wait()
 
 
 def call(kernel, out_shape, scratch=(), limit=8 * MIB, flops=0, specs=None):
@@ -265,7 +270,7 @@
 def make_body(rows, cols):
     def row_parts(value, step):
         count, stride = step
-        return [value] + [swap(value, "row", rows, d * stride) for d in range(1, count)]
+        return [value] + [swap(value, "row", rows, d * stride) for d in range(count - 1, 0, -1)][::-1]
 
     def col_parts(value):
         return [value] + [swap(value, "col", cols, d) for d in range(1, cols)]
@@ -298,33 +303,34 @@
             lambda *refs: product_kernel(grid, *refs), full((8, (n // 16 + 1) * n)), [pltpu.VMEM((n, depth), F32)],
         )(after(cbar_new_t, send), *c_parts)
         product = add_pairs(row_parts(product, grid.core))
-        summed = after(keep, panel) + swap(send, "row", rows, grid.core[1])
+        summed = keep + swap(send, "row", rows, grid.core[1])
         product, summed = lax.optimization_barrier((product, summed))
         panel = after(panel, summed)
-        product_parts = row_parts(product, grid.z_near)
+        product = add_pairs(row_parts(product, grid.z_near))
+        product_parts = row_parts(product, grid.z_far)
         panel_parts = row_parts(panel, grid.core)
-        bbar_out = pl.pallas_call(
-            bbar_kernel,
-            in_specs=[pl.BlockSpec(memory_space=pltpu.VMEM)] * (2 + len(panel_parts)),
-            out_specs=pl.BlockSpec(memory_space=pltpu.HBM),
-            out_shape=full((depth, breadth)),
+        product = add_pairs(product_parts)
+        for count, stride in grid.order[1:]:
+            own, *sends = summed.reshape(count, -1, breadth)
+            got = [swap(value, "row", rows, d * stride) for d, value in list(enumerate(sends, 1))[::-1]][::-1]
+            if stride == grid.x[1]:
+                own = after(own, product)
+            summed = add_pairs([own] + got[::-1])
+            if stride == grid.x[1]:
+                dbar_in = after(dbar_in, summed)
+        vmem = pl.BlockSpec(memory_space=pltpu.VMEM)
+        product_parts = row_parts(product, grid.x)
+        bbar_out, kernel_out, rbar = pl.pallas_call(
+            lambda *refs: finish_kernel(grid, *refs),
+            in_specs=[vmem] * (6 + len(panel_parts) + len(product_parts)),
+            out_specs=[pl.BlockSpec(memory_space=pltpu.HBM), vmem, vmem],
+            out_shape=(full((depth, breadth)), full((height, width)), full((height, breadth))),
             scratch_shapes=[
                 pltpu.VMEM((depth, breadth), F32), pltpu.VMEM((depth, 2 * n), BF16), pltpu.SemaphoreType.DMA((breadth // 256,))
             ],
             compiler_params=pltpu.CompilerParams(vmem_limit_bytes=16 * MIB),
-            cost_estimate=pl.CostEstimate(flops=0, bytes_accessed=1, transcendentals=0),
-        )(cbar_perm, bbar_in, *panel_parts)
-        product = add_pairs(product_parts)
-        product_parts = row_parts(product, grid.z_far)
-        for count, stride in grid.order[1:]:
-            own, *sends = summed.reshape(count, -1, breadth)
-            got = [swap(value, "row", rows, d * stride) for d, value in enumerate(sends, 1)]
-            summed = add_pairs([own] + got)
-            if stride == grid.x[1]:
-                product = add_pairs([after(product_parts[0], summed)] + product_parts[1:])
-        kernel_out, rbar = call(
-            lambda *refs: diagonal_kernel(grid, *refs), (full((height, width)), full((height, breadth))), flops=0
-        )(factor, inverse_t, dbar_in, rbar_in, *panel_parts, *row_parts(product, grid.x))
+            cost_estimate=pl.CostEstimate(flops=10 ** 9, bytes_accessed=1, transcendentals=0),
+        )(cbar_perm, bbar_in, factor, inverse_t, dbar_in, rbar_in, *panel_parts, *product_parts)
         return (cbar_out_t.T, bbar_out, kernel_out, rbar - summed)
 
     return body

time: 38.2 us -> 37.5 us (0.982)
  waiting for transfers between devices: 6.11 us -> 8.61 us
  starting transfers between devices: 19.8 us -> 17.4 us
  Pallas kernels: 9.87 us -> 9.04 us
    ppermute x16, waiting for transfers between devices: 6.11 us -> 8.61 us  [swap(): return lax.ppermute(value, axis, [(i, i ^ offset) for i in range(size)])]
    ppermute x16, starting transfers between devices: 19.8 us -> 17.4 us  [swap(): return lax.ppermute(value, axis, [(i, i ^ offset) for i in range(size)])]
    pallas_call x2 -> x1, Pallas kernels: 4.16 us -> 3.33 us  [body(): pl.pallas_call(lambda *refs: finish_kernel(grid, *refs), in_specs=[vmem]...]
  transfers between devices with their start and end apart: 16 -> 16, of which waited for: 5 -> 5; matrix products, arithmetic and copies ran while one was open for 0% -> 1% of each run, Pallas kernels for 26% -> 24%
where the time goes in v5:
time: 37.5 us; the launch traced here: 37.3 us
  starting transfers between devices  17.4 us (46%)
  Pallas kernels  9.04 us (24%)
  waiting for transfers between devices  8.61 us (23%)
  between operations  0.82 us (2%)
  other arithmetic  0.79 us (2%)
  local copies, waits for them, and re-layouts  0.66 us (2%)
    ppermute x16, starting transfers between devices, swap(): return lax.ppermute(value, axis, [(i, i ^ offset) for i in range(size)])  17.4 us
    ppermute x16, waiting for transfers between devices, swap(): return lax.ppermute(value, axis, [(i, i ^ offset) for i in range(size)])  8.61 us
    pallas_call x1, Pallas kernels, body(): pl.pallas_call(lambda *refs: finish_kernel(grid, *refs), in_specs=[vmem]...  3.33 us
    pallas_call x1, Pallas kernels, body(): call(prepare_kernel, (full((n, n)), full((depth, breadth), BF16), full((d...  3.1 us
    pallas_call x1, Pallas kernels, body(): call(lambda *refs: cbar_kernel(grid, *refs), (full((n, depth)), full((wid...  1.01 us
    pallas_call x1, Pallas kernels, body(): call(trailing_kernel, (full((n // 2, breadth)),) * 2, flops=10 ** 9)  0.97 us
  transfers between devices with their start and end apart: 16, of which 5 were waited for; matrix products, arithmetic and copies ran while one was open for 1% of the time, Pallas kernels for 24%

profile of v5, /device:TPU:0, one launch (start us, length us, event | category | flops | bytes accessed | tf_op | source)
XLA Modules:
  0.0 37.3 jit_solution(3029583381068027310)
XLA Ops:
  0.6 3.1 %collective-permute-start.7 = (f32[8,2048]{1,0:T(8,128)}, f32[8,2048]{1,0:T(8,128)S(1)}, u32[]{:S(2)}, u32[]{:S(2)}) collective-permute-start(f32[8,2048]{1,0:T(8,128)} %param.12), channel_id=1, source_target_pairs={{0,8},{2,10},{4,12},{6,14},{8,0},{10,2},{12,4},{14,6},{16,24},{18,... | collective-permute-start | bytes 196616 | tf_op jit(solution)/shard_map/ppermute | solution.py:57
  3.7 2.6 %collective-permute-start.8 = (f32[8,2048]{1,0:T(8,128)}, f32[8,2048]{1,0:T(8,128)S(1)}, u32[]{:S(2)}, u32[]{:S(2)}) collective-permute-start(f32[8,2048]{1,0:T(8,128)} %param.12), channel_id=1, source_target_pairs={{0,16},{2,18},{4,20},{6,22},{8,24},{10,26},{12,28},{14,30},{16,0},... | collective-permute-start | bytes 196616 | tf_op jit(solution)/shard_map/ppermute | solution.py:57
  6.3 0.0 collective-permute-start.9
  6.3 1.7 %collective-permute-start = (f32[64,512]{1,0:T(8,128)}, f32[64,512]{1,0:T(8,128)S(1)}, u32[]{:S(2)}, u32[]{:S(2)}) collective-permute-start(f32[64,512]{1,0:T(8,128)} %bitcast.5), channel_id=1, source_target_pairs={{0,1},{1,0},{2,3},{3,2},{4,5},{5,4},{6,7},{7,6},{8,9},{9,8},{10,11... | collective-permute-start | bytes 393224 | tf_op jit(solution)/shard_map/ppermute | solution.py:57
  8.1 0.0 copy-start.2
  8.1 0.3 collective-permute-start.1
  8.4 0.5 %copy-done.2 = f32[128,128]{1,0:T(8,128)S(1)} copy-done((f32[128,128]{1,0:T(8,128)S(1)}, f32[128,128]{1,0:T(8,128)}, u32[]{:S(2)}) %copy-start.2) | copy-done | bytes 65560
  8.9 0.0 copy-start.6
  8.9 0.0 copy-start.5
  8.9 3.1 %shard_map.112 = (f32[128,128]{1,0:T(8,128)S(1)}, bf16[512,2048]{1,0:T(8,128)(2,1)S(1)}, bf16[512,2048]{1,0:T(8,128)(2,1)S(1)}) custom-call(f32[128,128]{1,0:T(8,128)S(1)} %copy-done.2, f32[128,128]{1,0:T(8,128)S(1)} %shard_map.111.identity_ref, f32[512,2048]{1,0:T(8,128)} %b_hbm.1), custom_call_target="tpu_custom_call" | custom-call | flops 4000000000 | bytes 1 | tf_op jit(solution)/shard_map/pallas_call | solution.py:289
  12.0 0.0 copy-done.6
  12.0 0.0 collective-permute-done.7
  12.0 0.0 collective-permute-done.8
  12.0 0.6 %collective-permute-done.9 = f32[8,2048]{1,0:T(8,128)S(1)} collective-permute-done((f32[8,2048]{1,0:T(8,128)}, f32[8,2048]{1,0:T(8,128)S(1)}, u32[]{:S(2)}, u32[]{:S(2)}) %collective-permute-start.9) | collective-permute-done | bytes 65568 | tf_op jit(solution)/shard_map/ppermute | solution.py:57
  12.6 1.6 %collective-permute-start.10 = (f32[32,2048]{1,0:T(8,128)S(1)}, f32[32,2048]{1,0:T(8,128)S(1)}, u32[]{:S(2)}, u32[]{:S(2)}) collective-permute-start(f32[32,2048]{1,0:T(8,128)S(1)} %pad_maximum_fusion), channel_id=1, source_target_pairs={{0,4},{2,6},{4,0},{6,2},{8,12},{10,14},{12,8},{14,10},{16,20},{18,... | collective-permute-start | bytes 786440 | tf_op jit(solution)/shard_map/ppermute | solution.py:57
  14.2 0.0 collective-permute-done.refs_2_
  14.2 0.0 copy-done.5
  14.2 0.0 copy-start.1
  14.2 1.0 %shard_map.113 = (f32[128,512]{1,0:T(8,128)S(1)}, f32[64,512]{1,0:T(8,128)}, f32[128,512]{1,0:T(8,128)S(1)}, bf16[256,512]{1,0:T(8,128)(2,1)S(1)}) custom-call(f32[128,128]{1,0:T(8,128)S(1)} %get-tuple-element.22.refs_0_.refs_3_, f32[64,512]{1,0:T(8,128)S(1)} %bitcast.6, f32[64,512]{1,0:T(8,128)S(1)} %collective-permute-done.refs_2_), custom_call_target="tpu_custom_call" | custom-call | flops 1000000000 | bytes 1 | tf_op jit(solution)/shard_map/pallas_call | solution.py:296
  15.2 0.0 copy-start
  15.2 0.0 copy-start.3
  15.2 0.0 copy-start.4
  15.2 1.0 %shard_map.114 = (f32[64,2048]{1,0:T(8,128)S(1)}, f32[64,2048]{1,0:T(8,128)S(1)}) custom-call(bf16[256,512]{1,0:T(8,128)(2,1)S(1)} %get-tuple-element.26.stack_ref, bf16[512,2048]{1,0:T(8,128)(2,1)S(1)} %get-tuple-element.27.high_ref, bf16[512,2048]{1,0:T(8,128)(2,1)S(1)} %get-tuple-element.28.low_ref), custom_call_target="tpu_custom_call" | custom-call | flops 1000000000 | bytes 1 | tf_op jit(solution)/shard_map/pallas_call | solution.py:301
  16.2 0.1 collective-permute-start.3
  16.3 0.0 collective-permute-done.1.refs_2_
  16.3 0.0 copy-done.1
  16.3 0.6 %shard_map.115 = f32[8,1152]{1,0:T(8,128)S(1)} custom-call(f32[128,512]{1,0:T(8,128)S(1)} %get-tuple-element.30.refs_0_, f32[64,512]{1,0:T(8,128)S(1)} %bitcast.4, f32[64,512]{1,0:T(8,128)S(1)} %collective-permute-done.1.refs_2_), custom_call_target="tpu_custom_call" | custom-call | bytes 1 | tf_op jit(solution)/shard_map/pallas_call | solution.py:302
  16.9 0.5 %collective-permute-start.2 = (f32[8,1152]{1,0:T(8,128)S(1)}, f32[8,1152]{1,0:T(8,128)S(1)}, u32[]{:S(2)}, u32[]{:S(2)}) collective-permute-start(f32[8,1152]{1,0:T(8,128)S(1)} %shard_map.115), channel_id=1, source_target_pairs={{0,2},{2,0},{4,6},{6,4},{8,10},{10,8},{12,14},{14,12},{16,18},{18,... | collective-permute-start | bytes 110600 | tf_op jit(solution)/shard_map/ppermute | solution.py:57
  17.5 0.9 %collective-permute-done.2 = f32[8,1152]{1,0:T(8,128)S(1)} collective-permute-done((f32[8,1152]{1,0:T(8,128)S(1)}, f32[8,1152]{1,0:T(8,128)S(1)}, u32[]{:S(2)}, u32[]{:S(2)}) %collective-permute-start.2) | collective-permute-done | bytes 36896 | tf_op jit(solution)/shard_map/ppermute | solution.py:57
  18.4 0.0 collective-permute-done.3
  18.4 0.1 add.25
  18.4 0.2 collective-permute-start.4
  18.7 0.6 %collective-permute-start.6 = (f32[32,2048]{1,0:T(8,128)S(1)}, f32[32,2048]{1,0:T(8,128)S(1)}, u32[]{:S(2)}, u32[]{:S(2)}) collective-permute-start(f32[32,2048]{1,0:T(8,128)S(1)} %get-tuple-element.40), channel_id=1, source_target_pairs={{0,4},{2,6},{4,0},{6,2},{8,12},{10,14},{12,8},{14,10},{16,20},{18,... | collective-permute-start | bytes 786440 | tf_op jit(solution)/shard_map/ppermute | solution.py:57
  19.3 0.0 collective-permute-done.10
  19.3 0.1 collective-permute-start.11
  19.4 3.1 %collective-permute-done.4 = f32[8,1152]{1,0:T(8,128)S(1)} collective-permute-done((f32[8,1152]{1,0:T(8,128)S(1)}, f32[8,1152]{1,0:T(8,128)S(1)}, u32[]{:S(2)}, u32[]{:S(2)}) %collective-permute-start.4) | collective-permute-done | bytes 36896 | tf_op jit(solution)/shard_map/ppermute | solution.py:57
  22.5 1.6 %collective-permute-start.5 = (f32[8,1152]{1,0:T(8,128)S(1)}, f32[8,1152]{1,0:T(8,128)S(1)}, u32[]{:S(2)}, u32[]{:S(2)}) collective-permute-start(f32[8,1152]{1,0:T(8,128)S(1)} %add.26), channel_id=1, source_target_pairs={{0,16},{2,18},{4,20},{6,22},{8,24},{10,26},{12,28},{14,30},{16,0},... | collective-permute-start | bytes 110600 | tf_op jit(solution)/shard_map/ppermute | solution.py:57
  24.1 3.6 %collective-permute-done.5 = f32[8,1152]{1,0:T(8,128)S(1)} collective-permute-done((f32[8,1152]{1,0:T(8,128)S(1)}, f32[8,1152]{1,0:T(8,128)S(1)}, u32[]{:S(2)}, u32[]{:S(2)}) %collective-permute-start.5) | collective-permute-done | bytes 36896 | tf_op jit(solution)/shard_map/ppermute | solution.py:57
  27.7 0.5 %collective-permute-start.12 = (f32[8,1152]{1,0:T(8,128)S(1)}, f32[8,1152]{1,0:T(8,128)S(1)}, u32[]{:S(2)}, u32[]{:S(2)}) collective-permute-start(f32[8,1152]{1,0:T(8,128)S(1)} %add.27.refs_8_), channel_id=1, source_target_pairs={{0,4},{2,6},{4,0},{6,2},{8,12},{10,14},{12,8},{14,10},{16,20},{18,... | collective-permute-start | bytes 110600 | tf_op jit(solution)/shard_map/ppermute | solution.py:57
  28.3 0.0 collective-permute-done.6
  28.3 2.7 %collective-permute-start.13 = (f32[8,2048]{1,0:T(8,128)S(1)}, f32[8,2048]{1,0:T(8,128)S(1)}, u32[]{:S(2)}, u32[]{:S(2)}) collective-permute-start(f32[8,2048]{1,0:T(8,128)S(1)} %get-tuple-element.44), channel_id=1, source_target_pairs={{0,24},{2,26},{4,28},{6,30},{8,16},{10,18},{12,20},{14,22},{16,8},... | collective-permute-start | bytes 196616 | tf_op jit(solution)/shard_map/ppermute | solution.py:57
  31.1 0.0 collective-permute-start.14
  31.1 1.7 %collective-permute-start.15 = (f32[8,2048]{1,0:T(8,128)S(1)}, f32[8,2048]{1,0:T(8,128)S(1)}, u32[]{:S(2)}, u32[]{:S(2)}) collective-permute-start(f32[8,2048]{1,0:T(8,128)S(1)} %get-tuple-element.42), channel_id=1, source_target_pairs={{0,8},{2,10},{4,12},{6,14},{8,0},{10,2},{12,4},{14,6},{16,24},{18,... | collective-permute-start | bytes 196616 | tf_op jit(solution)/shard_map/ppermute | solution.py:57
  32.8 0.0 collective-permute-done.12.refs_9_
  32.8 0.0 collective-permute-done.11.refs_7_
  32.8 0.0 copy-done
  32.8 0.0 copy-done.3
  32.8 0.0 copy-done.4
  32.8 3.3 %shard_map.116 = (f32[512,2048]{1,0:T(8,128)}, f32[8,64]{1,0:T(8,128)}, f32[8,2048]{1,0:T(8,128)S(1)}) custom-call(f32[128,512]{1,0:T(8,128)S(1)} %get-tuple-element.24.refs_0_, f32[512,2048]{1,0:T(8,128)S(1)} %copy-done, f32[128,128]{1,0:T(8,128)S(1)} %copy-done.2, f32[128,128]{1,0:T(8,128)S(1)} %get-tuple-element.22.refs_0_.refs_3_, ...), custom_call_target="tpu_custom_call" | custom-call | flops 1000000000 | bytes 1 | tf_op jit(solution)/shard_map/pallas_call | solution.py:323
  36.2 0.0 collective-permute-done.13
  36.2 0.5 %collective-permute-done.14 = f32[8,2048]{1,0:T(8,128)S(1)} collective-permute-done((f32[8,2048]{1,0:T(8,128)S(1)}, f32[8,2048]{1,0:T(8,128)S(1)}, u32[]{:S(2)}, u32[]{:S(2)}) %collective-permute-start.14) | collective-permute-done | bytes 65568 | tf_op jit(solution)/shard_map/ppermute | solution.py:57
  36.6 0.0 collective-permute-done.15
  36.6 0.7 %fusion.1 = f32[8,2048]{1,0:T(8,128)} fusion(f32[8,2048]{1,0:T(8,128)S(1)} %get-tuple-element.39, f32[8,2048]{1,0:T(8,128)S(1)} %collective-permute-done.13, f32[32,2048]{1,0:T(8,128)S(1)} %add.28, f32[8,2048]{1,0:T(8,128)S(1)} %collective-permute-done.14, f32[8,2048]{1,0:T(8,128)S(1)} %collective-permute-done.15), kind=kLoop, calls=%fused_computation.3 | loop fusion | flops 65536 | bytes 393216 | tf_op jit(solution)/shard_map/sub | solution.py:334
  (13 shorter events, 0.2 us)
Async XLA Ops:
  0.6 11.4 %collective-permute-start.7 = (f32[8,2048]{1,0:T(8,128)}, f32[8,2048]{1,0:T(8,128)S(1)}, u32[]{:S(2)}, u32[]{:S(2)}) collective-permute-start(f32[8,2048]{1,0:T(8,128)} %param.12), channel_id=1, source_target_pairs={{0,8},{2,10},{4,12},{6,14},{8,0},{10,2},{12,4},{14,6},{16,24},{18,... | collective-permute-start | bytes 196616 | tf_op jit(solution)/shard_map/ppermute | solution.py:57
  3.7 8.3 %collective-permute-start.8 = (f32[8,2048]{1,0:T(8,128)}, f32[8,2048]{1,0:T(8,128)S(1)}, u32[]{:S(2)}, u32[]{:S(2)}) collective-permute-start(f32[8,2048]{1,0:T(8,128)} %param.12), channel_id=1, source_target_pairs={{0,16},{2,18},{4,20},{6,22},{8,24},{10,26},{12,28},{14,30},{16,0},... | collective-permute-start | bytes 196616 | tf_op jit(solution)/shard_map/ppermute | solution.py:57
  6.3 6.3 %collective-permute-start.9 = (f32[8,2048]{1,0:T(8,128)}, f32[8,2048]{1,0:T(8,128)S(1)}, u32[]{:S(2)}, u32[]{:S(2)}) collective-permute-start(f32[8,2048]{1,0:T(8,128)} %param.12), channel_id=1, source_target_pairs={{0,24},{2,26},{4,28},{6,30},{8,16},{10,18},{12,20},{14,22},{16,8},... | collective-permute-start | bytes 196616 | tf_op jit(solution)/shard_map/ppermute | solution.py:57
  6.3 7.9 %collective-permute-start = (f32[64,512]{1,0:T(8,128)}, f32[64,512]{1,0:T(8,128)S(1)}, u32[]{:S(2)}, u32[]{:S(2)}) collective-permute-start(f32[64,512]{1,0:T(8,128)} %bitcast.5), channel_id=1, source_target_pairs={{0,1},{1,0},{2,3},{3,2},{4,5},{5,4},{6,7},{7,6},{8,9},{9,8},{10,11... | collective-permute-start | bytes 393224 | tf_op jit(solution)/shard_map/ppermute | solution.py:57
  8.1 0.8 %copy-start.2 = (f32[128,128]{1,0:T(8,128)S(1)}, f32[128,128]{1,0:T(8,128)}, u32[]{:S(2)}) copy-start(f32[128,128]{1,0:T(8,128)} %refs_2_.1) | copy-start | bytes 196612
  8.1 8.3 %collective-permute-start.1 = (f32[64,512]{1,0:T(8,128)}, f32[64,512]{1,0:T(8,128)S(1)}, u32[]{:S(2)}, u32[]{:S(2)}) collective-permute-start(f32[64,512]{1,0:T(8,128)} %bitcast.3), channel_id=1, source_target_pairs={{0,1},{1,0},{2,3},{3,2},{4,5},{5,4},{6,7},{7,6},{8,9},{9,8},{10,11... | collective-permute-start | bytes 393224 | tf_op jit(solution)/shard_map/ppermute | solution.py:57
  8.9 3.1 %copy-start.6 = (f32[8,2048]{1,0:T(8,128)S(1)}, f32[8,2048]{1,0:T(8,128)}, u32[]{:S(2)}) copy-start(f32[8,2048]{1,0:T(8,128)} %param.12) | copy-start | bytes 196612
  8.9 5.3 %copy-start.5 = (f32[512,64]{0,1:T(8,128)S(1)}, f32[512,64]{0,1:T(8,128)}, u32[]{:S(2)}) copy-start(f32[512,64]{0,1:T(8,128)} %param.9) | copy-start | bytes 393220
  12.6 6.6 %collective-permute-start.10 = (f32[32,2048]{1,0:T(8,128)S(1)}, f32[32,2048]{1,0:T(8,128)S(1)}, u32[]{:S(2)}, u32[]{:S(2)}) collective-permute-start(f32[32,2048]{1,0:T(8,128)S(1)} %pad_maximum_fusion), channel_id=1, source_target_pairs={{0,4},{2,6},{4,0},{6,2},{8,12},{10,14},{12,8},{14,10},{16,20},{18,... | collective-permute-start | bytes 786440 | tf_op jit(solution)/shard_map/ppermute | solution.py:57
  14.2 2.1 %copy-start.1 = (f32[512,64]{0,1:T(8,128)S(1)}, f32[512,64]{0,1:T(8,128)}, u32[]{:S(2)}) copy-start(f32[512,64]{0,1:T(8,128)} %param.8) | copy-start | bytes 393220
  15.2 17.6 %copy-start = (f32[512,2048]{1,0:T(8,128)S(1)}, f32[512,2048]{1,0:T(8,128)}, u32[]{:S(2)}) copy-start(f32[512,2048]{1,0:T(8,128)} %refs_1_.1) | copy-start | bytes 12582916
  15.2 17.6 %copy-start.3 = (f32[128,128]{1,0:T(8,128)S(1)}, f32[128,128]{1,0:T(8,128)}, u32[]{:S(2)}) copy-start(f32[128,128]{1,0:T(8,128)} %refs_4_) | copy-start | bytes 196612
  15.2 17.6 %copy-start.4 = (f32[8,2048]{1,0:T(8,128)S(1)}, f32[8,2048]{1,0:T(8,128)}, u32[]{:S(2)}) copy-start(f32[8,2048]{1,0:T(8,128)} %refs_5_.1) | copy-start | bytes 196612
  16.2 2.2 %collective-permute-start.3 = (f32[64,2048]{1,0:T(8,128)S(1)}, f32[64,2048]{1,0:T(8,128)S(1)}, u32[]{:S(2)}, u32[]{:S(2)}) collective-permute-start(f32[64,2048]{1,0:T(8,128)S(1)} %get-tuple-element.29), channel_id=1, source_target_pairs={{0,2},{2,0},{4,6},{6,4},{8,10},{10,8},{12,14},{14,12},{16,18},{18,... | collective-permute-start | bytes 1572872 | tf_op jit(solution)/shard_map/ppermute | solution.py:57
  16.9 1.4 %collective-permute-start.2 = (f32[8,1152]{1,0:T(8,128)S(1)}, f32[8,1152]{1,0:T(8,128)S(1)}, u32[]{:S(2)}, u32[]{:S(2)}) collective-permute-start(f32[8,1152]{1,0:T(8,128)S(1)} %shard_map.115), channel_id=1, source_target_pairs={{0,2},{2,0},{4,6},{6,4},{8,10},{10,8},{12,14},{14,12},{16,18},{18,... | collective-permute-start | bytes 110600 | tf_op jit(solution)/shard_map/ppermute | solution.py:57
  18.4 4.0 %collective-permute-start.4 = (f32[8,1152]{1,0:T(8,128)S(1)}, f32[8,1152]{1,0:T(8,128)S(1)}, u32[]{:S(2)}, u32[]{:S(2)}) collective-permute-start(f32[8,1152]{1,0:T(8,128)S(1)} %add.24), channel_id=1, source_target_pairs={{0,8},{2,10},{4,12},{6,14},{8,0},{10,2},{12,4},{14,6},{16,24},{18,... | collective-permute-start | bytes 110600 | tf_op jit(solution)/shard_map/ppermute | solution.py:57
  18.7 9.6 %collective-permute-start.6 = (f32[32,2048]{1,0:T(8,128)S(1)}, f32[32,2048]{1,0:T(8,128)S(1)}, u32[]{:S(2)}, u32[]{:S(2)}) collective-permute-start(f32[32,2048]{1,0:T(8,128)S(1)} %get-tuple-element.40), channel_id=1, source_target_pairs={{0,4},{2,6},{4,0},{6,2},{8,12},{10,14},{12,8},{14,10},{16,20},{18,... | collective-permute-start | bytes 786440 | tf_op jit(solution)/shard_map/ppermute | solution.py:57
  19.3 13.5 %collective-permute-start.11 = (f32[64,2048]{1,0:T(8,128)S(1)}, f32[64,2048]{1,0:T(8,128)S(1)}, u32[]{:S(2)}, u32[]{:S(2)}) collective-permute-start(f32[64,2048]{1,0:T(8,128)S(1)} %constant_dynamic-update-slice_fusion.refs_6_), channel_id=1, source_target_pairs={{0,2},{2,0},{4,6},{6,4},{8,10},{10,8},{12,14},{14,12},{16,18},{18,... | collective-permute-start | bytes 1572872 | tf_op jit(solution)/shard_map/ppermute | solution.py:57
  22.5 5.3 %collective-permute-start.5 = (f32[8,1152]{1,0:T(8,128)S(1)}, f32[8,1152]{1,0:T(8,128)S(1)}, u32[]{:S(2)}, u32[]{:S(2)}) collective-permute-start(f32[8,1152]{1,0:T(8,128)S(1)} %add.26), channel_id=1, source_target_pairs={{0,16},{2,18},{4,20},{6,22},{8,24},{10,26},{12,28},{14,30},{16,0},... | collective-permute-start | bytes 110600 | tf_op jit(solution)/shard_map/ppermute | solution.py:57
  27.7 5.1 %collective-permute-start.12 = (f32[8,1152]{1,0:T(8,128)S(1)}, f32[8,1152]{1,0:T(8,128)S(1)}, u32[]{:S(2)}, u32[]{:S(2)}) collective-permute-start(f32[8,1152]{1,0:T(8,128)S(1)} %add.27.refs_8_), channel_id=1, source_target_pairs={{0,4},{2,6},{4,0},{6,2},{8,12},{10,14},{12,8},{14,10},{16,20},{18,... | collective-permute-start | bytes 110600 | tf_op jit(solution)/shard_map/ppermute | solution.py:57
  28.3 7.8 %collective-permute-start.13 = (f32[8,2048]{1,0:T(8,128)S(1)}, f32[8,2048]{1,0:T(8,128)S(1)}, u32[]{:S(2)}, u32[]{:S(2)}) collective-permute-start(f32[8,2048]{1,0:T(8,128)S(1)} %get-tuple-element.44), channel_id=1, source_target_pairs={{0,24},{2,26},{4,28},{6,30},{8,16},{10,18},{12,20},{14,22},{16,8},... | collective-permute-start | bytes 196616 | tf_op jit(solution)/shard_map/ppermute | solution.py:57
  31.1 5.6 %collective-permute-start.14 = (f32[8,2048]{1,0:T(8,128)S(1)}, f32[8,2048]{1,0:T(8,128)S(1)}, u32[]{:S(2)}, u32[]{:S(2)}) collective-permute-start(f32[8,2048]{1,0:T(8,128)S(1)} %get-tuple-element.43), channel_id=1, source_target_pairs={{0,16},{2,18},{4,20},{6,22},{8,24},{10,26},{12,28},{14,30},{16,0},... | collective-permute-start | bytes 196616 | tf_op jit(solution)/shard_map/ppermute | solution.py:57
  31.1 5.6 %collective-permute-start.15 = (f32[8,2048]{1,0:T(8,128)S(1)}, f32[8,2048]{1,0:T(8,128)S(1)}, u32[]{:S(2)}, u32[]{:S(2)}) collective-permute-start(f32[8,2048]{1,0:T(8,128)S(1)} %get-tuple-element.42), channel_id=1, source_target_pairs={{0,8},{2,10},{4,12},{6,14},{8,0},{10,2},{12,4},{14,6},{16,24},{18,... | collective-permute-start | bytes 196616 | tf_op jit(solution)/shard_map/ppermute | solution.py:57

commit v6 on v5

--- a/solution.py
+++ b/solution.py
@@ -305,19 +305,19 @@
         product = add_pairs(row_parts(product, grid.core))
         summed = keep + swap(send, "row", rows, grid.core[1])
         product, summed = lax.optimization_barrier((product, summed))
-        panel = after(panel, summed)
         product = add_pairs(row_parts(product, grid.z_near))
         product_parts = row_parts(product, grid.z_far)
-        panel_parts = row_parts(panel, grid.core)
         product = add_pairs(product_parts)
         for count, stride in grid.order[1:]:
             own, *sends = summed.reshape(count, -1, breadth)
             got = [swap(value, "row", rows, d * stride) for d, value in list(enumerate(sends, 1))[::-1]][::-1]
             if stride == grid.x[1]:
                 own = after(own, product)
+                panel = after(panel, product)
             summed = add_pairs([own] + got[::-1])
             if stride == grid.x[1]:
                 dbar_in = after(dbar_in, summed)
+        panel_parts = row_parts(panel, grid.core)
         vmem = pl.BlockSpec(memory_space=pltpu.VMEM)
         product_parts = row_parts(product, grid.x)
         bbar_out, kernel_out, rbar = pl.pallas_call(

time: 37.5 us -> 38 us (1.013)
  waiting for transfers between devices: 8.61 us -> 9.21 us
    ppermute x16, waiting for transfers between devices: 8.61 us -> 9.21 us  [swap(): return lax.ppermute(value, axis, [(i, i ^ offset) for i in range(size)])]
where the time goes in v6:
time: 38 us; the launch traced here: 37.9 us
  starting transfers between devices  17.4 us (46%)
  waiting for transfers between devices  9.21 us (24%)
  Pallas kernels  9.04 us (24%)
  between operations  0.82 us (2%)
  other arithmetic  0.79 us (2%)
  local copies, waits for them, and re-layouts  0.66 us (2%)
    ppermute x16, starting transfers between devices, swap(): return lax.ppermute(value, axis, [(i, i ^ offset) for i in range(size)])  17.4 us
    ppermute x16, waiting for transfers between devices, swap(): return lax.ppermute(value, axis, [(i, i ^ offset) for i in range(size)])  9.21 us
    pallas_call x1, Pallas kernels, body(): pl.pallas_call(lambda *refs: finish_kernel(grid, *refs), in_specs=[vmem]...  3.33 us
    pallas_call x1, Pallas kernels, body(): call(prepare_kernel, (full((n, n)), full((depth, breadth), BF16), full((d...  3.1 us
    pallas_call x1, Pallas kernels, body(): call(lambda *refs: cbar_kernel(grid, *refs), (full((n, depth)), full((wid...  1.01 us
    pallas_call x1, Pallas kernels, body(): call(trailing_kernel, (full((n // 2, breadth)),) * 2, flops=10 ** 9)  0.97 us
  transfers between devices with their start and end apart: 16, of which 5 were waited for; matrix products, arithmetic and copies ran while one was open for 1% of the time, Pallas kernels for 24%

profile of v6, /device:TPU:0, one launch (start us, length us, event | category | flops | bytes accessed | tf_op | source)
XLA Modules:
  0.0 37.9 jit_solution(1901187457284395610)
XLA Ops:
  0.6 3.1 %collective-permute-start.7 = (f32[8,2048]{1,0:T(8,128)}, f32[8,2048]{1,0:T(8,128)S(1)}, u32[]{:S(2)}, u32[]{:S(2)}) collective-permute-start(f32[8,2048]{1,0:T(8,128)} %param.12), channel_id=1, source_target_pairs={{0,8},{2,10},{4,12},{6,14},{8,0},{10,2},{12,4},{14,6},{16,24},{18,... | collective-permute-start | bytes 196616 | tf_op jit(solution)/shard_map/ppermute | solution.py:57
  3.7 2.6 %collective-permute-start.8 = (f32[8,2048]{1,0:T(8,128)}, f32[8,2048]{1,0:T(8,128)S(1)}, u32[]{:S(2)}, u32[]{:S(2)}) collective-permute-start(f32[8,2048]{1,0:T(8,128)} %param.12), channel_id=1, source_target_pairs={{0,16},{2,18},{4,20},{6,22},{8,24},{10,26},{12,28},{14,30},{16,0},... | collective-permute-start | bytes 196616 | tf_op jit(solution)/shard_map/ppermute | solution.py:57
  6.3 0.0 collective-permute-start.9
  6.3 1.7 %collective-permute-start = (f32[64,512]{1,0:T(8,128)}, f32[64,512]{1,0:T(8,128)S(1)}, u32[]{:S(2)}, u32[]{:S(2)}) collective-permute-start(f32[64,512]{1,0:T(8,128)} %bitcast.5), channel_id=1, source_target_pairs={{0,1},{1,0},{2,3},{3,2},{4,5},{5,4},{6,7},{7,6},{8,9},{9,8},{10,11... | collective-permute-start | bytes 393224 | tf_op jit(solution)/shard_map/ppermute | solution.py:57
  8.1 0.0 copy-start.2
  8.1 0.3 collective-permute-start.1
  8.4 0.5 %copy-done.2 = f32[128,128]{1,0:T(8,128)S(1)} copy-done((f32[128,128]{1,0:T(8,128)S(1)}, f32[128,128]{1,0:T(8,128)}, u32[]{:S(2)}) %copy-start.2) | copy-done | bytes 65560
  8.9 0.0 copy-start.6
  8.9 0.0 copy-start.5
  8.9 3.1 %shard_map.112 = (f32[128,128]{1,0:T(8,128)S(1)}, bf16[512,2048]{1,0:T(8,128)(2,1)S(1)}, bf16[512,2048]{1,0:T(8,128)(2,1)S(1)}) custom-call(f32[128,128]{1,0:T(8,128)S(1)} %copy-done.2, f32[128,128]{1,0:T(8,128)S(1)} %shard_map.111.identity_ref, f32[512,2048]{1,0:T(8,128)} %b_hbm.1), custom_call_target="tpu_custom_call" | custom-call | flops 4000000000 | bytes 1 | tf_op jit(solution)/shard_map/pallas_call | solution.py:289
  12.0 0.0 copy-done.6
  12.0 0.0 collective-permute-done.7
  12.0 0.0 collective-permute-done.8
  12.0 0.6 %collective-permute-done.9 = f32[8,2048]{1,0:T(8,128)S(1)} collective-permute-done((f32[8,2048]{1,0:T(8,128)}, f32[8,2048]{1,0:T(8,128)S(1)}, u32[]{:S(2)}, u32[]{:S(2)}) %collective-permute-start.9) | collective-permute-done | bytes 65568 | tf_op jit(solution)/shard_map/ppermute | solution.py:57
  12.6 1.6 %collective-permute-start.10 = (f32[32,2048]{1,0:T(8,128)S(1)}, f32[32,2048]{1,0:T(8,128)S(1)}, u32[]{:S(2)}, u32[]{:S(2)}) collective-permute-start(f32[32,2048]{1,0:T(8,128)S(1)} %pad_maximum_fusion), channel_id=1, source_target_pairs={{0,4},{2,6},{4,0},{6,2},{8,12},{10,14},{12,8},{14,10},{16,20},{18,... | collective-permute-start | bytes 786440 | tf_op jit(solution)/shard_map/ppermute | solution.py:57
  14.2 0.0 collective-permute-done.refs_2_
  14.2 0.0 copy-done.5
  14.2 0.0 copy-start.1
  14.2 1.0 %shard_map.113 = (f32[128,512]{1,0:T(8,128)S(1)}, f32[64,512]{1,0:T(8,128)}, f32[128,512]{1,0:T(8,128)S(1)}, bf16[256,512]{1,0:T(8,128)(2,1)S(1)}) custom-call(f32[128,128]{1,0:T(8,128)S(1)} %get-tuple-element.22.refs_0_.refs_3_, f32[64,512]{1,0:T(8,128)S(1)} %bitcast.6, f32[64,512]{1,0:T(8,128)S(1)} %collective-permute-done.refs_2_), custom_call_target="tpu_custom_call" | custom-call | flops 1000000000 | bytes 1 | tf_op jit(solution)/shard_map/pallas_call | solution.py:296
  15.2 0.0 copy-start
  15.2 0.0 copy-start.3
  15.2 0.0 copy-start.4
  15.2 1.0 %shard_map.114 = (f32[64,2048]{1,0:T(8,128)S(1)}, f32[64,2048]{1,0:T(8,128)S(1)}) custom-call(bf16[256,512]{1,0:T(8,128)(2,1)S(1)} %get-tuple-element.26.stack_ref, bf16[512,2048]{1,0:T(8,128)(2,1)S(1)} %get-tuple-element.27.high_ref, bf16[512,2048]{1,0:T(8,128)(2,1)S(1)} %get-tuple-element.28.low_ref), custom_call_target="tpu_custom_call" | custom-call | flops 1000000000 | bytes 1 | tf_op jit(solution)/shard_map/pallas_call | solution.py:301
  16.2 0.1 collective-permute-start.3
  16.3 0.0 collective-permute-done.1.refs_2_
  16.3 0.0 copy-done.1
  16.3 0.6 %shard_map.115 = f32[8,1152]{1,0:T(8,128)S(1)} custom-call(f32[128,512]{1,0:T(8,128)S(1)} %get-tuple-element.30.refs_0_, f32[64,512]{1,0:T(8,128)S(1)} %bitcast.4, f32[64,512]{1,0:T(8,128)S(1)} %collective-permute-done.1.refs_2_), custom_call_target="tpu_custom_call" | custom-call | bytes 1 | tf_op jit(solution)/shard_map/pallas_call | solution.py:302
  16.9 0.5 %collective-permute-start.2 = (f32[8,1152]{1,0:T(8,128)S(1)}, f32[8,1152]{1,0:T(8,128)S(1)}, u32[]{:S(2)}, u32[]{:S(2)}) collective-permute-start(f32[8,1152]{1,0:T(8,128)S(1)} %shard_map.115), channel_id=1, source_target_pairs={{0,2},{2,0},{4,6},{6,4},{8,10},{10,8},{12,14},{14,12},{16,18},{18,... | collective-permute-start | bytes 110600 | tf_op jit(solution)/shard_map/ppermute | solution.py:57
  17.5 0.9 %collective-permute-done.2 = f32[8,1152]{1,0:T(8,128)S(1)} collective-permute-done((f32[8,1152]{1,0:T(8,128)S(1)}, f32[8,1152]{1,0:T(8,128)S(1)}, u32[]{:S(2)}, u32[]{:S(2)}) %collective-permute-start.2) | collective-permute-done | bytes 36896 | tf_op jit(solution)/shard_map/ppermute | solution.py:57
  18.4 0.0 collective-permute-done.3
  18.4 0.1 add.25
  18.4 0.2 collective-permute-start.4
  18.7 0.6 %collective-permute-start.6 = (f32[32,2048]{1,0:T(8,128)S(1)}, f32[32,2048]{1,0:T(8,128)S(1)}, u32[]{:S(2)}, u32[]{:S(2)}) collective-permute-start(f32[32,2048]{1,0:T(8,128)S(1)} %get-tuple-element.40), channel_id=1, source_target_pairs={{0,4},{2,6},{4,0},{6,2},{8,12},{10,14},{12,8},{14,10},{16,20},{18,... | collective-permute-start | bytes 786440 | tf_op jit(solution)/shard_map/ppermute | solution.py:57
  19.3 3.2 %collective-permute-done.4 = f32[8,1152]{1,0:T(8,128)S(1)} collective-permute-done((f32[8,1152]{1,0:T(8,128)S(1)}, f32[8,1152]{1,0:T(8,128)S(1)}, u32[]{:S(2)}, u32[]{:S(2)}) %collective-permute-start.4) | collective-permute-done | bytes 36896 | tf_op jit(solution)/shard_map/ppermute | solution.py:57
  22.5 1.6 %collective-permute-start.5 = (f32[8,1152]{1,0:T(8,128)S(1)}, f32[8,1152]{1,0:T(8,128)S(1)}, u32[]{:S(2)}, u32[]{:S(2)}) collective-permute-start(f32[8,1152]{1,0:T(8,128)S(1)} %add.26), channel_id=1, source_target_pairs={{0,16},{2,18},{4,20},{6,22},{8,24},{10,26},{12,28},{14,30},{16,0},... | collective-permute-start | bytes 110600 | tf_op jit(solution)/shard_map/ppermute | solution.py:57
  24.1 0.0 collective-permute-done.10
  24.1 3.6 %collective-permute-done.5 = f32[8,1152]{1,0:T(8,128)S(1)} collective-permute-done((f32[8,1152]{1,0:T(8,128)S(1)}, f32[8,1152]{1,0:T(8,128)S(1)}, u32[]{:S(2)}, u32[]{:S(2)}) %collective-permute-start.5) | collective-permute-done | bytes 36896 | tf_op jit(solution)/shard_map/ppermute | solution.py:57
  27.7 0.0 collective-permute-start.11
  27.7 0.6 %collective-permute-start.12 = (f32[8,1152]{1,0:T(8,128)S(1)}, f32[8,1152]{1,0:T(8,128)S(1)}, u32[]{:S(2)}, u32[]{:S(2)}) collective-permute-start(f32[8,1152]{1,0:T(8,128)S(1)} %add.27.refs_8_), channel_id=1, source_target_pairs={{0,4},{2,6},{4,0},{6,2},{8,12},{10,14},{12,8},{14,10},{16,20},{18,... | collective-permute-start | bytes 110600 | tf_op jit(solution)/shard_map/ppermute | solution.py:57
  28.3 0.0 collective-permute-done.6
  28.4 2.7 %collective-permute-start.13 = (f32[8,2048]{1,0:T(8,128)S(1)}, f32[8,2048]{1,0:T(8,128)S(1)}, u32[]{:S(2)}, u32[]{:S(2)}) collective-permute-start(f32[8,2048]{1,0:T(8,128)S(1)} %get-tuple-element.44), channel_id=1, source_target_pairs={{0,24},{2,26},{4,28},{6,30},{8,16},{10,18},{12,20},{14,22},{16,8},... | collective-permute-start | bytes 196616 | tf_op jit(solution)/shard_map/ppermute | solution.py:57
  31.1 0.0 collective-permute-start.14
  31.1 1.7 %collective-permute-start.15 = (f32[8,2048]{1,0:T(8,128)S(1)}, f32[8,2048]{1,0:T(8,128)S(1)}, u32[]{:S(2)}, u32[]{:S(2)}) collective-permute-start(f32[8,2048]{1,0:T(8,128)S(1)} %get-tuple-element.42), channel_id=1, source_target_pairs={{0,8},{2,10},{4,12},{6,14},{8,0},{10,2},{12,4},{14,6},{16,24},{18,... | collective-permute-start | bytes 196616 | tf_op jit(solution)/shard_map/ppermute | solution.py:57
  32.9 0.0 collective-permute-done.12.refs_9_
  32.9 0.0 collective-permute-done.11.refs_7_
  32.9 0.0 copy-done
  32.9 0.0 copy-done.3
  32.9 0.0 copy-done.4
  32.9 3.3 %shard_map.116 = (f32[512,2048]{1,0:T(8,128)}, f32[8,64]{1,0:T(8,128)}, f32[8,2048]{1,0:T(8,128)S(1)}) custom-call(f32[128,512]{1,0:T(8,128)S(1)} %get-tuple-element.24.refs_0_, f32[512,2048]{1,0:T(8,128)S(1)} %copy-done, f32[128,128]{1,0:T(8,128)S(1)} %copy-done.2, f32[128,128]{1,0:T(8,128)S(1)} %get-tuple-element.22.refs_0_.refs_3_, ...), custom_call_target="tpu_custom_call" | custom-call | flops 1000000000 | bytes 1 | tf_op jit(solution)/shard_map/pallas_call | solution.py:323
  36.2 0.0 collective-permute-done.13
  36.2 1.0 %collective-permute-done.14 = f32[8,2048]{1,0:T(8,128)S(1)} collective-permute-done((f32[8,2048]{1,0:T(8,128)S(1)}, f32[8,2048]{1,0:T(8,128)S(1)}, u32[]{:S(2)}, u32[]{:S(2)}) %collective-permute-start.14) | collective-permute-done | bytes 65568 | tf_op jit(solution)/shard_map/ppermute | solution.py:57
  37.2 0.0 collective-permute-done.15
  37.2 0.7 %fusion.1 = f32[8,2048]{1,0:T(8,128)} fusion(f32[8,2048]{1,0:T(8,128)S(1)} %get-tuple-element.39, f32[8,2048]{1,0:T(8,128)S(1)} %collective-permute-done.13, f32[32,2048]{1,0:T(8,128)S(1)} %add.28, f32[8,2048]{1,0:T(8,128)S(1)} %collective-permute-done.14, f32[8,2048]{1,0:T(8,128)S(1)} %collective-permute-done.15), kind=kLoop, calls=%fused_computation.3 | loop fusion | flops 65536 | bytes 393216 | tf_op jit(solution)/shard_map/sub | solution.py:334
  (13 shorter events, 0.2 us)
Async XLA Ops:
  0.6 11.4 %collective-permute-start.7 = (f32[8,2048]{1,0:T(8,128)}, f32[8,2048]{1,0:T(8,128)S(1)}, u32[]{:S(2)}, u32[]{:S(2)}) collective-permute-start(f32[8,2048]{1,0:T(8,128)} %param.12), channel_id=1, source_target_pairs={{0,8},{2,10},{4,12},{6,14},{8,0},{10,2},{12,4},{14,6},{16,24},{18,... | collective-permute-start | bytes 196616 | tf_op jit(solution)/shard_map/ppermute | solution.py:57
  3.7 8.3 %collective-permute-start.8 = (f32[8,2048]{1,0:T(8,128)}, f32[8,2048]{1,0:T(8,128)S(1)}, u32[]{:S(2)}, u32[]{:S(2)}) collective-permute-start(f32[8,2048]{1,0:T(8,128)} %param.12), channel_id=1, source_target_pairs={{0,16},{2,18},{4,20},{6,22},{8,24},{10,26},{12,28},{14,30},{16,0},... | collective-permute-start | bytes 196616 | tf_op jit(solution)/shard_map/ppermute | solution.py:57
  6.3 6.3 %collective-permute-start.9 = (f32[8,2048]{1,0:T(8,128)}, f32[8,2048]{1,0:T(8,128)S(1)}, u32[]{:S(2)}, u32[]{:S(2)}) collective-permute-start(f32[8,2048]{1,0:T(8,128)} %param.12), channel_id=1, source_target_pairs={{0,24},{2,26},{4,28},{6,30},{8,16},{10,18},{12,20},{14,22},{16,8},... | collective-permute-start | bytes 196616 | tf_op jit(solution)/shard_map/ppermute | solution.py:57
  6.3 7.9 %collective-permute-start = (f32[64,512]{1,0:T(8,128)}, f32[64,512]{1,0:T(8,128)S(1)}, u32[]{:S(2)}, u32[]{:S(2)}) collective-permute-start(f32[64,512]{1,0:T(8,128)} %bitcast.5), channel_id=1, source_target_pairs={{0,1},{1,0},{2,3},{3,2},{4,5},{5,4},{6,7},{7,6},{8,9},{9,8},{10,11... | collective-permute-start | bytes 393224 | tf_op jit(solution)/shard_map/ppermute | solution.py:57
  8.1 0.8 %copy-start.2 = (f32[128,128]{1,0:T(8,128)S(1)}, f32[128,128]{1,0:T(8,128)}, u32[]{:S(2)}) copy-start(f32[128,128]{1,0:T(8,128)} %refs_2_.1) | copy-start | bytes 196612
  8.1 8.3 %collective-permute-start.1 = (f32[64,512]{1,0:T(8,128)}, f32[64,512]{1,0:T(8,128)S(1)}, u32[]{:S(2)}, u32[]{:S(2)}) collective-permute-start(f32[64,512]{1,0:T(8,128)} %bitcast.3), channel_id=1, source_target_pairs={{0,1},{1,0},{2,3},{3,2},{4,5},{5,4},{6,7},{7,6},{8,9},{9,8},{10,11... | collective-permute-start | bytes 393224 | tf_op jit(solution)/shard_map/ppermute | solution.py:57
  8.9 3.1 %copy-start.6 = (f32[8,2048]{1,0:T(8,128)S(1)}, f32[8,2048]{1,0:T(8,128)}, u32[]{:S(2)}) copy-start(f32[8,2048]{1,0:T(8,128)} %param.12) | copy-start | bytes 196612
  8.9 5.3 %copy-start.5 = (f32[512,64]{0,1:T(8,128)S(1)}, f32[512,64]{0,1:T(8,128)}, u32[]{:S(2)}) copy-start(f32[512,64]{0,1:T(8,128)} %param.9) | copy-start | bytes 393220
  12.6 11.5 %collective-permute-start.10 = (f32[32,2048]{1,0:T(8,128)S(1)}, f32[32,2048]{1,0:T(8,128)S(1)}, u32[]{:S(2)}, u32[]{:S(2)}) collective-permute-start(f32[32,2048]{1,0:T(8,128)S(1)} %pad_maximum_fusion), channel_id=1, source_target_pairs={{0,4},{2,6},{4,0},{6,2},{8,12},{10,14},{12,8},{14,10},{16,20},{18,... | collective-permute-start | bytes 786440 | tf_op jit(solution)/shard_map/ppermute | solution.py:57
  14.2 2.1 %copy-start.1 = (f32[512,64]{0,1:T(8,128)S(1)}, f32[512,64]{0,1:T(8,128)}, u32[]{:S(2)}) copy-start(f32[512,64]{0,1:T(8,128)} %param.8) | copy-start | bytes 393220
  15.2 17.7 %copy-start = (f32[512,2048]{1,0:T(8,128)S(1)}, f32[512,2048]{1,0:T(8,128)}, u32[]{:S(2)}) copy-start(f32[512,2048]{1,0:T(8,128)} %refs_1_.1) | copy-start | bytes 12582916
  15.2 17.7 %copy-start.3 = (f32[128,128]{1,0:T(8,128)S(1)}, f32[128,128]{1,0:T(8,128)}, u32[]{:S(2)}) copy-start(f32[128,128]{1,0:T(8,128)} %refs_4_) | copy-start | bytes 196612
  15.2 17.7 %copy-start.4 = (f32[8,2048]{1,0:T(8,128)S(1)}, f32[8,2048]{1,0:T(8,128)}, u32[]{:S(2)}) copy-start(f32[8,2048]{1,0:T(8,128)} %refs_5_.1) | copy-start | bytes 196612
  16.2 2.2 %collective-permute-start.3 = (f32[64,2048]{1,0:T(8,128)S(1)}, f32[64,2048]{1,0:T(8,128)S(1)}, u32[]{:S(2)}, u32[]{:S(2)}) collective-permute-start(f32[64,2048]{1,0:T(8,128)S(1)} %get-tuple-element.29), channel_id=1, source_target_pairs={{0,2},{2,0},{4,6},{6,4},{8,10},{10,8},{12,14},{14,12},{16,18},{18,... | collective-permute-start | bytes 1572872 | tf_op jit(solution)/shard_map/ppermute | solution.py:57
  16.9 1.4 %collective-permute-start.2 = (f32[8,1152]{1,0:T(8,128)S(1)}, f32[8,1152]{1,0:T(8,128)S(1)}, u32[]{:S(2)}, u32[]{:S(2)}) collective-permute-start(f32[8,1152]{1,0:T(8,128)S(1)} %shard_map.115), channel_id=1, source_target_pairs={{0,2},{2,0},{4,6},{6,4},{8,10},{10,8},{12,14},{14,12},{16,18},{18,... | collective-permute-start | bytes 110600 | tf_op jit(solution)/shard_map/ppermute | solution.py:57
  18.4 4.0 %collective-permute-start.4 = (f32[8,1152]{1,0:T(8,128)S(1)}, f32[8,1152]{1,0:T(8,128)S(1)}, u32[]{:S(2)}, u32[]{:S(2)}) collective-permute-start(f32[8,1152]{1,0:T(8,128)S(1)} %add.24), channel_id=1, source_target_pairs={{0,8},{2,10},{4,12},{6,14},{8,0},{10,2},{12,4},{14,6},{16,24},{18,... | collective-permute-start | bytes 110600 | tf_op jit(solution)/shard_map/ppermute | solution.py:57
  18.7 9.7 %collective-permute-start.6 = (f32[32,2048]{1,0:T(8,128)S(1)}, f32[32,2048]{1,0:T(8,128)S(1)}, u32[]{:S(2)}, u32[]{:S(2)}) collective-permute-start(f32[32,2048]{1,0:T(8,128)S(1)} %get-tuple-element.40), channel_id=1, source_target_pairs={{0,4},{2,6},{4,0},{6,2},{8,12},{10,14},{12,8},{14,10},{16,20},{18,... | collective-permute-start | bytes 786440 | tf_op jit(solution)/shard_map/ppermute | solution.py:57
  22.5 5.3 %collective-permute-start.5 = (f32[8,1152]{1,0:T(8,128)S(1)}, f32[8,1152]{1,0:T(8,128)S(1)}, u32[]{:S(2)}, u32[]{:S(2)}) collective-permute-start(f32[8,1152]{1,0:T(8,128)S(1)} %add.26), channel_id=1, source_target_pairs={{0,16},{2,18},{4,20},{6,22},{8,24},{10,26},{12,28},{14,30},{16,0},... | collective-permute-start | bytes 110600 | tf_op jit(solution)/shard_map/ppermute | solution.py:57
  27.7 5.1 %collective-permute-start.11 = (f32[64,2048]{1,0:T(8,128)S(1)}, f32[64,2048]{1,0:T(8,128)S(1)}, u32[]{:S(2)}, u32[]{:S(2)}) collective-permute-start(f32[64,2048]{1,0:T(8,128)S(1)} %constant_dynamic-update-slice_fusion.refs_6_), channel_id=1, source_target_pairs={{0,2},{2,0},{4,6},{6,4},{8,10},{10,8},{12,14},{14,12},{16,18},{18,... | collective-permute-start | bytes 1572872 | tf_op jit(solution)/shard_map/ppermute | solution.py:57
  27.7 5.1 %collective-permute-start.12 = (f32[8,1152]{1,0:T(8,128)S(1)}, f32[8,1152]{1,0:T(8,128)S(1)}, u32[]{:S(2)}, u32[]{:S(2)}) collective-permute-start(f32[8,1152]{1,0:T(8,128)S(1)} %add.27.refs_8_), channel_id=1, source_target_pairs={{0,4},{2,6},{4,0},{6,2},{8,12},{10,14},{12,8},{14,10},{16,20},{18,... | collective-permute-start | bytes 110600 | tf_op jit(solution)/shard_map/ppermute | solution.py:57
  28.4 7.8 %collective-permute-start.13 = (f32[8,2048]{1,0:T(8,128)S(1)}, f32[8,2048]{1,0:T(8,128)S(1)}, u32[]{:S(2)}, u32[]{:S(2)}) collective-permute-start(f32[8,2048]{1,0:T(8,128)S(1)} %get-tuple-element.44), channel_id=1, source_target_pairs={{0,24},{2,26},{4,28},{6,30},{8,16},{10,18},{12,20},{14,22},{16,8},... | collective-permute-start | bytes 196616 | tf_op jit(solution)/shard_map/ppermute | solution.py:57
  31.1 6.1 %collective-permute-start.14 = (f32[8,2048]{1,0:T(8,128)S(1)}, f32[8,2048]{1,0:T(8,128)S(1)}, u32[]{:S(2)}, u32[]{:S(2)}) collective-permute-start(f32[8,2048]{1,0:T(8,128)S(1)} %get-tuple-element.43), channel_id=1, source_target_pairs={{0,16},{2,18},{4,20},{6,22},{8,24},{10,26},{12,28},{14,30},{16,0},... | collective-permute-start | bytes 196616 | tf_op jit(solution)/shard_map/ppermute | solution.py:57
  31.1 6.1 %collective-permute-start.15 = (f32[8,2048]{1,0:T(8,128)S(1)}, f32[8,2048]{1,0:T(8,128)S(1)}, u32[]{:S(2)}, u32[]{:S(2)}) collective-permute-start(f32[8,2048]{1,0:T(8,128)S(1)} %get-tuple-element.42), channel_id=1, source_target_pairs={{0,8},{2,10},{4,12},{6,14},{8,0},{10,2},{12,4},{14,6},{16,24},{18,... | collective-permute-start | bytes 196616 | tf_op jit(solution)/shard_map/ppermute | solution.py:57

commit v7 on v5

--- a/solution.py
+++ b/solution.py
@@ -120,19 +120,24 @@
     diagonal = factor * identity_ref[...]
     recip_row = 1.0 / jnp.sum(diagonal, axis=0, keepdims=True)
     recip_col = 1.0 / jnp.sum(diagonal, axis=1, keepdims=True)
-    size, level = 1, 0
+    size, done = 16, 0
+    nilpotent = jnp.where((i // size == j // size) & (i > j), -(recip_col * factor), 0.0)
+    second = dot6(nilpotent, nilpotent)
+    fourth = dot6(second, second)
+    series = identity_ref[...] + nilpotent + second + dot6(nilpotent, second)
+    eighth = dot6(fourth, fourth)
+    series = series + dot6(series, fourth)
+    inverse = (series + dot6(series, eighth)) * recip_row
     while size < n:
         below = (i // (2 * size) == j // (2 * size)) & ((i // size) % 2 == 1) & ((j // size) % 2 == 0)
         block = jnp.where(below, factor, 0.0)
-        if level == 0:
-            inverse = jnp.where(i == j, recip_row, -(recip_col * block * recip_row))
-        else:
-            inverse = inverse - dot6(dot6(inverse, block), inverse)
-        if 2 <= level < 2 + chunks:
-            split_chunk(level - 2)
-        size, level = 2 * size, level + 1
+        inverse = inverse - dot6(dot6(inverse, block), inverse)
+        if done < chunks:
+            split_chunk(done)
+            done += 1
+        size *= 2
     inverse_t_ref[...] = inverse.T
-    for k in range(max(level - 2, 0), chunks):
+    for k in range(done, chunks):
         split_chunk(k)
 
 

time: 37.5 us -> 37.4 us (level)
  transfers between devices with their start and end apart: 16 -> 16, of which waited for: 5 -> 5; matrix products, arithmetic and copies ran while one was open for 1% -> 1% of each run, Pallas kernels for 24% -> 23%
where the time goes in v7:
time: 37.4 us; the launch traced here: 37.2 us
  starting transfers between devices  17.4 us (47%)
  waiting for transfers between devices  8.83 us (24%)
  Pallas kernels  8.7 us (23%)
  between operations  0.82 us (2%)
  other arithmetic  0.79 us (2%)
  local copies, waits for them, and re-layouts  0.66 us (2%)
    ppermute x16, starting transfers between devices, swap(): return lax.ppermute(value, axis, [(i, i ^ offset) for i in range(size)])  17.4 us
    ppermute x16, waiting for transfers between devices, swap(): return lax.ppermute(value, axis, [(i, i ^ offset) for i in range(size)])  8.83 us
    pallas_call x1, Pallas kernels, body(): pl.pallas_call(lambda *refs: finish_kernel(grid, *refs), in_specs=[vmem]...  3.33 us
    pallas_call x1, Pallas kernels, body(): call(prepare_kernel, (full((n, n)), full((depth, breadth), BF16), full((d...  2.76 us
    pallas_call x1, Pallas kernels, body(): call(lambda *refs: cbar_kernel(grid, *refs), (full((n, depth)), full((wid...  1.01 us
    pallas_call x1, Pallas kernels, body(): call(trailing_kernel, (full((n // 2, breadth)),) * 2, flops=10 ** 9)  0.97 us
  transfers between devices with their start and end apart: 16, of which 5 were waited for; matrix products, arithmetic and copies ran while one was open for 1% of the time, Pallas kernels for 23%

profile of v7, /device:TPU:0, one launch (start us, length us, event | category | flops | bytes accessed | tf_op | source)
XLA Modules:
  0.0 37.2 jit_solution(16074082613510382551)
XLA Ops:
  0.6 3.1 %collective-permute-start.7 = (f32[8,2048]{1,0:T(8,128)}, f32[8,2048]{1,0:T(8,128)S(1)}, u32[]{:S(2)}, u32[]{:S(2)}) collective-permute-start(f32[8,2048]{1,0:T(8,128)} %param.12), channel_id=1, source_target_pairs={{0,8},{2,10},{4,12},{6,14},{8,0},{10,2},{12,4},{14,6},{16,24},{18,... | collective-permute-start | bytes 196616 | tf_op jit(solution)/shard_map/ppermute | solution.py:57
  3.7 2.6 %collective-permute-start.8 = (f32[8,2048]{1,0:T(8,128)}, f32[8,2048]{1,0:T(8,128)S(1)}, u32[]{:S(2)}, u32[]{:S(2)}) collective-permute-start(f32[8,2048]{1,0:T(8,128)} %param.12), channel_id=1, source_target_pairs={{0,16},{2,18},{4,20},{6,22},{8,24},{10,26},{12,28},{14,30},{16,0},... | collective-permute-start | bytes 196616 | tf_op jit(solution)/shard_map/ppermute | solution.py:57
  6.3 0.0 collective-permute-start.9
  6.3 1.7 %collective-permute-start = (f32[64,512]{1,0:T(8,128)}, f32[64,512]{1,0:T(8,128)S(1)}, u32[]{:S(2)}, u32[]{:S(2)}) collective-permute-start(f32[64,512]{1,0:T(8,128)} %bitcast.5), channel_id=1, source_target_pairs={{0,1},{1,0},{2,3},{3,2},{4,5},{5,4},{6,7},{7,6},{8,9},{9,8},{10,11... | collective-permute-start | bytes 393224 | tf_op jit(solution)/shard_map/ppermute | solution.py:57
  8.1 0.0 copy-start.2
  8.1 0.3 collective-permute-start.1
  8.4 0.5 %copy-done.2 = f32[128,128]{1,0:T(8,128)S(1)} copy-done((f32[128,128]{1,0:T(8,128)S(1)}, f32[128,128]{1,0:T(8,128)}, u32[]{:S(2)}) %copy-start.2) | copy-done | bytes 65560
  8.9 0.0 copy-start.6
  8.9 0.0 copy-start.5
  8.9 2.8 %shard_map.112 = (f32[128,128]{1,0:T(8,128)S(1)}, bf16[512,2048]{1,0:T(8,128)(2,1)S(1)}, bf16[512,2048]{1,0:T(8,128)(2,1)S(1)}) custom-call(f32[128,128]{1,0:T(8,128)S(1)} %copy-done.2, f32[128,128]{1,0:T(8,128)S(1)} %shard_map.111.identity_ref, f32[512,2048]{1,0:T(8,128)} %b_hbm.1), custom_call_target="tpu_custom_call" | custom-call | flops 4000000000 | bytes 1 | tf_op jit(solution)/shard_map/pallas_call | solution.py:294
  11.7 0.0 copy-done.6
  11.7 0.0 collective-permute-done.7
  11.7 0.0 collective-permute-done.8
  11.7 0.9 %collective-permute-done.9 = f32[8,2048]{1,0:T(8,128)S(1)} collective-permute-done((f32[8,2048]{1,0:T(8,128)}, f32[8,2048]{1,0:T(8,128)S(1)}, u32[]{:S(2)}, u32[]{:S(2)}) %collective-permute-start.9) | collective-permute-done | bytes 65568 | tf_op jit(solution)/shard_map/ppermute | solution.py:57
  12.6 1.6 %collective-permute-start.10 = (f32[32,2048]{1,0:T(8,128)S(1)}, f32[32,2048]{1,0:T(8,128)S(1)}, u32[]{:S(2)}, u32[]{:S(2)}) collective-permute-start(f32[32,2048]{1,0:T(8,128)S(1)} %pad_maximum_fusion), channel_id=1, source_target_pairs={{0,4},{2,6},{4,0},{6,2},{8,12},{10,14},{12,8},{14,10},{16,20},{18,... | collective-permute-start | bytes 786440 | tf_op jit(solution)/shard_map/ppermute | solution.py:57
  14.2 0.0 collective-permute-done.refs_2_
  14.2 0.0 copy-done.5
  14.2 0.0 copy-start.1
  14.2 1.0 %shard_map.113 = (f32[128,512]{1,0:T(8,128)S(1)}, f32[64,512]{1,0:T(8,128)}, f32[128,512]{1,0:T(8,128)S(1)}, bf16[256,512]{1,0:T(8,128)(2,1)S(1)}) custom-call(f32[128,128]{1,0:T(8,128)S(1)} %get-tuple-element.22.refs_0_.refs_3_, f32[64,512]{1,0:T(8,128)S(1)} %bitcast.6, f32[64,512]{1,0:T(8,128)S(1)} %collective-permute-done.refs_2_), custom_call_target="tpu_custom_call" | custom-call | flops 1000000000 | bytes 1 | tf_op jit(solution)/shard_map/pallas_call | solution.py:301
  15.2 0.0 copy-start
  15.2 0.0 copy-start.3
  15.2 0.0 copy-start.4
  15.2 1.0 %shard_map.114 = (f32[64,2048]{1,0:T(8,128)S(1)}, f32[64,2048]{1,0:T(8,128)S(1)}) custom-call(bf16[256,512]{1,0:T(8,128)(2,1)S(1)} %get-tuple-element.26.stack_ref, bf16[512,2048]{1,0:T(8,128)(2,1)S(1)} %get-tuple-element.27.high_ref, bf16[512,2048]{1,0:T(8,128)(2,1)S(1)} %get-tuple-element.28.low_ref), custom_call_target="tpu_custom_call" | custom-call | flops 1000000000 | bytes 1 | tf_op jit(solution)/shard_map/pallas_call | solution.py:306
  16.2 0.1 collective-permute-start.3
  16.3 0.0 collective-permute-done.1.refs_2_
  16.3 0.0 copy-done.1
  16.3 0.6 %shard_map.115 = f32[8,1152]{1,0:T(8,128)S(1)} custom-call(f32[128,512]{1,0:T(8,128)S(1)} %get-tuple-element.30.refs_0_, f32[64,512]{1,0:T(8,128)S(1)} %bitcast.4, f32[64,512]{1,0:T(8,128)S(1)} %collective-permute-done.1.refs_2_), custom_call_target="tpu_custom_call" | custom-call | bytes 1 | tf_op jit(solution)/shard_map/pallas_call | solution.py:307
  16.9 0.5 %collective-permute-start.2 = (f32[8,1152]{1,0:T(8,128)S(1)}, f32[8,1152]{1,0:T(8,128)S(1)}, u32[]{:S(2)}, u32[]{:S(2)}) collective-permute-start(f32[8,1152]{1,0:T(8,128)S(1)} %shard_map.115), channel_id=1, source_target_pairs={{0,2},{2,0},{4,6},{6,4},{8,10},{10,8},{12,14},{14,12},{16,18},{18,... | collective-permute-start | bytes 110600 | tf_op jit(solution)/shard_map/ppermute | solution.py:57
  17.5 0.9 %collective-permute-done.2 = f32[8,1152]{1,0:T(8,128)S(1)} collective-permute-done((f32[8,1152]{1,0:T(8,128)S(1)}, f32[8,1152]{1,0:T(8,128)S(1)}, u32[]{:S(2)}, u32[]{:S(2)}) %collective-permute-start.2) | collective-permute-done | bytes 36896 | tf_op jit(solution)/shard_map/ppermute | solution.py:57
  18.4 0.0 collective-permute-done.3
  18.4 0.1 add.25
  18.4 0.1 collective-permute-start.4
  18.6 0.6 %collective-permute-start.6 = (f32[32,2048]{1,0:T(8,128)S(1)}, f32[32,2048]{1,0:T(8,128)S(1)}, u32[]{:S(2)}, u32[]{:S(2)}) collective-permute-start(f32[32,2048]{1,0:T(8,128)S(1)} %get-tuple-element.40), channel_id=1, source_target_pairs={{0,4},{2,6},{4,0},{6,2},{8,12},{10,14},{12,8},{14,10},{16,20},{18,... | collective-permute-start | bytes 786440 | tf_op jit(solution)/shard_map/ppermute | solution.py:57
  19.2 0.0 collective-permute-done.10
  19.2 0.1 collective-permute-start.11
  19.3 3.1 %collective-permute-done.4 = f32[8,1152]{1,0:T(8,128)S(1)} collective-permute-done((f32[8,1152]{1,0:T(8,128)S(1)}, f32[8,1152]{1,0:T(8,128)S(1)}, u32[]{:S(2)}, u32[]{:S(2)}) %collective-permute-start.4) | collective-permute-done | bytes 36896 | tf_op jit(solution)/shard_map/ppermute | solution.py:57
  22.5 1.6 %collective-permute-start.5 = (f32[8,1152]{1,0:T(8,128)S(1)}, f32[8,1152]{1,0:T(8,128)S(1)}, u32[]{:S(2)}, u32[]{:S(2)}) collective-permute-start(f32[8,1152]{1,0:T(8,128)S(1)} %add.26), channel_id=1, source_target_pairs={{0,16},{2,18},{4,20},{6,22},{8,24},{10,26},{12,28},{14,30},{16,0},... | collective-permute-start | bytes 110600 | tf_op jit(solution)/shard_map/ppermute | solution.py:57
  24.0 3.5 %collective-permute-done.5 = f32[8,1152]{1,0:T(8,128)S(1)} collective-permute-done((f32[8,1152]{1,0:T(8,128)S(1)}, f32[8,1152]{1,0:T(8,128)S(1)}, u32[]{:S(2)}, u32[]{:S(2)}) %collective-permute-start.5) | collective-permute-done | bytes 36896 | tf_op jit(solution)/shard_map/ppermute | solution.py:57
  27.5 0.7 %collective-permute-start.12 = (f32[8,1152]{1,0:T(8,128)S(1)}, f32[8,1152]{1,0:T(8,128)S(1)}, u32[]{:S(2)}, u32[]{:S(2)}) collective-permute-start(f32[8,1152]{1,0:T(8,128)S(1)} %add.27.refs_8_), channel_id=1, source_target_pairs={{0,4},{2,6},{4,0},{6,2},{8,12},{10,14},{12,8},{14,10},{16,20},{18,... | collective-permute-start | bytes 110600 | tf_op jit(solution)/shard_map/ppermute | solution.py:57
  28.2 0.0 collective-permute-done.6
  28.3 2.6 %collective-permute-start.13 = (f32[8,2048]{1,0:T(8,128)S(1)}, f32[8,2048]{1,0:T(8,128)S(1)}, u32[]{:S(2)}, u32[]{:S(2)}) collective-permute-start(f32[8,2048]{1,0:T(8,128)S(1)} %get-tuple-element.44), channel_id=1, source_target_pairs={{0,24},{2,26},{4,28},{6,30},{8,16},{10,18},{12,20},{14,22},{16,8},... | collective-permute-start | bytes 196616 | tf_op jit(solution)/shard_map/ppermute | solution.py:57
  30.9 0.0 collective-permute-start.14
  30.9 1.9 %collective-permute-start.15 = (f32[8,2048]{1,0:T(8,128)S(1)}, f32[8,2048]{1,0:T(8,128)S(1)}, u32[]{:S(2)}, u32[]{:S(2)}) collective-permute-start(f32[8,2048]{1,0:T(8,128)S(1)} %get-tuple-element.42), channel_id=1, source_target_pairs={{0,8},{2,10},{4,12},{6,14},{8,0},{10,2},{12,4},{14,6},{16,24},{18,... | collective-permute-start | bytes 196616 | tf_op jit(solution)/shard_map/ppermute | solution.py:57
  32.8 0.0 collective-permute-done.12.refs_9_
  32.8 0.0 collective-permute-done.11.refs_7_
  32.8 0.0 copy-done
  32.8 0.0 copy-done.3
  32.8 0.0 copy-done.4
  32.8 3.3 %shard_map.116 = (f32[512,2048]{1,0:T(8,128)}, f32[8,64]{1,0:T(8,128)}, f32[8,2048]{1,0:T(8,128)S(1)}) custom-call(f32[128,512]{1,0:T(8,128)S(1)} %get-tuple-element.24.refs_0_, f32[512,2048]{1,0:T(8,128)S(1)} %copy-done, f32[128,128]{1,0:T(8,128)S(1)} %copy-done.2, f32[128,128]{1,0:T(8,128)S(1)} %get-tuple-element.22.refs_0_.refs_3_, ...), custom_call_target="tpu_custom_call" | custom-call | flops 1000000000 | bytes 1 | tf_op jit(solution)/shard_map/pallas_call | solution.py:328
  36.1 0.0 collective-permute-done.13
  36.1 0.4 %collective-permute-done.14 = f32[8,2048]{1,0:T(8,128)S(1)} collective-permute-done((f32[8,2048]{1,0:T(8,128)S(1)}, f32[8,2048]{1,0:T(8,128)S(1)}, u32[]{:S(2)}, u32[]{:S(2)}) %collective-permute-start.14) | collective-permute-done | bytes 65568 | tf_op jit(solution)/shard_map/ppermute | solution.py:57
  36.6 0.0 collective-permute-done.15
  36.6 0.7 %fusion.1 = f32[8,2048]{1,0:T(8,128)} fusion(f32[8,2048]{1,0:T(8,128)S(1)} %get-tuple-element.39, f32[8,2048]{1,0:T(8,128)S(1)} %collective-permute-done.13, f32[32,2048]{1,0:T(8,128)S(1)} %add.28, f32[8,2048]{1,0:T(8,128)S(1)} %collective-permute-done.14, f32[8,2048]{1,0:T(8,128)S(1)} %collective-permute-done.15), kind=kLoop, calls=%fused_computation.3 | loop fusion | flops 65536 | bytes 393216 | tf_op jit(solution)/shard_map/sub | solution.py:339
  (13 shorter events, 0.2 us)
Async XLA Ops:
  0.6 11.1 %collective-permute-start.7 = (f32[8,2048]{1,0:T(8,128)}, f32[8,2048]{1,0:T(8,128)S(1)}, u32[]{:S(2)}, u32[]{:S(2)}) collective-permute-start(f32[8,2048]{1,0:T(8,128)} %param.12), channel_id=1, source_target_pairs={{0,8},{2,10},{4,12},{6,14},{8,0},{10,2},{12,4},{14,6},{16,24},{18,... | collective-permute-start | bytes 196616 | tf_op jit(solution)/shard_map/ppermute | solution.py:57
  3.7 8.0 %collective-permute-start.8 = (f32[8,2048]{1,0:T(8,128)}, f32[8,2048]{1,0:T(8,128)S(1)}, u32[]{:S(2)}, u32[]{:S(2)}) collective-permute-start(f32[8,2048]{1,0:T(8,128)} %param.12), channel_id=1, source_target_pairs={{0,16},{2,18},{4,20},{6,22},{8,24},{10,26},{12,28},{14,30},{16,0},... | collective-permute-start | bytes 196616 | tf_op jit(solution)/shard_map/ppermute | solution.py:57
  6.3 6.3 %collective-permute-start.9 = (f32[8,2048]{1,0:T(8,128)}, f32[8,2048]{1,0:T(8,128)S(1)}, u32[]{:S(2)}, u32[]{:S(2)}) collective-permute-start(f32[8,2048]{1,0:T(8,128)} %param.12), channel_id=1, source_target_pairs={{0,24},{2,26},{4,28},{6,30},{8,16},{10,18},{12,20},{14,22},{16,8},... | collective-permute-start | bytes 196616 | tf_op jit(solution)/shard_map/ppermute | solution.py:57
  6.3 7.9 %collective-permute-start = (f32[64,512]{1,0:T(8,128)}, f32[64,512]{1,0:T(8,128)S(1)}, u32[]{:S(2)}, u32[]{:S(2)}) collective-permute-start(f32[64,512]{1,0:T(8,128)} %bitcast.5), channel_id=1, source_target_pairs={{0,1},{1,0},{2,3},{3,2},{4,5},{5,4},{6,7},{7,6},{8,9},{9,8},{10,11... | collective-permute-start | bytes 393224 | tf_op jit(solution)/shard_map/ppermute | solution.py:57
  8.1 0.8 %copy-start.2 = (f32[128,128]{1,0:T(8,128)S(1)}, f32[128,128]{1,0:T(8,128)}, u32[]{:S(2)}) copy-start(f32[128,128]{1,0:T(8,128)} %refs_2_.1) | copy-start | bytes 196612
  8.1 8.3 %collective-permute-start.1 = (f32[64,512]{1,0:T(8,128)}, f32[64,512]{1,0:T(8,128)S(1)}, u32[]{:S(2)}, u32[]{:S(2)}) collective-permute-start(f32[64,512]{1,0:T(8,128)} %bitcast.3), channel_id=1, source_target_pairs={{0,1},{1,0},{2,3},{3,2},{4,5},{5,4},{6,7},{7,6},{8,9},{9,8},{10,11... | collective-permute-start | bytes 393224 | tf_op jit(solution)/shard_map/ppermute | solution.py:57
  8.9 2.8 %copy-start.6 = (f32[8,2048]{1,0:T(8,128)S(1)}, f32[8,2048]{1,0:T(8,128)}, u32[]{:S(2)}) copy-start(f32[8,2048]{1,0:T(8,128)} %param.12) | copy-start | bytes 196612
  8.9 5.3 %copy-start.5 = (f32[512,64]{0,1:T(8,128)S(1)}, f32[512,64]{0,1:T(8,128)}, u32[]{:S(2)}) copy-start(f32[512,64]{0,1:T(8,128)} %param.9) | copy-start | bytes 393220
  12.6 6.5 %collective-permute-start.10 = (f32[32,2048]{1,0:T(8,128)S(1)}, f32[32,2048]{1,0:T(8,128)S(1)}, u32[]{:S(2)}, u32[]{:S(2)}) collective-permute-start(f32[32,2048]{1,0:T(8,128)S(1)} %pad_maximum_fusion), channel_id=1, source_target_pairs={{0,4},{2,6},{4,0},{6,2},{8,12},{10,14},{12,8},{14,10},{16,20},{18,... | collective-permute-start | bytes 786440 | tf_op jit(solution)/shard_map/ppermute | solution.py:57
  14.2 2.1 %copy-start.1 = (f32[512,64]{0,1:T(8,128)S(1)}, f32[512,64]{0,1:T(8,128)}, u32[]{:S(2)}) copy-start(f32[512,64]{0,1:T(8,128)} %param.8) | copy-start | bytes 393220
  15.2 17.6 %copy-start = (f32[512,2048]{1,0:T(8,128)S(1)}, f32[512,2048]{1,0:T(8,128)}, u32[]{:S(2)}) copy-start(f32[512,2048]{1,0:T(8,128)} %refs_1_.1) | copy-start | bytes 12582916
  15.2 17.6 %copy-start.3 = (f32[128,128]{1,0:T(8,128)S(1)}, f32[128,128]{1,0:T(8,128)}, u32[]{:S(2)}) copy-start(f32[128,128]{1,0:T(8,128)} %refs_4_) | copy-start | bytes 196612
  15.2 17.6 %copy-start.4 = (f32[8,2048]{1,0:T(8,128)S(1)}, f32[8,2048]{1,0:T(8,128)}, u32[]{:S(2)}) copy-start(f32[8,2048]{1,0:T(8,128)} %refs_5_.1) | copy-start | bytes 196612
  16.2 2.2 %collective-permute-start.3 = (f32[64,2048]{1,0:T(8,128)S(1)}, f32[64,2048]{1,0:T(8,128)S(1)}, u32[]{:S(2)}, u32[]{:S(2)}) collective-permute-start(f32[64,2048]{1,0:T(8,128)S(1)} %get-tuple-element.29), channel_id=1, source_target_pairs={{0,2},{2,0},{4,6},{6,4},{8,10},{10,8},{12,14},{14,12},{16,18},{18,... | collective-permute-start | bytes 1572872 | tf_op jit(solution)/shard_map/ppermute | solution.py:57
  16.9 1.4 %collective-permute-start.2 = (f32[8,1152]{1,0:T(8,128)S(1)}, f32[8,1152]{1,0:T(8,128)S(1)}, u32[]{:S(2)}, u32[]{:S(2)}) collective-permute-start(f32[8,1152]{1,0:T(8,128)S(1)} %shard_map.115), channel_id=1, source_target_pairs={{0,2},{2,0},{4,6},{6,4},{8,10},{10,8},{12,14},{14,12},{16,18},{18,... | collective-permute-start | bytes 110600 | tf_op jit(solution)/shard_map/ppermute | solution.py:57
  18.4 4.0 %collective-permute-start.4 = (f32[8,1152]{1,0:T(8,128)S(1)}, f32[8,1152]{1,0:T(8,128)S(1)}, u32[]{:S(2)}, u32[]{:S(2)}) collective-permute-start(f32[8,1152]{1,0:T(8,128)S(1)} %add.24), channel_id=1, source_target_pairs={{0,8},{2,10},{4,12},{6,14},{8,0},{10,2},{12,4},{14,6},{16,24},{18,... | collective-permute-start | bytes 110600 | tf_op jit(solution)/shard_map/ppermute | solution.py:57
  18.6 9.7 %collective-permute-start.6 = (f32[32,2048]{1,0:T(8,128)S(1)}, f32[32,2048]{1,0:T(8,128)S(1)}, u32[]{:S(2)}, u32[]{:S(2)}) collective-permute-start(f32[32,2048]{1,0:T(8,128)S(1)} %get-tuple-element.40), channel_id=1, source_target_pairs={{0,4},{2,6},{4,0},{6,2},{8,12},{10,14},{12,8},{14,10},{16,20},{18,... | collective-permute-start | bytes 786440 | tf_op jit(solution)/shard_map/ppermute | solution.py:57
  19.2 13.6 %collective-permute-start.11 = (f32[64,2048]{1,0:T(8,128)S(1)}, f32[64,2048]{1,0:T(8,128)S(1)}, u32[]{:S(2)}, u32[]{:S(2)}) collective-permute-start(f32[64,2048]{1,0:T(8,128)S(1)} %constant_dynamic-update-slice_fusion.refs_6_), channel_id=1, source_target_pairs={{0,2},{2,0},{4,6},{6,4},{8,10},{10,8},{12,14},{14,12},{16,18},{18,... | collective-permute-start | bytes 1572872 | tf_op jit(solution)/shard_map/ppermute | solution.py:57
  22.5 5.0 %collective-permute-start.5 = (f32[8,1152]{1,0:T(8,128)S(1)}, f32[8,1152]{1,0:T(8,128)S(1)}, u32[]{:S(2)}, u32[]{:S(2)}) collective-permute-start(f32[8,1152]{1,0:T(8,128)S(1)} %add.26), channel_id=1, source_target_pairs={{0,16},{2,18},{4,20},{6,22},{8,24},{10,26},{12,28},{14,30},{16,0},... | collective-permute-start | bytes 110600 | tf_op jit(solution)/shard_map/ppermute | solution.py:57
  27.5 5.2 %collective-permute-start.12 = (f32[8,1152]{1,0:T(8,128)S(1)}, f32[8,1152]{1,0:T(8,128)S(1)}, u32[]{:S(2)}, u32[]{:S(2)}) collective-permute-start(f32[8,1152]{1,0:T(8,128)S(1)} %add.27.refs_8_), channel_id=1, source_target_pairs={{0,4},{2,6},{4,0},{6,2},{8,12},{10,14},{12,8},{14,10},{16,20},{18,... | collective-permute-start | bytes 110600 | tf_op jit(solution)/shard_map/ppermute | solution.py:57
  28.3 7.8 %collective-permute-start.13 = (f32[8,2048]{1,0:T(8,128)S(1)}, f32[8,2048]{1,0:T(8,128)S(1)}, u32[]{:S(2)}, u32[]{:S(2)}) collective-permute-start(f32[8,2048]{1,0:T(8,128)S(1)} %get-tuple-element.44), channel_id=1, source_target_pairs={{0,24},{2,26},{4,28},{6,30},{8,16},{10,18},{12,20},{14,22},{16,8},... | collective-permute-start | bytes 196616 | tf_op jit(solution)/shard_map/ppermute | solution.py:57
  30.9 5.7 %collective-permute-start.14 = (f32[8,2048]{1,0:T(8,128)S(1)}, f32[8,2048]{1,0:T(8,128)S(1)}, u32[]{:S(2)}, u32[]{:S(2)}) collective-permute-start(f32[8,2048]{1,0:T(8,128)S(1)} %get-tuple-element.43), channel_id=1, source_target_pairs={{0,16},{2,18},{4,20},{6,22},{8,24},{10,26},{12,28},{14,30},{16,0},... | collective-permute-start | bytes 196616 | tf_op jit(solution)/shard_map/ppermute | solution.py:57
  30.9 5.7 %collective-permute-start.15 = (f32[8,2048]{1,0:T(8,128)S(1)}, f32[8,2048]{1,0:T(8,128)S(1)}, u32[]{:S(2)}, u32[]{:S(2)}) collective-permute-start(f32[8,2048]{1,0:T(8,128)S(1)} %get-tuple-element.42), channel_id=1, source_target_pairs={{0,8},{2,10},{4,12},{6,14},{8,0},{10,2},{12,4},{14,6},{16,24},{18,... | collective-permute-start | bytes 196616 | tf_op jit(solution)/shard_map/ppermute | solution.py:57
